TPU v7x, 256 devices: a whole 4x4x8 slice. The times are simulated.
256 devices in a mesh: tensor: 4 (over y), context: 64 (over x, z, core).
Axes of the slice: x: 4, y: 4, z: 8, core: 2. Of those that a mesh axis runs over, the one named last changes fastest.
Arguments:
- query_gate: bfloat16 [8192, 4096], P('context', 'tensor'), may hold values from -6 to 6
- key_gate: bfloat16 [8192, 4096], P('context', 'tensor'), may hold values from -6 to 6
- value_in: bfloat16 [8192, 4096], P('context', 'tensor'), may hold values from -6 to 6
- filter_raw: float32 [8192, 256], P('context', 'tensor'), may hold values from -6 to 6
- grad_out: bfloat16 [8192, 4096], P('context', 'tensor'), may hold values from -6 to 6
Outputs:
- output: bfloat16 [8192, 4096], P('context', 'tensor')
- grad_query: bfloat16 [8192, 4096], P('context', 'tensor')
- grad_key: bfloat16 [8192, 4096], P('context', 'tensor')
- grad_value: bfloat16 [8192, 4096], P('context', 'tensor')
- grad_filter: float32 [8192, 256], P('context', 'tensor')
All inputs are finite; a program needn't handle non-finite values.
Results may differ from a plain program's by a relative error of at most 0.0011.
Values sent between devices are 32-bit elements; how exact they have to be, the bound alone decides.
No kernel may reach another device: no remote copies, remote signals or barrier semaphores. Data moves between devices by JAX's collectives and lax.ppermute only.
A program may use at most 64 MiB of HBM per device.

v0:
```python
import math

import jax
import jax.numpy as jnp
from jax import lax
from jax.sharding import PartitionSpec as P

highest = lax.Precision.HIGHEST


def phase_table(count_rows, count_cols, period):
    row_index = lax.broadcasted_iota(jnp.int32, (count_rows, count_cols), 0)
    col_index = lax.broadcasted_iota(jnp.int32, (count_rows, count_cols), 1)
    return (row_index * col_index % period).astype(jnp.float32) * (2.0 * math.pi / period)


def rotate(real_part, imag_part, cosine, sine):
    return (real_part * cosine - imag_part * sine, real_part * sine + imag_part * cosine)


def local(query_gate, key_gate, value_in, filter_raw, grad_out):
    groups = lax.axis_size("context")
    here = lax.axis_index("context")
    rows = query_gate.shape[0]
    width = query_gate.shape[1]
    filter_count = filter_raw.shape[1]
    group_size = width // filter_count
    points = 2 * groups * rows
    scale = 1.0 / math.sqrt(groups * rows)
    local_phase = phase_table(rows, rows, rows)
    cos_local = jnp.cos(local_phase)
    sin_local = jnp.sin(local_phase)
    row_iota = lax.broadcasted_iota(jnp.int32, (1, rows, 1), 1)
    parity = lax.broadcasted_iota(jnp.int32, (2, 1, 1), 0)

    def twiddle_phase(first):
        frequency = 2 * first + parity
        return (row_iota * frequency % points).astype(jnp.float32) * (2.0 * math.pi / points)

    def transpose_forward(signal):
        pieces = lax.all_to_all(signal[None], "context", split_axis=1, concat_axis=0, tiled=True)
        angles = phase_table(2 * groups, groups, 2 * groups)
        spread_re = jnp.einsum("ap,plc->alc", jnp.cos(angles), pieces, precision=highest)
        spread_im = -jnp.einsum("ap,plc->alc", jnp.sin(angles), pieces, precision=highest)
        return lax.all_to_all(
            jnp.stack([spread_re, spread_im]), "context", split_axis=1, concat_axis=2, tiled=True
        )

    def forward(signal):
        spec = transpose_forward(signal)
        phase = twiddle_phase(here)
        tw_re, tw_im = rotate(spec[0], spec[1], jnp.cos(phase), -jnp.sin(phase))
        out_re = jnp.einsum("br,erc->ebc", cos_local, tw_re, precision=highest) + jnp.einsum(
            "br,erc->ebc", sin_local, tw_im, precision=highest
        )
        out_im = jnp.einsum("br,erc->ebc", cos_local, tw_im, precision=highest) - jnp.einsum(
            "br,erc->ebc", sin_local, tw_re, precision=highest
        )
        return jnp.stack([out_re, out_im])

    def transpose_inverse(spec):
        pieces = lax.all_to_all(spec, "context", split_axis=2, concat_axis=1, tiled=True)
        angles = phase_table(groups, 2 * groups, 2 * groups)
        values = jnp.einsum(
            "pa,alc->plc", jnp.cos(angles), pieces[0], precision=highest
        ) - jnp.einsum("pa,alc->plc", jnp.sin(angles), pieces[1], precision=highest)
        return lax.all_to_all(values, "context", split_axis=0, concat_axis=1, tiled=True)[0]

    def turned(spec, first):
        loc_re = jnp.einsum("rb,ebc->erc", cos_local, spec[0], precision=highest) - jnp.einsum(
            "rb,ebc->erc", sin_local, spec[1], precision=highest
        )
        loc_im = jnp.einsum("rb,ebc->erc", cos_local, spec[1], precision=highest) + jnp.einsum(
            "rb,ebc->erc", sin_local, spec[0], precision=highest
        )
        phase = twiddle_phase(first)
        rot_re, rot_im = rotate(loc_re, loc_im, jnp.cos(phase), jnp.sin(phase))
        return jnp.stack([rot_re, rot_im])

    def inverse(spec):
        signal = transpose_inverse(turned(spec, here))
        return signal * (1.0 / points)

    def widen(part):
        spread = jnp.broadcast_to(part[..., None], part.shape + (group_size,))
        return spread.reshape(part.shape[:-1] + (width,))

    def group_total(part):
        return jnp.sum(part.reshape(part.shape[:-1] + (filter_count, group_size)), axis=-1)

    query_full = query_gate.astype(jnp.float32)
    key_full = key_gate.astype(jnp.float32)
    value_full = value_in.astype(jnp.float32)
    grad_full = grad_out.astype(jnp.float32)
    gated = key_full * value_full
    grad_conv = grad_full * query_full
    filt_part = filter_raw * scale
    spec_gated = forward(gated)
    spec_grad = forward(grad_conv)
    spec_filt = forward(filt_part)
    gated_re, gated_im = (spec_gated[0], spec_gated[1])
    filt_re, filt_im = (widen(spec_filt[0]), widen(spec_filt[1]))
    grad_re, grad_im = (spec_grad[0], spec_grad[1])
    conv_spec = jnp.stack(
        [gated_re * filt_re - gated_im * filt_im, gated_re * filt_im + gated_im * filt_re]
    )
    back_spec = jnp.stack(
        [filt_re * grad_re + filt_im * grad_im, filt_re * grad_im - filt_im * grad_re]
    )
    corr_spec = jnp.stack(
        [
            group_total(gated_re * grad_re + gated_im * grad_im),
            group_total(gated_re * grad_im - gated_im * grad_re),
        ]
    )
    conv = inverse(conv_spec)
    grad_gated = inverse(back_spec)
    corr = inverse(corr_spec)
    output = (query_full * conv).astype(jnp.bfloat16)
    grad_query = (grad_full * conv).astype(jnp.bfloat16)
    grad_key = (grad_gated * value_full).astype(jnp.bfloat16)
    grad_value = (grad_gated * key_full).astype(jnp.bfloat16)
    grad_filter = corr * scale
    return (output, grad_query, grad_key, grad_value, grad_filter)


def solution(mesh):
    return jax.shard_map(
        local,
        mesh=mesh,
        in_specs=(
            P("context", "tensor"),
            P("context", "tensor"),
            P("context", "tensor"),
            P("context", "tensor"),
            P("context", "tensor"),
        ),
        out_specs=(
            P("context", "tensor"),
            P("context", "tensor"),
            P("context", "tensor"),
            P("context", "tensor"),
            P("context", "tensor"),
        ),
        check_vma=False,
    )
```

profile of v0, /device:TPU:1, one launch (start us, length us, event | category | flops | bytes accessed | tf_op | source)
XLA Modules:
  0.0 464.5 jit_solution(2489953482252501909)
XLA Ops:
  3.5 13.0 %all-to-all-start.2 = ((f32[64,1,128]{2,1,0:T(1,128)}), f32[64,1,128]{2,1,0:T(1,128)S(1)}, u32[]{:S(2)}, u32[]{:S(2)}) async-start(f32[64,1,128]{2,1,0:T(1,128)} %reshape.183), calls=%async_computation.2 | async-start | bytes 65536 | tf_op jit(solution)/shard_map/all_to_all | solution.py:41
  16.5 1.1 fusion.21
  17.6 1.3 copy.90
  19.0 6.8 %all-to-all-done.2 = f32[64,1,128]{2,1,0:T(1,128)S(1)} async-done(((f32[64,1,128]{2,1,0:T(1,128)}), f32[64,1,128]{2,1,0:T(1,128)S(1)}, u32[]{:S(2)}, u32[]{:S(2)}) %all-to-all-start.2) | async-done | bytes 32800 | tf_op jit(solution)/shard_map/all_to_all | solution.py:41
  25.7 4.7 %all-to-all-start.6 = ((f32[1,128,1024]{2,0,1:T(1,128)}), f32[1,128,1024]{2,0,1:T(1,128)S(1)}, u32[]{:S(2)}, u32[]{:S(2)}) async-start(f32[1,128,1024]{2,0,1:T(1,128)} %copy.90), calls=%async_computation.6 | async-start | bytes 1048576 | tf_op jit(solution)/shard_map/all_to_all | solution.py:41
  32.3 0.9 reshape.185
  33.3 14.6 %all-to-all-done.6 = f32[1,128,1024]{2,0,1:T(1,128)S(1)} async-done(((f32[1,128,1024]{2,0,1:T(1,128)}), f32[1,128,1024]{2,0,1:T(1,128)S(1)}, u32[]{:S(2)}, u32[]{:S(2)}) %all-to-all-start.6) | async-done | bytes 524320 | tf_op jit(solution)/shard_map/all_to_all | solution.py:41
  47.8 6.4 %all-to-all-start.3 = ((f32[64,1,512]{2,1,0:T(1,128)}), f32[64,1,512]{2,1,0:T(1,128)S(1)}, u32[]{:S(2)}, u32[]{:S(2)}) async-start(f32[64,1,512]{2,1,0:T(1,128)} %reshape.185), calls=%async_computation.3 | async-start | bytes 262144 | tf_op jit(solution)/shard_map/all_to_all | solution.py:45
  54.2 1.2 reduce.1
  55.8 1.2 fusion
  57.0 1.2 convolution_bitcast_fusion
  58.4 3.0 copy.93
  61.3 3.2 all-to-all-done.3
  64.6 17.3 %all-to-all-start.7 = ((f32[2,128,2,1024]{3,2,0,1:T(2,128)}), f32[2,128,2,1024]{3,2,0,1:T(2,128)S(1)}, u32[]{:S(2)}, u32[]{:S(2)}) async-start(f32[2,128,2,1024]{3,2,0,1:T(2,128)} %copy.93), calls=%async_computation.7 | async-start | bytes 4194304 | tf_op jit(solution)/shard_map/all_to_all | solution.py:45
  82.2 1.0 reduce.4
  86.0 47.2 %all-to-all-done.7 = f32[2,128,2,1024]{3,2,0,1:T(2,128)S(1)} async-done(((f32[2,128,2,1024]{3,2,0,1:T(2,128)}), f32[2,128,2,1024]{3,2,0,1:T(2,128)S(1)}, u32[]{:S(2)}, u32[]{:S(2)}) %all-to-all-start.7) | async-done | bytes 2097184 | tf_op jit(solution)/shard_map/all_to_all | solution.py:45
  133.2 1.6 copy.130
  135.7 1.3 fusion.12
  138.0 1.2 fusion.49
  139.2 1.2 fusion.51
  140.4 1.2 fusion.2
  141.7 2.4 fusion.10
  144.1 1.2 fusion.47
  145.3 1.2 fusion.45
  146.6 1.2 convolution_add_fusion
  147.8 1.4 subtract_bitcast_fusion
  149.3 2.4 copy.99
  151.8 57.5 %all_to_all.153 = f32[2,2,128,1024]{3,1,0,2:T(2,128)S(1)} all-to-all(f32[2,2,128,1024]{3,1,0,2:T(2,128)} %copy.99), channel_id=1, replica_groups=mesh['tensor'=4,'context'=64] {'context'}, dimensions={2} | all-to-all | bytes 4194304 | tf_op jit(solution)/shard_map/all_to_all | solution.py:62
  210.0 1.8 fusion.287
  212.6 1.3 copy.101
  213.9 1.7 squeeze.47
  215.6 2.0 fusion.83
  218.9 22.9 %all_to_all.154 = f32[64,2,1024]{2,1,0:T(2,128)S(1)} all-to-all(f32[64,2,1024]{2,1,0:T(2,128)S(1)} %copy.103), channel_id=1, replica_groups=mesh['tensor'=4,'context'=64] {'context'}, dimensions={0} | all-to-all | bytes 1048576 | tf_op jit(solution)/shard_map/all_to_all | solution.py:67
  242.4 0.9 fusion.17
  243.9 23.4 %all_to_all.155 = f32[1,128,1024]{2,0,1:T(1,128)S(1)} all-to-all(f32[1,128,1024]{2,0,1:T(1,128)S(1)} %copy.63), channel_id=1, replica_groups=mesh['tensor'=4,'context'=64] {'context'}, dimensions={1} | all-to-all | bytes 1048576 | tf_op jit(solution)/shard_map/all_to_all | solution.py:41
  267.3 1.2 reduce
  268.9 1.2 fusion.1
  270.0 1.2 convolution_bitcast_fusion.1
  271.5 1.6 copy.66
  273.1 57.5 %all_to_all.156 = f32[2,128,2,1024]{3,2,0,1:T(2,128)S(1)} all-to-all(f32[2,128,2,1024]{3,2,0,1:T(2,128)S(1)} %copy.66), channel_id=1, replica_groups=mesh['tensor'=4,'context'=64] {'context'}, dimensions={1} | all-to-all | bytes 4194304 | tf_op jit(solution)/shard_map/all_to_all | solution.py:45
  330.6 1.6 copy.131
  333.1 2.1 fusion.14
  335.7 1.5 copy.71
  337.2 1.2 fusion.59
  338.4 1.2 fusion.63
  339.6 1.3 fusion.4
  340.9 2.7 fusion.8
  346.6 0.9 reshape.187
  347.5 5.8 %all-to-all-start.10 = ((f32[64,1,512]{2,1,0:T(1,128)}), f32[64,1,512]{2,1,0:T(1,128)S(1)}, u32[]{:S(2)}, u32[]{:S(2)}) async-start(f32[64,1,512]{2,1,0:T(1,128)} %reshape.187), calls=%async_computation.10 | async-start | bytes 262144 | tf_op jit(solution)/shard_map/all_to_all | solution.py:62
  353.3 1.2 fusion.55
  354.6 1.2 fusion.53
  355.8 1.2 convolution_add_fusion.2
  357.0 1.4 subtract_bitcast_fusion.1
  358.6 2.4 copy.85
  361.0 2.7 all-to-all-done.10
  363.7 7.7 %all-to-all-start.4 = ((f32[2,2,128,1024]{3,1,0,2:T(2,128)}), f32[2,2,128,1024]{3,1,0,2:T(2,128)S(1)}, u32[]{:S(2)}, u32[]{:S(2)}) async-start(f32[2,2,128,1024]{3,1,0,2:T(2,128)} %copy.85), calls=%async_computation.4 | async-start | bytes 4194304 | tf_op jit(solution)/shard_map/all_to_all | solution.py:62
  371.4 1.0 reduce.5
  374.3 48.3 %all-to-all-done.4 = f32[2,2,128,1024]{3,1,0,2:T(2,128)S(1)} async-done(((f32[2,2,128,1024]{3,1,0,2:T(2,128)}), f32[2,2,128,1024]{3,1,0,2:T(2,128)S(1)}, u32[]{:S(2)}, u32[]{:S(2)}) %all-to-all-start.4) | async-done | bytes 2097184 | tf_op jit(solution)/shard_map/all_to_all | solution.py:62
  422.6 6.2 %all-to-all-start.11 = ((f32[64,1,128]{2,1,0:T(1,128)}), f32[64,1,128]{2,1,0:T(1,128)S(1)}, u32[]{:S(2)}, u32[]{:S(2)}) async-start(f32[64,1,128]{2,1,0:T(1,128)} %reshape.189), calls=%async_computation.11 | async-start | bytes 65536 | tf_op jit(solution)/shard_map/all_to_all | solution.py:67
  433.6 1.2 copy.89
  434.8 3.1 all-to-all-done.11
  438.0 7.2 %all-to-all-start.5 = ((f32[64,2,1024]{2,1,0:T(2,128)}), f32[64,2,1024]{2,1,0:T(2,128)S(1)}, u32[]{:S(2)}, u32[]{:S(2)}) async-start(f32[64,2,1024]{2,1,0:T(2,128)} %copy.89), calls=%async_computation.5 | async-start | bytes 1048576 | tf_op jit(solution)/shard_map/all_to_all | solution.py:67
  446.8 15.7 %all-to-all-done.5 = f32[64,2,1024]{2,1,0:T(2,128)S(1)} async-done(((f32[64,2,1024]{2,1,0:T(2,128)}), f32[64,2,1024]{2,1,0:T(2,128)S(1)}, u32[]{:S(2)}, u32[]{:S(2)}) %all-to-all-start.5) | async-done | bytes 524320 | tf_op jit(solution)/shard_map/all_to_all | solution.py:67
  463.1 0.9 fusion.20
  (87 shorter events, 28.0 us)
Async XLA Ops:
  3.5 22.2 %all-to-all-start.2 = ((f32[64,1,128]{2,1,0:T(1,128)}), f32[64,1,128]{2,1,0:T(1,128)S(1)}, u32[]{:S(2)}, u32[]{:S(2)}) async-start(f32[64,1,128]{2,1,0:T(1,128)} %reshape.183), calls=%async_computation.2 | async-start | bytes 65536 | tf_op jit(solution)/shard_map/all_to_all | solution.py:41
  25.7 22.1 %all-to-all-start.6 = ((f32[1,128,1024]{2,0,1:T(1,128)}), f32[1,128,1024]{2,0,1:T(1,128)S(1)}, u32[]{:S(2)}, u32[]{:S(2)}) async-start(f32[1,128,1024]{2,0,1:T(1,128)} %copy.90), calls=%async_computation.6 | async-start | bytes 1048576 | tf_op jit(solution)/shard_map/all_to_all | solution.py:41
  47.8 16.7 %all-to-all-start.3 = ((f32[64,1,512]{2,1,0:T(1,128)}), f32[64,1,512]{2,1,0:T(1,128)S(1)}, u32[]{:S(2)}, u32[]{:S(2)}) async-start(f32[64,1,512]{2,1,0:T(1,128)} %reshape.185), calls=%async_computation.3 | async-start | bytes 262144 | tf_op jit(solution)/shard_map/all_to_all | solution.py:45
  64.6 68.6 %all-to-all-start.7 = ((f32[2,128,2,1024]{3,2,0,1:T(2,128)}), f32[2,128,2,1024]{3,2,0,1:T(2,128)S(1)}, u32[]{:S(2)}, u32[]{:S(2)}) async-start(f32[2,128,2,1024]{3,2,0,1:T(2,128)} %copy.93), calls=%async_computation.7 | async-start | bytes 4194304 | tf_op jit(solution)/shard_map/all_to_all | solution.py:45
  218.4 24.0 %copy-start.4 = (bf16[128,1024]{1,0:T(8,128)(2,1)S(1)}, bf16[128,1024]{1,0:T(8,128)(2,1)}, u32[]{:S(2)}) copy-start(bf16[128,1024]{1,0:T(8,128)(2,1)} %param.6) | copy-start | bytes 786436
  218.4 24.0 %copy-start.5 = (bf16[128,1024]{1,0:T(8,128)(2,1)S(1)}, bf16[128,1024]{1,0:T(8,128)(2,1)}, u32[]{:S(2)}) copy-start(bf16[128,1024]{1,0:T(8,128)(2,1)} %param.7) | copy-start | bytes 786436
  337.1 2.5 copy-start
  340.9 2.7 copy-start.1
  347.5 16.1 %all-to-all-start.10 = ((f32[64,1,512]{2,1,0:T(1,128)}), f32[64,1,512]{2,1,0:T(1,128)S(1)}, u32[]{:S(2)}, u32[]{:S(2)}) async-start(f32[64,1,512]{2,1,0:T(1,128)} %reshape.187), calls=%async_computation.10 | async-start | bytes 262144 | tf_op jit(solution)/shard_map/all_to_all | solution.py:62
  363.7 58.9 %all-to-all-start.4 = ((f32[2,2,128,1024]{3,1,0,2:T(2,128)}), f32[2,2,128,1024]{3,1,0,2:T(2,128)S(1)}, u32[]{:S(2)}, u32[]{:S(2)}) async-start(f32[2,2,128,1024]{3,1,0,2:T(2,128)} %copy.85), calls=%async_computation.4 | async-start | bytes 4194304 | tf_op jit(solution)/shard_map/all_to_all | solution.py:62
  422.6 15.4 %all-to-all-start.11 = ((f32[64,1,128]{2,1,0:T(1,128)}), f32[64,1,128]{2,1,0:T(1,128)S(1)}, u32[]{:S(2)}, u32[]{:S(2)}) async-start(f32[64,1,128]{2,1,0:T(1,128)} %reshape.189), calls=%async_computation.11 | async-start | bytes 65536 | tf_op jit(solution)/shard_map/all_to_all | solution.py:67
  433.6 29.5 %copy-start.2 = (bf16[128,1024]{1,0:T(8,128)(2,1)S(1)}, bf16[128,1024]{1,0:T(8,128)(2,1)}, u32[]{:S(2)}) copy-start(bf16[128,1024]{1,0:T(8,128)(2,1)} %param.5) | copy-start | bytes 786436
  433.6 29.5 %copy-start.3 = (bf16[128,1024]{1,0:T(8,128)(2,1)S(1)}, bf16[128,1024]{1,0:T(8,128)(2,1)}, u32[]{:S(2)}) copy-start(bf16[128,1024]{1,0:T(8,128)(2,1)} %param.9) | copy-start | bytes 786436
  438.0 24.6 %all-to-all-start.5 = ((f32[64,2,1024]{2,1,0:T(2,128)}), f32[64,2,1024]{2,1,0:T(2,128)S(1)}, u32[]{:S(2)}, u32[]{:S(2)}) async-start(f32[64,2,1024]{2,1,0:T(2,128)} %copy.89), calls=%async_computation.5 | async-start | bytes 1048576 | tf_op jit(solution)/shard_map/all_to_all | solution.py:67
where the time goes:
time: 474 us; the launch traced here: 464 us
  blocking collectives  161 us (34%)
  waiting for transfers between devices  142 us (30%)
  starting transfers between devices  68.2 us (14%)
  local copies, waits for them, and re-layouts  38.9 us (8%)
  matrix products  37.5 us (8%)
  other arithmetic  15.1 us (3%)
    all_to_all x1, blocking collectives, transpose_forward(): lax.all_to_all(jnp.stack([spread_re, spread_im]), 'context', split_axis=1...  57.5 us
    all_to_all x1, blocking collectives, transpose_inverse(): lax.all_to_all(spec, 'context', split_axis=2, concat_axis=1, tiled=True)  57.5 us
    all_to_all x2, waiting for transfers between devices, transpose_inverse(): lax.all_to_all(spec, 'context', split_axis=2, concat_axis=1, tiled=True)  51 us
    all_to_all x2, waiting for transfers between devices, transpose_forward(): lax.all_to_all(jnp.stack([spread_re, spread_im]), 'context', split_axis=1...  50.4 us
    all_to_all x2, starting transfers between devices, transpose_forward(): lax.all_to_all(jnp.stack([spread_re, spread_im]), 'context', split_axis=1...  23.6 us
    all_to_all x1, blocking collectives, transpose_forward(): lax.all_to_all(signal[None], 'context', split_axis=1, concat_axis=0, tile...  23.4 us
    all_to_all x1, blocking collectives, transpose_inverse(): lax.all_to_all(values, 'context', split_axis=0, concat_axis=1, tiled=True)  22.9 us
    all_to_all x2, waiting for transfers between devices, transpose_forward(): lax.all_to_all(signal[None], 'context', split_axis=1, concat_axis=0, tile...  21.4 us
  transfers between devices with their start and end apart: 8, of which 8 were waited for; matrix products, arithmetic and copies ran while one was open for 7% of the time, Pallas kernels for 0%

commit v1 on v0

v1 whole, which is shorter than its diff:
```python
import math

import jax
import jax.numpy as jnp
import ml_dtypes
import numpy as np
from jax import lax
from jax.experimental import pallas as pl
from jax.experimental.pallas import tpu as pltpu
from jax.sharding import PartitionSpec as P

bf16 = jnp.bfloat16
f32 = jnp.float32


def split_table(table):
    high = table.astype(np.float32).astype(ml_dtypes.bfloat16)
    low = (table - high.astype(np.float64)).astype(np.float32).astype(ml_dtypes.bfloat16)
    return high, low


def tables(blocks, inner, scale):
    points = 2 * blocks * inner
    a = np.arange(blocks)
    b = np.arange(inner)
    odd = 2 * np.arange(blocks) + 1
    across = np.pi * np.outer(odd, a) / (2 * blocks)
    fore = np.concatenate([np.cos(across), -np.sin(across)], axis=0)
    back = np.concatenate([np.cos(across), -np.sin(across)], axis=0).T
    fore_high, fore_low = split_table(fore)
    back_high, back_low = split_table(back)
    turn = np.pi * np.outer(odd, b) / points
    turn_fore = np.stack([np.cos(turn), -np.sin(turn)]).astype(np.float32)
    turn_back = (np.stack([np.cos(turn), np.sin(turn)]) * (2.0 * scale / points)).astype(np.float32)
    within = 2 * np.pi * np.outer(b, b) / inner
    cosine, sine = np.cos(within), np.sin(within)
    wide_fore = np.block([[cosine, -sine], [sine, cosine]])
    wide_back = np.block([[cosine, sine], [-sine, cosine]])
    fh, fl = split_table(wide_fore)
    bh, bl = split_table(wide_back)
    return (
        np.concatenate([fore_high, fore_high, fore_low], axis=1),
        np.concatenate([back_high, back_high, back_low], axis=1),
        np.concatenate([fh, fh, fl], axis=0),
        np.concatenate([bh, bh, bl], axis=0),
        turn_fore,
        turn_back,
    )


def halves(value):
    high = value.astype(bf16)
    return high, (value - high.astype(f32)).astype(bf16)


def dot(left, right):
    return jnp.dot(left, right, preferred_element_type=f32)


def pack_kernel(peers, lanes, query_ref, key_ref, value_ref, filter_ref, grad_ref, out_ref, turned_ref):
    rows = 2 * lanes + 1
    width = peers * lanes
    for index, (left, right) in enumerate(((key_ref, value_ref), (grad_ref, query_ref))):
        for start in range(0, width, 128):
            part = pl.ds(start, 128)
            product = left[:, part].astype(f32) * right[:, part].astype(f32)
            turned_ref[pl.ds(index * width + start, 128), :] = product.T
    for index in range(2):
        for lane in range(lanes):
            out_ref[pl.ds(index * lanes + lane, peers, stride=rows), :] = turned_ref[
                pl.ds(index * width + lane, peers, stride=lanes), :
            ]
    out_ref[pl.ds(2 * lanes, peers, stride=rows), :] = filter_ref[...].T


def convolve_kernel(
    peers,
    lanes,
    in_ref,
    fore_ref,
    back_ref,
    wide_fore_ref,
    wide_back_ref,
    turn_fore_ref,
    turn_back_ref,
    out_ref,
    high_ref,
    low_ref,
):
    rows = 2 * lanes + 1
    inner = in_ref.shape[1]
    chunk = 4

    def place(first, count=1):
        return pl.ds(first * peers, count * peers)

    def put(first, value):
        high, low = halves(value)
        here = pl.ds(first * peers, value.shape[0])
        high_ref[here, :] = high
        low_ref[here, :] = low

    def transformed(first, count, table_ref):
        high = high_ref[place(first, count), :]
        low = low_ref[place(first, count), :]
        return dot(jnp.concatenate([high, low, high], axis=1), table_ref[...])

    def rotated(real, imag, turn_ref):
        cosine, sine = turn_ref[0], turn_ref[1]
        return jnp.concatenate(
            [real * cosine - imag * sine, real * sine + imag * cosine], axis=1
        )

    fore = fore_ref[...]
    order = [2 * lanes] + list(range(2 * lanes))
    for start in range(0, rows, 2):
        chosen = order[start : start + 2]
        columns = []
        for row in chosen:
            high, low = halves(in_ref[pl.ds(row, peers, stride=rows), :])
            columns.append(jnp.concatenate([high, low, high], axis=0))
        spread = dot(fore, jnp.concatenate(columns, axis=1))
        for index, row in enumerate(chosen):
            part = spread[:, index * inner : (index + 1) * inner]
            put(row, rotated(part[:peers], part[peers:], turn_fore_ref))

    filt = transformed(2 * lanes, 1, wide_fore_ref)
    filt_re, filt_im = filt[:, :inner], filt[:, inner:]
    corr_re = jnp.zeros((peers, inner), f32)
    corr_im = jnp.zeros((peers, inner), f32)
    for first in range(0, lanes, chunk):
        gated = transformed(first, chunk, wide_fore_ref)
        grad = transformed(lanes + first, chunk, wide_fore_ref)
        for index in range(chunk):
            part = slice(index * peers, (index + 1) * peers)
            gated_re, gated_im = gated[part, :inner], gated[part, inner:]
            grad_re, grad_im = grad[part, :inner], grad[part, inner:]
            put(
                first + index,
                jnp.concatenate(
                    [
                        gated_re * filt_re - gated_im * filt_im,
                        gated_re * filt_im + gated_im * filt_re,
                    ],
                    axis=1,
                ),
            )
            put(
                lanes + first + index,
                jnp.concatenate(
                    [
                        filt_re * grad_re + filt_im * grad_im,
                        filt_re * grad_im - filt_im * grad_re,
                    ],
                    axis=1,
                ),
            )
            corr_re = corr_re + (gated_re * grad_re + gated_im * grad_im)
            corr_im = corr_im + (gated_re * grad_im - gated_im * grad_re)
    put(2 * lanes, jnp.concatenate([corr_re, corr_im], axis=1))

    back = back_ref[...]
    for first in range(0, rows, chunk):
        count = min(chunk, rows - first)
        spec = transformed(first, count, wide_back_ref)
        for start in range(0, count, 2):
            columns = []
            for index in range(start, min(start + 2, count)):
                part = spec[index * peers : (index + 1) * peers]
                turned = rotated(part[:, :inner], part[:, inner:], turn_back_ref)
                stacked = jnp.concatenate([turned[:, :inner], turned[:, inner:]], axis=0)
                high, low = halves(stacked)
                columns.append(jnp.concatenate([high, low, high], axis=0))
            signal = dot(back, jnp.concatenate(columns, axis=1))
            for index in range(len(columns)):
                out_ref[pl.ds(first + start + index, peers, stride=rows), :] = signal[
                    :, index * inner : (index + 1) * inner
                ]


def unpack_kernel(
    peers,
    lanes,
    in_ref,
    query_ref,
    key_ref,
    value_ref,
    grad_ref,
    output_ref,
    grad_query_ref,
    grad_key_ref,
    grad_value_ref,
    grad_filter_ref,
    turned_ref,
):
    rows = 2 * lanes + 1
    width = peers * lanes
    for index in range(2):
        for lane in range(lanes):
            turned_ref[pl.ds(index * width + lane, peers, stride=lanes), :] = in_ref[
                pl.ds(index * lanes + lane, peers, stride=rows), :
            ]
    for start in range(0, width, 128):
        part = pl.ds(start, 128)
        conv = turned_ref[part, :].T
        output_ref[:, part] = (query_ref[:, part].astype(f32) * conv).astype(bf16)
        grad_query_ref[:, part] = (grad_ref[:, part].astype(f32) * conv).astype(bf16)
        grad_gated = turned_ref[pl.ds(width + start, 128), :].T
        grad_key_ref[:, part] = (grad_gated * value_ref[:, part].astype(f32)).astype(bf16)
        grad_value_ref[:, part] = (grad_gated * key_ref[:, part].astype(f32)).astype(bf16)
    grad_filter_ref[...] = in_ref[pl.ds(2 * lanes, peers, stride=rows), :].T


def exchange(signal, rows):
    pieces = signal.reshape(signal.shape[0], 1, signal.shape[1])
    pieces = lax.all_to_all(pieces, "context", 0, 0, tiled=True)
    return pieces.reshape(signal.shape)


def solution(mesh):
    peers = mesh.shape["context"]
    params = pltpu.CompilerParams(vmem_limit_bytes=48 * 1024 * 1024)

    def local(query_gate, key_gate, value_in, filter_raw, grad_out):
        inner, width = query_gate.shape
        lanes = width // filter_raw.shape[1]
        rows = 2 * lanes + 1
        scale = 1.0 / math.sqrt(peers * inner)
        packed = jax.ShapeDtypeStruct((peers * rows, inner), f32)
        turned = pltpu.VMEM((2 * width, inner), f32)
        sent = pl.pallas_call(
            lambda *refs: pack_kernel(peers, lanes, *refs),
            out_shape=packed,
            scratch_shapes=[turned],
            compiler_params=params,
            name="pack",
        )(query_gate, key_gate, value_in, filter_raw, grad_out)
        held = exchange(sent, rows)
        result = pl.pallas_call(
            lambda *refs: convolve_kernel(peers, lanes, *refs),
            out_shape=packed,
            scratch_shapes=[pltpu.VMEM((peers * rows, 2 * inner), bf16)] * 2,
            compiler_params=params,
            name="convolve",
        )(held, *(jnp.asarray(table) for table in tables(peers, inner, scale)))
        back = exchange(result, rows)
        wide = jax.ShapeDtypeStruct((inner, width), bf16)
        return pl.pallas_call(
            lambda *refs: unpack_kernel(peers, lanes, *refs),
            out_shape=(wide, wide, wide, wide, jax.ShapeDtypeStruct(filter_raw.shape, f32)),
            scratch_shapes=[turned],
            compiler_params=params,
            name="unpack",
        )(back, query_gate, key_gate, value_in, grad_out)

    spec = P("context", "tensor")
    return jax.shard_map(
        local, mesh=mesh, in_specs=(spec,) * 5, out_specs=(spec,) * 5, check_vma=False
    )
```

time: 474 us -> 91.4 us (0.19); the launches traced: 464 us -> 91 us
  waiting for transfers between devices: 142 us -> 0 us
  blocking collectives: 161 us -> 77.6 us
  starting transfers between devices: 68.2 us -> 0 us
  matrix products: 37.5 us -> 0 us
  local copies, waits for them, and re-layouts: 38.9 us -> 5.41 us
  other arithmetic: 15.1 us -> 0 us
  Pallas kernels: 0 us -> 7.27 us
    all_to_all x8 -> x0, waiting for transfers between devices: 142 us -> none  [the longest x2 51 us: transpose_inverse(): lax.all_to_all(spec, 'context', split_axis=2, concat_axis=1, tiled=True)]
    all_to_all x4 -> x2, blocking collectives: 161 us -> 77.6 us  [exchange(): pieces = lax.all_to_all(pieces, 'context', 0, 0, tiled=True)]
    all_to_all x8 -> x0, starting transfers between devices: 68.2 us -> none  [the longest x2 23.6 us: transpose_forward(): lax.all_to_all(jnp.stack([spread_re, spread_im]), 'context', split_axis=1...]
    dot_general x34 -> x0, matrix products: 36.8 us -> none  [the longest x3 5.72 us: forward(): jnp.einsum('br,erc->ebc', sin_local, tw_im, precision=highest)]
    another operation x6 -> x0, local copies, waits for them, and re-layouts: 9.84 us -> none  [the longest x3 5.07 us: turned(): return jnp.stack([rot_re, rot_im])]
    pallas_call x0 -> x3, Pallas kernels: none -> 7.27 us  [the longest x1 5.07 us: local(): pl.pallas_call(lambda *refs: convolve_kernel(peers, lanes, *refs), out_sh...]
    slice x14 -> x0, local copies, waits for them, and re-layouts: 6.25 us -> none  [the longest x6 2.9 us: transpose_inverse(): pieces[1]]
    all_to_all x6 -> x0, other arithmetic: 5.83 us -> none  [the longest x3 3.2 us: transpose_forward(): lax.all_to_all(signal[None], 'context', split_axis=1, concat_axis=0, tile...]
  transfers between devices with their start and end apart: 8 -> 0, of which waited for: 8 -> 0; matrix products, arithmetic and copies ran while one was open for 7% -> 0% of each run, Pallas kernels for 0% -> 0%
where the time goes in v1:
time: 91.4 us; the launch traced here: 91 us
  blocking collectives  77.6 us (85%)
  Pallas kernels  7.27 us (8%)
  local copies, waits for them, and re-layouts  5.41 us (6%)
    all_to_all x2, blocking collectives, exchange(): pieces = lax.all_to_all(pieces, 'context', 0, 0, tiled=True)  77.6 us
    pallas_call x1, Pallas kernels, local(): pl.pallas_call(lambda *refs: convolve_kernel(peers, lanes, *refs), out_sh...  5.07 us
    unnamed x29, local copies, waits for them, and re-layouts  4.71 us

profile of v1, /device:TPU:1, one launch (start us, length us, event | category | flops | bytes accessed | tf_op | source)
XLA Modules:
  0.0 91.0 jit_solution(16432123336977102025)
XLA Ops:
  0.6 0.8 copy.18.refs_3_
  1.5 0.0 copy-start
  1.5 0.9 %copy-done = bf16[128,1024]{1,0:T(8,128)(2,1)S(1)} copy-done((bf16[128,1024]{1,0:T(8,128)(2,1)S(1)}, bf16[128,1024]{1,0:T(8,128)(2,1)}, u32[]{:S(2)}) %copy-start) | copy-done | bytes 262168
  2.4 0.0 copy-start.2
  2.4 0.9 %copy-done.2 = bf16[128,1024]{1,0:T(8,128)(2,1)S(1)} copy-done((bf16[128,1024]{1,0:T(8,128)(2,1)S(1)}, bf16[128,1024]{1,0:T(8,128)(2,1)}, u32[]{:S(2)}) %copy-start.2) | copy-done | bytes 262168
  3.4 0.0 copy-start.4
  3.4 0.9 %copy-done.4 = bf16[128,1024]{1,0:T(8,128)(2,1)S(1)} copy-done((bf16[128,1024]{1,0:T(8,128)(2,1)S(1)}, bf16[128,1024]{1,0:T(8,128)(2,1)}, u32[]{:S(2)}) %copy-start.4) | copy-done | bytes 262168
  4.3 0.0 copy-start.6
  4.3 0.9 %copy-done.6 = bf16[128,1024]{1,0:T(8,128)(2,1)S(1)} copy-done((bf16[128,1024]{1,0:T(8,128)(2,1)S(1)}, bf16[128,1024]{1,0:T(8,128)(2,1)}, u32[]{:S(2)}) %copy-start.6) | copy-done | bytes 262168
  5.3 0.5 pack.1
  5.8 0.0 copy-start.8
  5.9 0.0 copy-start.9
  5.9 0.0 copy-start.10
  5.9 0.0 copy-start.11
  5.9 0.0 copy-start.12
  5.9 0.0 copy-start.13
  5.9 42.2 %all_to_all.10 = f32[2112,1,128]{2,1,0:T(1,128)S(1)} all-to-all(f32[2112,1,128]{2,1,0:T(1,128)S(1)} %bitcast.11), channel_id=1, replica_groups=mesh['tensor'=4,'context'=64] {'context'}, dimensions={0} | all-to-all | bytes 2162688 | tf_op jit(solution)/shard_map/all_to_all | solution.py:216
  48.1 0.0 copy-done.8
  48.1 0.0 copy-done.9
  48.1 0.0 copy-done.10
  48.1 0.0 copy-done.11
  48.1 0.0 copy-done.12
  48.1 0.0 copy-done.13
  48.1 5.1 %convolve.1 = f32[2112,128]{1,0:T(8,128)S(1)} custom-call(f32[2112,128]{1,0:T(8,128)S(1)} %bitcast.8, bf16[128,192]{1,0:T(8,128)(2,1)S(1)} %copy-done.12, bf16[64,384]{1,0:T(8,128)(2,1)S(1)} %copy-done.13, bf16[768,256]{1,0:T(8,128)(2,1)S(1)} %copy-done.9, bf16[768,256]{1,0:T(8,128)(2,1)S(1)} %copy-done.8, f32[2,64,128]{2,1,0:T(8,128)S(1)} %copy-done.11, ...), custom_call_target="tpu_custom_call" | custom-call | tf_op jit(solution)/shard_map/convolve/pallas_call | solution.py:239
  53.2 0.0 copy-start.1
  53.2 0.0 copy-start.3
  53.2 0.0 copy-start.5
  53.2 0.0 copy-start.7
  53.3 35.4 %all_to_all.11 = f32[2112,1,128]{2,1,0:T(1,128)S(1)} all-to-all(f32[2112,1,128]{2,1,0:T(1,128)S(1)} %bitcast.9), channel_id=1, replica_groups=mesh['tensor'=4,'context'=64] {'context'}, dimensions={0} | all-to-all | bytes 2162688 | tf_op jit(solution)/shard_map/all_to_all | solution.py:216
  88.6 0.0 copy-done.1
  88.6 0.0 copy-done.3
  88.6 0.0 copy-done.5
  88.6 0.0 copy-done.7
  88.7 1.7 %unpack.1 = (bf16[128,1024]{1,0:T(8,128)(2,1)}, bf16[128,1024]{1,0:T(8,128)(2,1)}, bf16[128,1024]{1,0:T(8,128)(2,1)}, bf16[128,1024]{1,0:T(8,128)(2,1)}, f32[128,64]{1,0:T(8,128)S(1)}) custom-call(f32[2112,128]{1,0:T(8,128)S(1)} %bitcast.10, bf16[128,1024]{1,0:T(8,128)(2,1)S(1)} %copy-done.1, bf16[128,1024]{1,0:T(8,128)(2,1)S(1)} %copy-done.3, ...), custom_call_target="tpu_custom_call" | custom-call | tf_op jit(solution)/shard_map/unpack/pallas_call | solution.py:248
  90.3 0.7 copy.21
Async XLA Ops:
  1.5 1.0 %copy-start = (bf16[128,1024]{1,0:T(8,128)(2,1)S(1)}, bf16[128,1024]{1,0:T(8,128)(2,1)}, u32[]{:S(2)}) copy-start(bf16[128,1024]{1,0:T(8,128)(2,1)} %refs_1_.4) | copy-start | bytes 786436
  2.4 0.9 %copy-start.2 = (bf16[128,1024]{1,0:T(8,128)(2,1)S(1)}, bf16[128,1024]{1,0:T(8,128)(2,1)}, u32[]{:S(2)}) copy-start(bf16[128,1024]{1,0:T(8,128)(2,1)} %refs_2_.4) | copy-start | bytes 786436
  3.4 0.9 %copy-start.4 = (bf16[128,1024]{1,0:T(8,128)(2,1)S(1)}, bf16[128,1024]{1,0:T(8,128)(2,1)}, u32[]{:S(2)}) copy-start(bf16[128,1024]{1,0:T(8,128)(2,1)} %refs_3_.3) | copy-start | bytes 786436
  4.3 0.9 %copy-start.6 = (bf16[128,1024]{1,0:T(8,128)(2,1)S(1)}, bf16[128,1024]{1,0:T(8,128)(2,1)}, u32[]{:S(2)}) copy-start(bf16[128,1024]{1,0:T(8,128)(2,1)} %refs_4_.4) | copy-start | bytes 786436
  5.8 42.3 %copy-start.8 = (bf16[768,256]{1,0:T(8,128)(2,1)S(1)}, bf16[768,256]{1,0:T(8,128)(2,1)}, u32[]{:S(2)}) copy-start(bf16[768,256]{1,0:T(8,128)(2,1)} %constant.15.clone.refs_4_) | copy-start | bytes 1179652
  5.9 42.2 %copy-start.9 = (bf16[768,256]{1,0:T(8,128)(2,1)S(1)}, bf16[768,256]{1,0:T(8,128)(2,1)}, u32[]{:S(2)}) copy-start(bf16[768,256]{1,0:T(8,128)(2,1)} %constant.14.clone.refs_3_) | copy-start | bytes 1179652
  5.9 42.2 %copy-start.10 = (f32[2,64,128]{2,1,0:T(8,128)S(1)}, f32[2,64,128]{2,1,0:T(8,128)}, u32[]{:S(2)}) copy-start(f32[2,64,128]{2,1,0:T(8,128)} %constant.17.clone.refs_6_) | copy-start | bytes 196612
  5.9 42.2 %copy-start.11 = (f32[2,64,128]{2,1,0:T(8,128)S(1)}, f32[2,64,128]{2,1,0:T(8,128)}, u32[]{:S(2)}) copy-start(f32[2,64,128]{2,1,0:T(8,128)} %constant.16.clone.refs_5_) | copy-start | bytes 196612
  5.9 42.2 %copy-start.12 = (bf16[128,192]{1,0:T(8,128)(2,1)S(1)}, bf16[128,192]{1,0:T(8,128)(2,1)}, u32[]{:S(2)}) copy-start(bf16[128,192]{1,0:T(8,128)(2,1)} %constant.12.clone.refs_1_) | copy-start | bytes 147460
  5.9 42.2 %copy-start.13 = (bf16[64,384]{1,0:T(8,128)(2,1)S(1)}, bf16[64,384]{1,0:T(8,128)(2,1)}, u32[]{:S(2)}) copy-start(bf16[64,384]{1,0:T(8,128)(2,1)} %constant.13.clone.refs_2_) | copy-start | bytes 147460
  53.2 35.4 %copy-start.1 = (bf16[128,1024]{1,0:T(8,128)(2,1)S(1)}, bf16[128,1024]{1,0:T(8,128)(2,1)}, u32[]{:S(2)}) copy-start(bf16[128,1024]{1,0:T(8,128)(2,1)} %refs_1_.4) | copy-start | bytes 786436
  53.2 35.4 %copy-start.3 = (bf16[128,1024]{1,0:T(8,128)(2,1)S(1)}, bf16[128,1024]{1,0:T(8,128)(2,1)}, u32[]{:S(2)}) copy-start(bf16[128,1024]{1,0:T(8,128)(2,1)} %refs_2_.4) | copy-start | bytes 786436
  53.2 35.4 %copy-start.5 = (bf16[128,1024]{1,0:T(8,128)(2,1)S(1)}, bf16[128,1024]{1,0:T(8,128)(2,1)}, u32[]{:S(2)}) copy-start(bf16[128,1024]{1,0:T(8,128)(2,1)} %refs_3_.3) | copy-start | bytes 786436
  53.2 35.4 %copy-start.7 = (bf16[128,1024]{1,0:T(8,128)(2,1)S(1)}, bf16[128,1024]{1,0:T(8,128)(2,1)}, u32[]{:S(2)}) copy-start(bf16[128,1024]{1,0:T(8,128)(2,1)} %refs_4_.4) | copy-start | bytes 786436

commit v2 on v1

--- a/solution.py
+++ b/solution.py
@@ -57,20 +57,57 @@
     return jnp.dot(left, right, preferred_element_type=f32)
 
 
-def pack_kernel(peers, lanes, query_ref, key_ref, value_ref, filter_ref, grad_ref, out_ref, turned_ref):
+def pack_kernel(
+    peers,
+    lanes,
+    parts,
+    query_hbm,
+    key_hbm,
+    value_hbm,
+    filter_hbm,
+    grad_hbm,
+    out_ref,
+    query_ref,
+    key_ref,
+    value_ref,
+    grad_ref,
+    filter_ref,
+    turned_ref,
+    sems,
+):
     rows = 2 * lanes + 1
     width = peers * lanes
-    for index, (left, right) in enumerate(((key_ref, value_ref), (grad_ref, query_ref))):
-        for start in range(0, width, 128):
-            part = pl.ds(start, 128)
-            product = left[:, part].astype(f32) * right[:, part].astype(f32)
-            turned_ref[pl.ds(index * width + start, 128), :] = product.T
-    for index in range(2):
+    span = width // parts
+    pairs = (
+        ((key_hbm, key_ref), (value_hbm, value_ref)),
+        ((grad_hbm, grad_ref), (query_hbm, query_ref)),
+    )
+    copies = {}
+    for index, pair in enumerate(pairs):
+        for part in range(parts):
+            for side, (source, target) in enumerate(pair):
+                columns = pl.ds(part * span, span)
+                copy = pltpu.make_async_copy(
+                    source.at[:, columns], target.at[:, columns], sems.at[index, side, part]
+                )
+                copy.start()
+                copies[index, side, part] = copy
+    filter_copy = pltpu.make_async_copy(filter_hbm, filter_ref, sems.at[2, 0, 0])
+    filter_copy.start()
+    for index, ((_, left), (_, right)) in enumerate(pairs):
+        for part in range(parts):
+            copies[index, 0, part].wait()
+            copies[index, 1, part].wait()
+            for start in range(part * span, (part + 1) * span, 128):
+                columns = pl.ds(start, 128)
+                product = left[:, columns].astype(f32) * right[:, columns].astype(f32)
+                turned_ref[pl.ds(index * width + start, 128), :] = product.T
         for lane in range(lanes):
             out_ref[pl.ds(index * lanes + lane, peers, stride=rows), :] = turned_ref[
                 pl.ds(index * width + lane, peers, stride=lanes), :
             ]
-    out_ref[pl.ds(2 * lanes, peers, stride=rows), :] = filter_ref[...].T
+    filter_copy.wait()
+    out_ref[pl.ds(2 * lanes, peers, stride=rows), :] = filter_ref[...]
 
 
 def convolve_kernel(
@@ -159,59 +196,89 @@
             corr_im = corr_im + (gated_re * grad_im - gated_im * grad_re)
     put(2 * lanes, jnp.concatenate([corr_re, corr_im], axis=1))
 
-    back = back_ref[...]
     for first in range(0, rows, chunk):
         count = min(chunk, rows - first)
         spec = transformed(first, count, wide_back_ref)
-        for start in range(0, count, 2):
-            columns = []
-            for index in range(start, min(start + 2, count)):
-                part = spec[index * peers : (index + 1) * peers]
-                turned = rotated(part[:, :inner], part[:, inner:], turn_back_ref)
-                stacked = jnp.concatenate([turned[:, :inner], turned[:, inner:]], axis=0)
-                high, low = halves(stacked)
-                columns.append(jnp.concatenate([high, low, high], axis=0))
-            signal = dot(back, jnp.concatenate(columns, axis=1))
-            for index in range(len(columns)):
-                out_ref[pl.ds(first + start + index, peers, stride=rows), :] = signal[
-                    :, index * inner : (index + 1) * inner
-                ]
+        for index in range(count):
+            part = spec[index * peers : (index + 1) * peers]
+            put(first + index, rotated(part[:, :inner], part[:, inner:], turn_back_ref))
+
+    back = back_ref[...]
+    for start in range(0, rows, 2):
+        columns = []
+        for row in range(start, min(start + 2, rows)):
+            high, low = high_ref[place(row), :], low_ref[place(row), :]
+            high = jnp.concatenate([high[:, :inner], high[:, inner:]], axis=0)
+            low = jnp.concatenate([low[:, :inner], low[:, inner:]], axis=0)
+            columns.append(jnp.concatenate([high, low, high], axis=0))
+        signal = dot(back, jnp.concatenate(columns, axis=1))
+        for index in range(len(columns)):
+            out_ref[pl.ds(start + index, peers, stride=rows), :] = signal[
+                :, index * inner : (index + 1) * inner
+            ]
 
 
 def unpack_kernel(
     peers,
     lanes,
+    parts,
     in_ref,
     query_ref,
     key_ref,
     value_ref,
     grad_ref,
+    output_hbm,
+    grad_query_hbm,
+    grad_key_hbm,
+    grad_value_hbm,
+    grad_filter_hbm,
     output_ref,
     grad_query_ref,
     grad_key_ref,
     grad_value_ref,
     grad_filter_ref,
     turned_ref,
+    sems,
 ):
     rows = 2 * lanes + 1
     width = peers * lanes
-    for index in range(2):
+    span = width // parts
+    grad_filter_ref[...] = in_ref[pl.ds(2 * lanes, peers, stride=rows), :]
+    copies = [pltpu.make_async_copy(grad_filter_ref, grad_filter_hbm, sems.at[4, 0])]
+    copies[0].start()
+    sides = (
+        (
+            (query_ref, output_ref, output_hbm),
+            (grad_ref, grad_query_ref, grad_query_hbm),
+        ),
+        (
+            (value_ref, grad_key_ref, grad_key_hbm),
+            (key_ref, grad_value_ref, grad_value_hbm),
+        ),
+    )
+    for index, pair in enumerate(sides):
         for lane in range(lanes):
             turned_ref[pl.ds(index * width + lane, peers, stride=lanes), :] = in_ref[
                 pl.ds(index * lanes + lane, peers, stride=rows), :
             ]
-    for start in range(0, width, 128):
-        part = pl.ds(start, 128)
-        conv = turned_ref[part, :].T
-        output_ref[:, part] = (query_ref[:, part].astype(f32) * conv).astype(bf16)
-        grad_query_ref[:, part] = (grad_ref[:, part].astype(f32) * conv).astype(bf16)
-        grad_gated = turned_ref[pl.ds(width + start, 128), :].T
-        grad_key_ref[:, part] = (grad_gated * value_ref[:, part].astype(f32)).astype(bf16)
-        grad_value_ref[:, part] = (grad_gated * key_ref[:, part].astype(f32)).astype(bf16)
-    grad_filter_ref[...] = in_ref[pl.ds(2 * lanes, peers, stride=rows), :].T
-
-
-def exchange(signal, rows):
+        for part in range(parts):
+            for start in range(part * span, (part + 1) * span, 128):
+                columns = pl.ds(start, 128)
+                signal = turned_ref[pl.ds(index * width + start, 128), :].T
+                for factor, target, _ in pair:
+                    target[:, columns] = (factor[:, columns].astype(f32) * signal).astype(bf16)
+            columns = pl.ds(part * span, span)
+            for side, (_, source, target) in enumerate(pair):
+                copy = pltpu.make_async_copy(
+                    source.at[:, columns], target.at[:, columns], sems.at[2 * index + side, part]
+                )
+                copy.start()
+                copies.append(copy)
+    for copy in copies:
+        copy.wait()
+
+
+def exchange(signal):
     pieces = signal.reshape(signal.shape[0], 1, signal.shape[1])
     pieces = lax.all_to_all(pieces, "context", 0, 0, tiled=True)
     return pieces.reshape(signal.shape)
@@ -228,14 +295,24 @@
         scale = 1.0 / math.sqrt(peers * inner)
         packed = jax.ShapeDtypeStruct((peers * rows, inner), f32)
         turned = pltpu.VMEM((2 * width, inner), f32)
+        held_wide = pltpu.VMEM((inner, width), bf16)
+        held_filter = pltpu.VMEM((peers, inner), f32)
+        parts = 4
         sent = pl.pallas_call(
-            lambda *refs: pack_kernel(peers, lanes, *refs),
+            lambda *refs: pack_kernel(peers, lanes, parts, *refs),
             out_shape=packed,
-            scratch_shapes=[turned],
+            in_specs=[pl.BlockSpec(memory_space=pltpu.HBM)] * 5,
+            scratch_shapes=[held_wide] * 4
+            + [held_filter, turned, pltpu.SemaphoreType.DMA((3, 2, parts))],
             compiler_params=params,
             name="pack",
-        )(query_gate, key_gate, value_in, filter_raw, grad_out)
-        held = exchange(sent, rows)
+        )(
+            *(
+                pltpu.with_memory_space_constraint(array, pltpu.HBM)
+                for array in (query_gate, key_gate, value_in, filter_raw.T, grad_out)
+            )
+        )
+        held = exchange(sent)
         result = pl.pallas_call(
             lambda *refs: convolve_kernel(peers, lanes, *refs),
             out_shape=packed,
@@ -243,15 +320,18 @@
             compiler_params=params,
             name="convolve",
         )(held, *(jnp.asarray(table) for table in tables(peers, inner, scale)))
-        back = exchange(result, rows)
+        back = exchange(result)
         wide = jax.ShapeDtypeStruct((inner, width), bf16)
-        return pl.pallas_call(
-            lambda *refs: unpack_kernel(peers, lanes, *refs),
-            out_shape=(wide, wide, wide, wide, jax.ShapeDtypeStruct(filter_raw.shape, f32)),
-            scratch_shapes=[turned],
+        *outputs, grad_filter = pl.pallas_call(
+            lambda *refs: unpack_kernel(peers, lanes, parts, *refs),
+            out_shape=(wide,) * 4 + (jax.ShapeDtypeStruct((peers, inner), f32),),
+            out_specs=(pl.BlockSpec(memory_space=pltpu.HBM),) * 5,
+            scratch_shapes=[held_wide] * 4
+            + [held_filter, turned, pltpu.SemaphoreType.DMA((5, parts))],
             compiler_params=params,
             name="unpack",
         )(back, query_gate, key_gate, value_in, grad_out)
+        return (*outputs, grad_filter.T)
 
     spec = P("context", "tensor")
     return jax.shard_map(

time: 91.4 us -> 85.2 us (0.932)
  local copies, waits for them, and re-layouts: 5.41 us -> 0.07 us
    unnamed x29 -> x20, local copies, waits for them, and re-layouts: 4.71 us -> 0.07 us
    pallas_call x1, Pallas kernels: 5.07 us -> 2.91 us  [local(): pl.pallas_call(lambda *refs: convolve_kernel(peers, lanes, *refs), out_sh...]
    pallas_call x2, Pallas kernels: 2.2 us -> 3.67 us  [the longest x1 2.25 us: local(): pl.pallas_call(lambda *refs: pack_kernel(peers, lanes, parts, *refs), out...]
where the time goes in v2:
time: 85.2 us; the launch traced here: 85 us
  blocking collectives  77.5 us (91%)
  Pallas kernels  6.58 us (8%)
    all_to_all x2, blocking collectives, exchange(): pieces = lax.all_to_all(pieces, 'context', 0, 0, tiled=True)  77.5 us
    pallas_call x1, Pallas kernels, local(): pl.pallas_call(lambda *refs: convolve_kernel(peers, lanes, *refs), out_sh...  2.91 us
    pallas_call x1, Pallas kernels, local(): pl.pallas_call(lambda *refs: pack_kernel(peers, lanes, parts, *refs), out...  2.25 us

profile of v2, /device:TPU:1, one launch (start us, length us, event | category | flops | bytes accessed | tf_op | source)
XLA Modules:
  0.0 85.0 jit_solution(16640793114903816638)
XLA Ops:
  0.6 2.2 %pack.1 = f32[2112,128]{1,0:T(8,128)S(1)} custom-call(bf16[128,1024]{1,0:T(8,128)(2,1)} %refs_1_.4, bf16[128,1024]{1,0:T(8,128)(2,1)} %refs_2_.4, bf16[128,1024]{1,0:T(8,128)(2,1)} %refs_3_.2, f32[64,128]{1,0:T(8,128)} %bitcast.14, bf16[128,1024]{1,0:T(8,128)(2,1)} %refs_4_.4), custom_call_target="tpu_custom_call" | custom-call | tf_op jit(solution)/shard_map/pack/pallas_call | solution.py:301
  2.9 0.0 copy-start.4
  2.9 0.0 copy-start.5
  2.9 0.0 copy-start.6
  2.9 0.0 copy-start.7
  2.9 0.0 copy-start.8
  2.9 0.0 copy-start.9
  3.0 42.2 %all_to_all.10 = f32[2112,1,128]{2,1,0:T(1,128)S(1)} all-to-all(f32[2112,1,128]{2,1,0:T(1,128)S(1)} %bitcast.13), channel_id=1, replica_groups=mesh['tensor'=4,'context'=64] {'context'}, dimensions={0} | all-to-all | bytes 2162688 | tf_op jit(solution)/shard_map/all_to_all | solution.py:283
  45.1 0.0 copy-done.4
  45.1 0.0 copy-done.5
  45.1 0.0 copy-done.6
  45.1 0.0 copy-done.7
  45.2 0.0 copy-done.8
  45.2 0.0 copy-done.9
  45.2 2.9 %convolve.1 = f32[2112,128]{1,0:T(8,128)S(1)} custom-call(f32[2112,128]{1,0:T(8,128)S(1)} %bitcast.10, bf16[128,192]{1,0:T(8,128)(2,1)S(1)} %copy-done.8, bf16[64,384]{1,0:T(8,128)(2,1)S(1)} %copy-done.9, bf16[768,256]{1,0:T(8,128)(2,1)S(1)} %copy-done.5, bf16[768,256]{1,0:T(8,128)(2,1)S(1)} %copy-done.4, f32[2,64,128]{2,1,0:T(8,128)S(1)} %copy-done.7, ...), custom_call_target="tpu_custom_call" | custom-call | tf_op jit(solution)/shard_map/convolve/pallas_call | solution.py:316
  48.1 0.0 copy-start
  48.1 0.0 copy-start.1
  48.1 0.0 copy-start.2
  48.1 0.0 copy-start.3
  48.1 35.4 %all_to_all.11 = f32[2112,1,128]{2,1,0:T(1,128)S(1)} all-to-all(f32[2112,1,128]{2,1,0:T(1,128)S(1)} %bitcast.11), channel_id=1, replica_groups=mesh['tensor'=4,'context'=64] {'context'}, dimensions={0} | all-to-all | bytes 2162688 | tf_op jit(solution)/shard_map/all_to_all | solution.py:283
  83.5 0.0 copy-done
  83.5 0.0 copy-done.1
  83.5 0.0 copy-done.2
  83.5 0.0 copy-done.3
  83.5 1.4 %unpack.1 = (bf16[128,1024]{1,0:T(8,128)(2,1)}, bf16[128,1024]{1,0:T(8,128)(2,1)}, bf16[128,1024]{1,0:T(8,128)(2,1)}, bf16[128,1024]{1,0:T(8,128)(2,1)}, f32[64,128]{1,0:T(8,128)}) custom-call(f32[2112,128]{1,0:T(8,128)S(1)} %bitcast.12, bf16[128,1024]{1,0:T(8,128)(2,1)S(1)} %copy-done, bf16[128,1024]{1,0:T(8,128)(2,1)S(1)} %copy-done.1, ...), custom_call_target="tpu_custom_call" | custom-call | tf_op jit(solution)/shard_map/unpack/pallas_call | solution.py:325
Async XLA Ops:
  2.9 42.3 %copy-start.4 = (bf16[768,256]{1,0:T(8,128)(2,1)S(1)}, bf16[768,256]{1,0:T(8,128)(2,1)}, u32[]{:S(2)}) copy-start(bf16[768,256]{1,0:T(8,128)(2,1)} %constant.15.clone.refs_4_) | copy-start | bytes 1179652
  2.9 42.2 %copy-start.5 = (bf16[768,256]{1,0:T(8,128)(2,1)S(1)}, bf16[768,256]{1,0:T(8,128)(2,1)}, u32[]{:S(2)}) copy-start(bf16[768,256]{1,0:T(8,128)(2,1)} %constant.14.clone.refs_3_) | copy-start | bytes 1179652
  2.9 42.2 %copy-start.6 = (f32[2,64,128]{2,1,0:T(8,128)S(1)}, f32[2,64,128]{2,1,0:T(8,128)}, u32[]{:S(2)}) copy-start(f32[2,64,128]{2,1,0:T(8,128)} %constant.17.clone.refs_6_) | copy-start | bytes 196612
  2.9 42.2 %copy-start.7 = (f32[2,64,128]{2,1,0:T(8,128)S(1)}, f32[2,64,128]{2,1,0:T(8,128)}, u32[]{:S(2)}) copy-start(f32[2,64,128]{2,1,0:T(8,128)} %constant.16.clone.refs_5_) | copy-start | bytes 196612
  2.9 42.2 %copy-start.8 = (bf16[128,192]{1,0:T(8,128)(2,1)S(1)}, bf16[128,192]{1,0:T(8,128)(2,1)}, u32[]{:S(2)}) copy-start(bf16[128,192]{1,0:T(8,128)(2,1)} %constant.12.clone.refs_1_) | copy-start | bytes 147460
  2.9 42.2 %copy-start.9 = (bf16[64,384]{1,0:T(8,128)(2,1)S(1)}, bf16[64,384]{1,0:T(8,128)(2,1)}, u32[]{:S(2)}) copy-start(bf16[64,384]{1,0:T(8,128)(2,1)} %constant.13.clone.refs_2_) | copy-start | bytes 147460
  48.1 35.4 %copy-start = (bf16[128,1024]{1,0:T(8,128)(2,1)S(1)}, bf16[128,1024]{1,0:T(8,128)(2,1)}, u32[]{:S(2)}) copy-start(bf16[128,1024]{1,0:T(8,128)(2,1)} %refs_1_.4) | copy-start | bytes 786436
  48.1 35.4 %copy-start.1 = (bf16[128,1024]{1,0:T(8,128)(2,1)S(1)}, bf16[128,1024]{1,0:T(8,128)(2,1)}, u32[]{:S(2)}) copy-start(bf16[128,1024]{1,0:T(8,128)(2,1)} %refs_2_.4) | copy-start | bytes 786436
  48.1 35.4 %copy-start.2 = (bf16[128,1024]{1,0:T(8,128)(2,1)S(1)}, bf16[128,1024]{1,0:T(8,128)(2,1)}, u32[]{:S(2)}) copy-start(bf16[128,1024]{1,0:T(8,128)(2,1)} %refs_3_.2) | copy-start | bytes 786436
  48.1 35.4 %copy-start.3 = (bf16[128,1024]{1,0:T(8,128)(2,1)S(1)}, bf16[128,1024]{1,0:T(8,128)(2,1)}, u32[]{:S(2)}) copy-start(bf16[128,1024]{1,0:T(8,128)(2,1)} %refs_4_.4) | copy-start | bytes 786436

commit v3 on v2

--- a/solution.py
+++ b/solution.py
@@ -72,7 +72,6 @@
     value_ref,
     grad_ref,
     filter_ref,
-    turned_ref,
     sems,
 ):
     rows = 2 * lanes + 1
@@ -101,11 +100,10 @@
             for start in range(part * span, (part + 1) * span, 128):
                 columns = pl.ds(start, 128)
                 product = left[:, columns].astype(f32) * right[:, columns].astype(f32)
-                turned_ref[pl.ds(index * width + start, 128), :] = product.T
-        for lane in range(lanes):
-            out_ref[pl.ds(index * lanes + lane, peers, stride=rows), :] = turned_ref[
-                pl.ds(index * width + lane, peers, stride=lanes), :
-            ]
+                turned = product.T
+                for offset in range(0, 128, lanes):
+                    first = (start + offset) // lanes * rows + index * lanes
+                    out_ref[pl.ds(first, lanes), :] = turned[offset : offset + lanes]
     filter_copy.wait()
     out_ref[pl.ds(2 * lanes, peers, stride=rows), :] = filter_ref[...]
 
@@ -237,7 +235,6 @@
     grad_key_ref,
     grad_value_ref,
     grad_filter_ref,
-    turned_ref,
     sems,
 ):
     rows = 2 * lanes + 1
@@ -257,14 +254,14 @@
         ),
     )
     for index, pair in enumerate(sides):
-        for lane in range(lanes):
-            turned_ref[pl.ds(index * width + lane, peers, stride=lanes), :] = in_ref[
-                pl.ds(index * lanes + lane, peers, stride=rows), :
-            ]
         for part in range(parts):
             for start in range(part * span, (part + 1) * span, 128):
                 columns = pl.ds(start, 128)
-                signal = turned_ref[pl.ds(index * width + start, 128), :].T
+                blocks = []
+                for offset in range(0, 128, lanes):
+                    first = (start + offset) // lanes * rows + index * lanes
+                    blocks.append(in_ref[pl.ds(first, lanes), :])
+                signal = jnp.concatenate(blocks, axis=0).T
                 for factor, target, _ in pair:
                     target[:, columns] = (factor[:, columns].astype(f32) * signal).astype(bf16)
             columns = pl.ds(part * span, span)
@@ -294,16 +291,14 @@
         rows = 2 * lanes + 1
         scale = 1.0 / math.sqrt(peers * inner)
         packed = jax.ShapeDtypeStruct((peers * rows, inner), f32)
-        turned = pltpu.VMEM((2 * width, inner), f32)
         held_wide = pltpu.VMEM((inner, width), bf16)
         held_filter = pltpu.VMEM((peers, inner), f32)
-        parts = 4
         sent = pl.pallas_call(
-            lambda *refs: pack_kernel(peers, lanes, parts, *refs),
+            lambda *refs: pack_kernel(peers, lanes, 1, *refs),
             out_shape=packed,
             in_specs=[pl.BlockSpec(memory_space=pltpu.HBM)] * 5,
             scratch_shapes=[held_wide] * 4
-            + [held_filter, turned, pltpu.SemaphoreType.DMA((3, 2, parts))],
+            + [held_filter, pltpu.SemaphoreType.DMA((3, 2, 1))],
             compiler_params=params,
             name="pack",
         )(
@@ -323,11 +318,11 @@
         back = exchange(result)
         wide = jax.ShapeDtypeStruct((inner, width), bf16)
         *outputs, grad_filter = pl.pallas_call(
-            lambda *refs: unpack_kernel(peers, lanes, parts, *refs),
+            lambda *refs: unpack_kernel(peers, lanes, 2, *refs),
             out_shape=(wide,) * 4 + (jax.ShapeDtypeStruct((peers, inner), f32),),
             out_specs=(pl.BlockSpec(memory_space=pltpu.HBM),) * 5,
             scratch_shapes=[held_wide] * 4
-            + [held_filter, turned, pltpu.SemaphoreType.DMA((5, parts))],
+            + [held_filter, pltpu.SemaphoreType.DMA((5, 2))],
             compiler_params=params,
             name="unpack",
         )(back, query_gate, key_gate, value_in, grad_out)

time: 85.2 us -> 84.2 us (0.988)
  Pallas kernels: 6.58 us -> 5.59 us
    pallas_call x2, Pallas kernels: 3.67 us -> 2.68 us  [the longest x1 1.5 us: local(): pl.pallas_call(lambda *refs: pack_kernel(peers, lanes, 1, *refs), out_sha...]
where the time goes in v3:
time: 84.2 us; the launch traced here: 84 us
  blocking collectives  77.6 us (92%)
  Pallas kernels  5.59 us (7%)
    all_to_all x2, blocking collectives, exchange(): pieces = lax.all_to_all(pieces, 'context', 0, 0, tiled=True)  77.6 us
    pallas_call x1, Pallas kernels, local(): pl.pallas_call(lambda *refs: convolve_kernel(peers, lanes, *refs), out_sh...  2.91 us

profile of v3, /device:TPU:1, one launch (start us, length us, event | category | flops | bytes accessed | tf_op | source)
XLA Modules:
  0.0 84.0 jit_solution(15543441345189831407)
XLA Ops:
  0.6 1.5 %pack.1 = f32[2112,128]{1,0:T(8,128)S(1)} custom-call(bf16[128,1024]{1,0:T(8,128)(2,1)} %refs_1_.4, bf16[128,1024]{1,0:T(8,128)(2,1)} %refs_2_.4, bf16[128,1024]{1,0:T(8,128)(2,1)} %refs_3_.2, f32[64,128]{1,0:T(8,128)} %bitcast.14, bf16[128,1024]{1,0:T(8,128)(2,1)} %refs_4_.4), custom_call_target="tpu_custom_call" | custom-call | tf_op jit(solution)/shard_map/pack/pallas_call | solution.py:296
  2.1 0.0 copy-start.4
  2.2 0.0 copy-start.5
  2.2 0.0 copy-start.6
  2.2 0.0 copy-start.7
  2.2 0.0 copy-start.8
  2.2 0.0 copy-start.9
  2.2 42.2 %all_to_all.10 = f32[2112,1,128]{2,1,0:T(1,128)S(1)} all-to-all(f32[2112,1,128]{2,1,0:T(1,128)S(1)} %bitcast.13), channel_id=1, replica_groups=mesh['tensor'=4,'context'=64] {'context'}, dimensions={0} | all-to-all | bytes 2162688 | tf_op jit(solution)/shard_map/all_to_all | solution.py:280
  44.4 0.0 copy-done.4
  44.4 0.0 copy-done.5
  44.4 0.0 copy-done.6
  44.4 0.0 copy-done.7
  44.4 0.0 copy-done.8
  44.4 0.0 copy-done.9
  44.4 2.9 %convolve.1 = f32[2112,128]{1,0:T(8,128)S(1)} custom-call(f32[2112,128]{1,0:T(8,128)S(1)} %bitcast.10, bf16[128,192]{1,0:T(8,128)(2,1)S(1)} %copy-done.8, bf16[64,384]{1,0:T(8,128)(2,1)S(1)} %copy-done.9, bf16[768,256]{1,0:T(8,128)(2,1)S(1)} %copy-done.5, bf16[768,256]{1,0:T(8,128)(2,1)S(1)} %copy-done.4, f32[2,64,128]{2,1,0:T(8,128)S(1)} %copy-done.7, ...), custom_call_target="tpu_custom_call" | custom-call | tf_op jit(solution)/shard_map/convolve/pallas_call | solution.py:311
  47.3 0.0 copy-start
  47.4 0.0 copy-start.1
  47.4 0.0 copy-start.2
  47.4 0.0 copy-start.3
  47.4 35.4 %all_to_all.11 = f32[2112,1,128]{2,1,0:T(1,128)S(1)} all-to-all(f32[2112,1,128]{2,1,0:T(1,128)S(1)} %bitcast.11), channel_id=1, replica_groups=mesh['tensor'=4,'context'=64] {'context'}, dimensions={0} | all-to-all | bytes 2162688 | tf_op jit(solution)/shard_map/all_to_all | solution.py:280
  82.8 0.0 copy-done
  82.8 0.0 copy-done.1
  82.8 0.0 copy-done.2
  82.8 0.0 copy-done.3
  82.8 1.2 %unpack.1 = (bf16[128,1024]{1,0:T(8,128)(2,1)}, bf16[128,1024]{1,0:T(8,128)(2,1)}, bf16[128,1024]{1,0:T(8,128)(2,1)}, bf16[128,1024]{1,0:T(8,128)(2,1)}, f32[64,128]{1,0:T(8,128)}) custom-call(f32[2112,128]{1,0:T(8,128)S(1)} %bitcast.12, bf16[128,1024]{1,0:T(8,128)(2,1)S(1)} %copy-done, bf16[128,1024]{1,0:T(8,128)(2,1)S(1)} %copy-done.1, ...), custom_call_target="tpu_custom_call" | custom-call | tf_op jit(solution)/shard_map/unpack/pallas_call | solution.py:320
Async XLA Ops:
  2.1 42.3 %copy-start.4 = (bf16[768,256]{1,0:T(8,128)(2,1)S(1)}, bf16[768,256]{1,0:T(8,128)(2,1)}, u32[]{:S(2)}) copy-start(bf16[768,256]{1,0:T(8,128)(2,1)} %constant.15.clone.refs_4_) | copy-start | bytes 1179652
  2.2 42.2 %copy-start.5 = (bf16[768,256]{1,0:T(8,128)(2,1)S(1)}, bf16[768,256]{1,0:T(8,128)(2,1)}, u32[]{:S(2)}) copy-start(bf16[768,256]{1,0:T(8,128)(2,1)} %constant.14.clone.refs_3_) | copy-start | bytes 1179652
  2.2 42.2 %copy-start.6 = (f32[2,64,128]{2,1,0:T(8,128)S(1)}, f32[2,64,128]{2,1,0:T(8,128)}, u32[]{:S(2)}) copy-start(f32[2,64,128]{2,1,0:T(8,128)} %constant.17.clone.refs_6_) | copy-start | bytes 196612
  2.2 42.2 %copy-start.7 = (f32[2,64,128]{2,1,0:T(8,128)S(1)}, f32[2,64,128]{2,1,0:T(8,128)}, u32[]{:S(2)}) copy-start(f32[2,64,128]{2,1,0:T(8,128)} %constant.16.clone.refs_5_) | copy-start | bytes 196612
  2.2 42.2 %copy-start.8 = (bf16[128,192]{1,0:T(8,128)(2,1)S(1)}, bf16[128,192]{1,0:T(8,128)(2,1)}, u32[]{:S(2)}) copy-start(bf16[128,192]{1,0:T(8,128)(2,1)} %constant.12.clone.refs_1_) | copy-start | bytes 147460
  2.2 42.2 %copy-start.9 = (bf16[64,384]{1,0:T(8,128)(2,1)S(1)}, bf16[64,384]{1,0:T(8,128)(2,1)}, u32[]{:S(2)}) copy-start(bf16[64,384]{1,0:T(8,128)(2,1)} %constant.13.clone.refs_2_) | copy-start | bytes 147460
  47.3 35.4 %copy-start = (bf16[128,1024]{1,0:T(8,128)(2,1)S(1)}, bf16[128,1024]{1,0:T(8,128)(2,1)}, u32[]{:S(2)}) copy-start(bf16[128,1024]{1,0:T(8,128)(2,1)} %refs_1_.4) | copy-start | bytes 786436
  47.4 35.4 %copy-start.1 = (bf16[128,1024]{1,0:T(8,128)(2,1)S(1)}, bf16[128,1024]{1,0:T(8,128)(2,1)}, u32[]{:S(2)}) copy-start(bf16[128,1024]{1,0:T(8,128)(2,1)} %refs_2_.4) | copy-start | bytes 786436
  47.4 35.4 %copy-start.2 = (bf16[128,1024]{1,0:T(8,128)(2,1)S(1)}, bf16[128,1024]{1,0:T(8,128)(2,1)}, u32[]{:S(2)}) copy-start(bf16[128,1024]{1,0:T(8,128)(2,1)} %refs_3_.2) | copy-start | bytes 786436
  47.4 35.4 %copy-start.3 = (bf16[128,1024]{1,0:T(8,128)(2,1)S(1)}, bf16[128,1024]{1,0:T(8,128)(2,1)}, u32[]{:S(2)}) copy-start(bf16[128,1024]{1,0:T(8,128)(2,1)} %refs_4_.4) | copy-start | bytes 786436

commit v4 on v3

--- a/solution.py
+++ b/solution.py
@@ -25,7 +25,8 @@
     b = np.arange(inner)
     odd = 2 * np.arange(blocks) + 1
     across = np.pi * np.outer(odd, a) / (2 * blocks)
-    fore = np.concatenate([np.cos(across), -np.sin(across)], axis=0)
+    order = np.concatenate([np.arange(0, blocks, 2), np.arange(1, blocks, 2)])
+    fore = np.concatenate([np.cos(across), -np.sin(across)], axis=0)[:, order]
     back = np.concatenate([np.cos(across), -np.sin(across)], axis=0).T
     fore_high, fore_low = split_table(fore)
     back_high, back_low = split_table(back)
@@ -58,15 +59,17 @@
 
 
 def pack_kernel(
-    peers,
+    hosts,
     lanes,
-    parts,
+    early,
     query_hbm,
     key_hbm,
     value_hbm,
     filter_hbm,
     grad_hbm,
-    out_ref,
+    own_ref,
+    other_ref,
+    early_ref,
     query_ref,
     key_ref,
     value_ref,
@@ -75,43 +78,63 @@
     sems,
 ):
     rows = 2 * lanes + 1
-    width = peers * lanes
-    span = width // parts
-    pairs = (
-        ((key_hbm, key_ref), (value_hbm, value_ref)),
-        ((grad_hbm, grad_ref), (query_hbm, query_ref)),
+    half = hosts * lanes
+    arrays = (
+        (key_hbm, key_ref),
+        (value_hbm, value_ref),
+        (grad_hbm, grad_ref),
+        (query_hbm, query_ref),
+        (filter_hbm, filter_ref),
     )
-    copies = {}
-    for index, pair in enumerate(pairs):
-        for part in range(parts):
-            for side, (source, target) in enumerate(pair):
-                columns = pl.ds(part * span, span)
-                copy = pltpu.make_async_copy(
-                    source.at[:, columns], target.at[:, columns], sems.at[index, side, part]
-                )
-                copy.start()
-                copies[index, side, part] = copy
-    filter_copy = pltpu.make_async_copy(filter_hbm, filter_ref, sems.at[2, 0, 0])
-    filter_copy.start()
-    for index, ((_, left), (_, right)) in enumerate(pairs):
-        for part in range(parts):
-            copies[index, 0, part].wait()
-            copies[index, 1, part].wait()
-            for start in range(part * span, (part + 1) * span, 128):
-                columns = pl.ds(start, 128)
+    copies = []
+    for index, (source, target) in enumerate(arrays):
+        copies.append(pltpu.make_async_copy(source, target, sems.at[index]))
+        copies[-1].start()
+    core = lax.rem(lax.axis_index("context"), 2)
+    for index, (left, right) in enumerate(((key_ref, value_ref), (grad_ref, query_ref))):
+        copies[2 * index].wait()
+        copies[2 * index + 1].wait()
+        for target, side in ((other_ref, 1 - core), (own_ref, core)):
+            for start in range(0, half, 128):
+                columns = pl.ds(pl.multiple_of(side * half + start, 128), 128)
                 product = left[:, columns].astype(f32) * right[:, columns].astype(f32)
                 turned = product.T
                 for offset in range(0, 128, lanes):
-                    first = (start + offset) // lanes * rows + index * lanes
-                    out_ref[pl.ds(first, lanes), :] = turned[offset : offset + lanes]
-    filter_copy.wait()
-    out_ref[pl.ds(2 * lanes, peers, stride=rows), :] = filter_ref[...]
+                    host = (start + offset) // lanes
+                    block = turned[offset : offset + lanes]
+                    target[pl.ds(host * rows + index * lanes, lanes), :] = block
+                    if target is own_ref and index == 0:
+                        early_ref[pl.ds(host * early, early), :] = block[:early]
+    copies[4].wait()
+    for target, side in ((other_ref, 1 - core), (own_ref, core)):
+        target[pl.ds(2 * lanes, hosts, stride=rows), :] = filter_ref[
+            pl.ds(pl.multiple_of(side * hosts, hosts), hosts), :
+        ]
+
+
+def join_kernel(hosts, first_ref, second_ref, out_ref):
+    rows = first_ref.shape[0] // hosts
+    more = second_ref.shape[0] // hosts
+    for host in range(hosts):
+        start = host * (rows + more)
+        out_ref[pl.ds(start, rows), :] = first_ref[pl.ds(host * rows, rows), :]
+        out_ref[pl.ds(start + rows, more), :] = second_ref[pl.ds(host * more, more), :]
+
+
+def join_late_kernel(hosts, early, own_ref, given_ref, out_ref):
+    rows = own_ref.shape[0] // hosts
+    late = rows - early
+    for host in range(hosts):
+        start = host * (rows + late)
+        out_ref[pl.ds(start, late), :] = own_ref[pl.ds(host * rows + early, late), :]
+        out_ref[pl.ds(start + late, rows), :] = given_ref[pl.ds(host * rows, rows), :]
 
 
 def convolve_kernel(
     peers,
     lanes,
-    in_ref,
+    early,
+    in_refs,
     fore_ref,
     back_ref,
     wide_fore_ref,
@@ -123,7 +146,8 @@
     low_ref,
 ):
     rows = 2 * lanes + 1
-    inner = in_ref.shape[1]
+    inner = out_ref.shape[1]
+    hosts = peers // 2
     chunk = 4
 
     def place(first, count=1):
@@ -145,6 +169,19 @@
         return jnp.concatenate(
             [real * cosine - imag * sine, real * sine + imag * cosine], axis=1
         )
+
+    def received(row):
+        if len(in_refs) == 1:
+            even = in_refs[0][pl.ds(row, hosts, stride=2 * rows), :]
+            odd = in_refs[0][pl.ds(rows + row, hosts, stride=2 * rows), :]
+        else:
+            stride = 2 * rows - early
+            even = in_refs[1][pl.ds(rows - early + row, hosts, stride=stride), :]
+            if row < early:
+                odd = in_refs[0][pl.ds(row, hosts, stride=early), :]
+            else:
+                odd = in_refs[1][pl.ds(row - early, hosts, stride=stride), :]
+        return jnp.concatenate([even, odd], axis=0)
 
     fore = fore_ref[...]
     order = [2 * lanes] + list(range(2 * lanes))
@@ -152,7 +189,7 @@
         chosen = order[start : start + 2]
         columns = []
         for row in chosen:
-            high, low = halves(in_ref[pl.ds(row, peers, stride=rows), :])
+            high, low = halves(received(row))
             columns.append(jnp.concatenate([high, low, high], axis=0))
         spread = dot(fore, jnp.concatenate(columns, axis=1))
         for index, row in enumerate(chosen):
@@ -217,10 +254,10 @@
 
 
 def unpack_kernel(
-    peers,
+    hosts,
     lanes,
-    parts,
-    in_ref,
+    own_ref,
+    given_ref,
     query_ref,
     key_ref,
     value_ref,
@@ -238,11 +275,7 @@
     sems,
 ):
     rows = 2 * lanes + 1
-    width = peers * lanes
-    span = width // parts
-    grad_filter_ref[...] = in_ref[pl.ds(2 * lanes, peers, stride=rows), :]
-    copies = [pltpu.make_async_copy(grad_filter_ref, grad_filter_hbm, sems.at[4, 0])]
-    copies[0].start()
+    half = hosts * lanes
     sides = (
         (
             (query_ref, output_ref, output_hbm),
@@ -253,52 +286,85 @@
             (key_ref, grad_value_ref, grad_value_hbm),
         ),
     )
-    for index, pair in enumerate(sides):
-        for part in range(parts):
-            for start in range(part * span, (part + 1) * span, 128):
-                columns = pl.ds(start, 128)
-                blocks = []
-                for offset in range(0, 128, lanes):
-                    first = (start + offset) // lanes * rows + index * lanes
-                    blocks.append(in_ref[pl.ds(first, lanes), :])
-                signal = jnp.concatenate(blocks, axis=0).T
-                for factor, target, _ in pair:
-                    target[:, columns] = (factor[:, columns].astype(f32) * signal).astype(bf16)
-            columns = pl.ds(part * span, span)
-            for side, (_, source, target) in enumerate(pair):
-                copy = pltpu.make_async_copy(
-                    source.at[:, columns], target.at[:, columns], sems.at[2 * index + side, part]
-                )
-                copy.start()
-                copies.append(copy)
-    for copy in copies:
-        copy.wait()
-
-
-def exchange(signal):
+
+    def finish(core):
+        mine = core * rows
+        copies = []
+        for part, source in ((core, own_ref), (1 - core, given_ref)):
+            grad_filter_ref[pl.ds(part * hosts, hosts), :] = source[
+                pl.ds(mine + 2 * lanes, hosts, stride=2 * rows), :
+            ]
+        copies.append(pltpu.make_async_copy(grad_filter_ref, grad_filter_hbm, sems.at[4, 0]))
+        copies[-1].start()
+        for index, pair in enumerate(sides):
+            for part, source in ((core, own_ref), (1 - core, given_ref)):
+                for start in range(0, half, 128):
+                    columns = pl.ds(part * half + start, 128)
+                    blocks = []
+                    for offset in range(0, 128, lanes):
+                        host = (start + offset) // lanes
+                        first = host * 2 * rows + mine + index * lanes
+                        blocks.append(source[pl.ds(first, lanes), :])
+                    signal = jnp.concatenate(blocks, axis=0).T
+                    for factor, target, _ in pair:
+                        target[:, columns] = (factor[:, columns].astype(f32) * signal).astype(
+                            bf16
+                        )
+                columns = pl.ds(part * half, half)
+                for side, (_, kept, target) in enumerate(pair):
+                    copies.append(
+                        pltpu.make_async_copy(
+                            kept.at[:, columns],
+                            target.at[:, columns],
+                            sems.at[2 * index + side, part],
+                        )
+                    )
+                    copies[-1].start()
+        for copy in copies:
+            copy.wait()
+
+    core = lax.rem(lax.axis_index("context"), 2)
+
+    @pl.when(core == 0)
+    def _():
+        finish(0)
+
+    @pl.when(core == 1)
+    def _():
+        finish(1)
+
+
+def exchange(signal, groups):
     pieces = signal.reshape(signal.shape[0], 1, signal.shape[1])
-    pieces = lax.all_to_all(pieces, "context", 0, 0, tiled=True)
+    pieces = lax.all_to_all(pieces, "context", 0, 0, axis_index_groups=groups, tiled=True)
     return pieces.reshape(signal.shape)
 
 
 def solution(mesh):
     peers = mesh.shape["context"]
+    hosts = peers // 2
+    groups = [[2 * host + core for host in range(hosts)] for core in range(2)]
+    swap = [(rank, rank ^ 1) for rank in range(peers)]
     params = pltpu.CompilerParams(vmem_limit_bytes=48 * 1024 * 1024)
+    early = 8
 
     def local(query_gate, key_gate, value_in, filter_raw, grad_out):
         inner, width = query_gate.shape
         lanes = width // filter_raw.shape[1]
         rows = 2 * lanes + 1
         scale = 1.0 / math.sqrt(peers * inner)
-        packed = jax.ShapeDtypeStruct((peers * rows, inner), f32)
         held_wide = pltpu.VMEM((inner, width), bf16)
         held_filter = pltpu.VMEM((peers, inner), f32)
-        sent = pl.pallas_call(
-            lambda *refs: pack_kernel(peers, lanes, 1, *refs),
-            out_shape=packed,
+        constants = [jnp.asarray(table) for table in tables(peers, inner, scale)]
+
+        def block_rows(count):
+            return jax.ShapeDtypeStruct((hosts * count, inner), f32)
+
+        own, other, ahead = pl.pallas_call(
+            lambda *refs: pack_kernel(hosts, lanes, early, *refs),
+            out_shape=(block_rows(rows), block_rows(rows), block_rows(early)),
             in_specs=[pl.BlockSpec(memory_space=pltpu.HBM)] * 5,
-            scratch_shapes=[held_wide] * 4
-            + [held_filter, pltpu.SemaphoreType.DMA((3, 2, 1))],
+            scratch_shapes=[held_wide] * 4 + [held_filter, pltpu.SemaphoreType.DMA((5,))],
             compiler_params=params,
             name="pack",
         )(
@@ -307,25 +373,47 @@
                 for array in (query_gate, key_gate, value_in, filter_raw.T, grad_out)
             )
         )
-        held = exchange(sent)
-        result = pl.pallas_call(
-            lambda *refs: convolve_kernel(peers, lanes, *refs),
-            out_shape=packed,
-            scratch_shapes=[pltpu.VMEM((peers * rows, 2 * inner), bf16)] * 2,
-            compiler_params=params,
-            name="convolve",
-        )(held, *(jnp.asarray(table) for table in tables(peers, inner, scale)))
-        back = exchange(result)
+
+        def convolve(*held):
+            count = len(held)
+            return pl.pallas_call(
+                lambda *refs: convolve_kernel(peers, lanes, early, refs[:count], *refs[count:]),
+                out_shape=block_rows(2 * rows),
+                scratch_shapes=[pltpu.VMEM((peers * rows, 2 * inner), bf16)] * 2,
+                compiler_params=params,
+                name="convolve",
+            )(*held, *constants)
+
+        def join(kernel, size, *parts):
+            return pl.pallas_call(
+                kernel, out_shape=block_rows(size), compiler_params=params, name="join"
+            )(*parts)
+
+        leads = lax.rem(lax.axis_index("context"), 2) == 0
+        given = lax.ppermute(other, "context", swap)
+
+        def lead(own, ahead, given):
+            sent = join(lambda *refs: join_kernel(hosts, *refs), 2 * rows, own, given)
+            return exchange(convolve(exchange(sent, groups)), groups)
+
+        def follow(own, ahead, given):
+            sent = join(
+                lambda *refs: join_late_kernel(hosts, early, *refs), 2 * rows - early, own, given
+            )
+            held_ahead = exchange(ahead, groups)
+            return exchange(convolve(held_ahead, exchange(sent, groups)), groups)
+
+        back = lax.cond(leads, lead, follow, own, ahead, given)
+        back_given = lax.ppermute(back, "context", swap)
         wide = jax.ShapeDtypeStruct((inner, width), bf16)
         *outputs, grad_filter = pl.pallas_call(
-            lambda *refs: unpack_kernel(peers, lanes, 2, *refs),
+            lambda *refs: unpack_kernel(hosts, lanes, *refs),
             out_shape=(wide,) * 4 + (jax.ShapeDtypeStruct((peers, inner), f32),),
             out_specs=(pl.BlockSpec(memory_space=pltpu.HBM),) * 5,
-            scratch_shapes=[held_wide] * 4
-            + [held_filter, pltpu.SemaphoreType.DMA((5, 2))],
+            scratch_shapes=[held_wide] * 4 + [held_filter, pltpu.SemaphoreType.DMA((5, 2))],
             compiler_params=params,
             name="unpack",
-        )(back, query_gate, key_gate, value_in, grad_out)
+        )(back, back_given, query_gate, key_gate, value_in, grad_out)
         return (*outputs, grad_filter.T)
 
     spec = P("context", "tensor")

time: 84.2 us -> 81.2 us (0.964)
  blocking collectives: 77.6 us -> 47.5 us
  waiting for transfers between devices: 0 us -> 13.5 us
  starting transfers between devices: 0 us -> 12.8 us
    all_to_all x2, blocking collectives: 77.6 us -> 47.5 us  [exchange(): lax.all_to_all(pieces, 'context', 0, 0, axis_index_groups=groups, tiled=T...]
    all_to_all x0 -> x1, starting transfers between devices: none -> 9.44 us  [exchange(): lax.all_to_all(pieces, 'context', 0, 0, axis_index_groups=groups, tiled=T...]
    all_to_all x0 -> x1, waiting for transfers between devices: none -> 9.21 us  [exchange(): lax.all_to_all(pieces, 'context', 0, 0, axis_index_groups=groups, tiled=T...]
    ppermute x0 -> x2, waiting for transfers between devices: none -> 4.26 us  [the longest x1 2.7 us: local(): back_given = lax.ppermute(back, 'context', swap)]
    ppermute x0 -> x2, starting transfers between devices: none -> 3.33 us  [the longest x1 3.33 us: local(): given = lax.ppermute(other, 'context', swap)]
    pallas_call x3 -> x4, Pallas kernels: 5.59 us -> 6.4 us  [the longest x1 2.91 us: convolve(): pl.pallas_call(lambda *refs: convolve_kernel(peers, lanes, early, refs[:c...]
  transfers between devices with their start and end apart: 0 -> 3, of which waited for: 0 -> 3; matrix products, arithmetic and copies ran while one was open for 0% -> 0% of each run, Pallas kernels for 0% -> 0%
where the time goes in v4:
time: 81.2 us; the launch traced here: 81 us
  blocking collectives  47.5 us (58%)
  waiting for transfers between devices  13.5 us (17%)
  starting transfers between devices  12.8 us (16%)
  Pallas kernels  6.4 us (8%)
    all_to_all x2, blocking collectives, exchange(): lax.all_to_all(pieces, 'context', 0, 0, axis_index_groups=groups, tiled=T...  47.5 us
    all_to_all x1, starting transfers between devices, exchange(): lax.all_to_all(pieces, 'context', 0, 0, axis_index_groups=groups, tiled=T...  9.44 us
    all_to_all x1, waiting for transfers between devices, exchange(): lax.all_to_all(pieces, 'context', 0, 0, axis_index_groups=groups, tiled=T...  9.21 us
    ppermute x1, starting transfers between devices, local(): given = lax.ppermute(other, 'context', swap)  3.33 us
    pallas_call x1, Pallas kernels, convolve(): pl.pallas_call(lambda *refs: convolve_kernel(peers, lanes, early, refs[:c...  2.91 us
    ppermute x1, waiting for transfers between devices, local(): back_given = lax.ppermute(back, 'context', swap)  2.7 us
    pallas_call x1, Pallas kernels, local(): pl.pallas_call(lambda *refs: pack_kernel(hosts, lanes, early, *refs), out...  2.21 us
  transfers between devices with their start and end apart: 3, of which 3 were waited for; matrix products, arithmetic and copies ran while one was open for 0% of the time, Pallas kernels for 0%

profile of v4, /device:TPU:1, one launch (start us, length us, event | category | flops | bytes accessed | tf_op | source)
XLA Modules:
  0.0 81.0 jit_solution(11540656356605133202)
XLA Ops:
  0.6 0.0 copy-start.8
  0.6 0.0 copy-start.9
  0.7 0.0 copy-start.11
  0.7 0.0 copy-start.10
  0.7 2.2 %pack.1 = (f32[1056,128]{1,0:T(8,128)S(1)}, f32[1056,128]{1,0:T(8,128)S(1)}, f32[256,128]{1,0:T(8,128)}) custom-call(bf16[128,1024]{1,0:T(8,128)(2,1)} %refs_2_.3, bf16[128,1024]{1,0:T(8,128)(2,1)} %refs_3_.1, bf16[128,1024]{1,0:T(8,128)(2,1)} %refs_4_.3, f32[64,128]{1,0:T(8,128)} %bitcast.29, bf16[128,1024]{1,0:T(8,128)(2,1)} %refs_5_.1), custom_call_target="tpu_custom_call" | custom-call | tf_op jit(solution)/shard_map/pack/pallas_call | solution.py:363
  2.9 3.3 %collective-permute-start = (f32[1056,128]{1,0:T(8,128)S(1)}, f32[1056,128]{1,0:T(8,128)S(1)}, u32[]{:S(2)}, u32[]{:S(2)}) collective-permute-start(f32[1056,128]{1,0:T(8,128)S(1)} %get-tuple-element.71), channel_id=1, source_target_pairs={{0,1},{1,0},{2,3},{3,2},{4,5},{5,4},{6,7},{7,6},{8,9},{9,8},{10,11... | collective-permute-start | bytes 1622024 | tf_op jit(solution)/shard_map/ppermute | solution.py:393
  6.2 1.6 %collective-permute-done = f32[1056,128]{1,0:T(8,128)S(1)} collective-permute-done((f32[1056,128]{1,0:T(8,128)S(1)}, f32[1056,128]{1,0:T(8,128)S(1)}, u32[]{:S(2)}, u32[]{:S(2)}) %collective-permute-start) | collective-permute-done | bytes 540704 | tf_op jit(solution)/shard_map/ppermute | solution.py:393
  7.8 0.0 copy-done.8
  7.8 0.0 copy-done.9
  7.8 0.0 copy-done.11
  7.8 0.0 copy-done.10
  7.8 0.0 copy-start
  7.8 0.0 copy-start.1
  7.8 0.0 copy-start.2
  7.8 0.0 copy-start.3
  7.8 69.2 %conditional.1 = (f32[2112,128]{1,0:T(8,128)S(1)}) conditional(s32[]{:T(128)} %convert_element_type.3, (f32[256,128]{1,0:T(8,128)}, f32[1056,128]{1,0:T(8,128)S(1)}, f32[1056,128]{1,0:T(8,128)S(1)}, bf16[128,192]{1,0:T(8,128)(2,1)S(1)}, bf16[64,384]{1,0:T(8,128)(2,1)S(1)}, /*index=5*/bf16[768,256]{1,0:T(8,128)(2,1)}, bf16[768,256]{1,0:T(8,128)(2,1)}, ...), branch_computations={%region_0.0_spmd, %region_1.0_spmd} | conditional | bytes 7602272 | solution.py:406
  7.9 9.4 %all-to-all-start = ((f32[256,1,128]{2,1,0:T(1,128)}), f32[256,1,128]{2,1,0:T(1,128)S(1)}, u32[]{:S(2)}, u32[]{:S(2)}) async-start(f32[256,1,128]{2,1,0:T(1,128)} %bitcast), calls=%async_computation | async-start | bytes 262144 | tf_op jit(solution)/shard_map/cond/branch_0_fun/all_to_all | solution.py:339
  17.3 0.1 join.2
  17.4 0.0 copy-start.4
  17.4 0.0 copy-start.6
  17.4 9.2 %all-to-all-done = f32[256,1,128]{2,1,0:T(1,128)S(1)} async-done(((f32[256,1,128]{2,1,0:T(1,128)}), f32[256,1,128]{2,1,0:T(1,128)S(1)}, u32[]{:S(2)}, u32[]{:S(2)}) %all-to-all-start) | async-done | bytes 131104 | tf_op jit(solution)/shard_map/cond/branch_0_fun/all_to_all | solution.py:339
  26.6 20.8 %all_to_all.20 = f32[1856,1,128]{2,1,0:T(1,128)S(1)} all-to-all(f32[1856,1,128]{2,1,0:T(1,128)S(1)} %bitcast.25), channel_id=1, replica_groups={{0,2,4,6,8,10,12,14,16,18,20,22,24,26,28,30,32,34,36,38,40,42,44,46,48,..., dimensions={0} | all-to-all | bytes 1900544 | tf_op jit(solution)/shard_map/cond/branch_0_fun/all_to_all | solution.py:339
  47.4 0.0 copy-done.4
  47.4 0.0 copy-done.6
  47.4 2.9 %convolve.2 = f32[2112,128]{1,0:T(8,128)S(1)} custom-call(f32[256,128]{1,0:T(8,128)S(1)} %bitcast.26, f32[1856,128]{1,0:T(8,128)S(1)} %bitcast.24, bf16[128,192]{1,0:T(8,128)(2,1)S(1)} %get-tuple-element.42.refs_2_, bf16[64,384]{1,0:T(8,128)(2,1)S(1)} %get-tuple-element.43.refs_3_, bf16[768,256]{1,0:T(8,128)(2,1)S(1)} %copy-done.6, ...), custom_call_target="tpu_custom_call" | custom-call | tf_op jit(solution)/shard_map/cond/branch_0_fun/convolve/pallas_call | solution.py:379
  50.4 26.7 %all_to_all.21 = f32[2112,1,128]{2,1,0:T(1,128)S(1)} all-to-all(f32[2112,1,128]{2,1,0:T(1,128)S(1)} %bitcast.20), channel_id=1, replica_groups={{0,2,4,6,8,10,12,14,16,18,20,22,24,26,28,30,32,34,36,38,40,42,44,46,48,..., dimensions={0} | all-to-all | bytes 2162688 | tf_op jit(solution)/shard_map/cond/branch_0_fun/all_to_all | solution.py:339
  77.0 0.0 collective-permute-start.1
  77.0 2.7 %collective-permute-done.1.refs_1_ = f32[2112,128]{1,0:T(8,128)S(1)} collective-permute-done((f32[2112,128]{1,0:T(8,128)S(1)}, f32[2112,128]{1,0:T(8,128)S(1)}, u32[]{:S(2)}, u32[]{:S(2)}) %collective-permute-start.1) | collective-permute-done | bytes 1081376 | tf_op jit(solution)/shard_map/ppermute | solution.py:407
  79.7 0.0 copy-done
  79.7 0.0 copy-done.1
  79.7 0.0 copy-done.2
  79.8 0.0 copy-done.3
  79.8 1.2 %unpack.1 = (bf16[128,1024]{1,0:T(8,128)(2,1)}, bf16[128,1024]{1,0:T(8,128)(2,1)}, bf16[128,1024]{1,0:T(8,128)(2,1)}, bf16[128,1024]{1,0:T(8,128)(2,1)}, f32[64,128]{1,0:T(8,128)}) custom-call(f32[2112,128]{1,0:T(8,128)S(1)} %get-tuple-element.77.refs_0_, f32[2112,128]{1,0:T(8,128)S(1)} %collective-permute-done.1.refs_1_, bf16[128,1024]{1,0:T(8,128)(2,1)S(1)} %copy-done, ...), custom_call_target="tpu_custom_call" | custom-call | tf_op jit(solution)/shard_map/unpack/pallas_call | solution.py:409
Async XLA Ops:
  0.6 7.2 %copy-start.8 = (f32[2,64,128]{2,1,0:T(8,128)S(1)}, f32[2,64,128]{2,1,0:T(8,128)}, u32[]{:S(2)}) copy-start(f32[2,64,128]{2,1,0:T(8,128)} %constant.27.clone) | copy-start | bytes 196612
  0.6 7.2 %copy-start.9 = (f32[2,64,128]{2,1,0:T(8,128)S(1)}, f32[2,64,128]{2,1,0:T(8,128)}, u32[]{:S(2)}) copy-start(f32[2,64,128]{2,1,0:T(8,128)} %constant.26.clone) | copy-start | bytes 196612
  0.7 7.1 %copy-start.11 = (bf16[64,384]{1,0:T(8,128)(2,1)S(1)}, bf16[64,384]{1,0:T(8,128)(2,1)}, u32[]{:S(2)}) copy-start(bf16[64,384]{1,0:T(8,128)(2,1)} %constant.23.clone) | copy-start | bytes 147460
  0.7 7.1 %copy-start.10 = (bf16[128,192]{1,0:T(8,128)(2,1)S(1)}, bf16[128,192]{1,0:T(8,128)(2,1)}, u32[]{:S(2)}) copy-start(bf16[128,192]{1,0:T(8,128)(2,1)} %constant.22.clone) | copy-start | bytes 147460
  2.9 4.9 %collective-permute-start = (f32[1056,128]{1,0:T(8,128)S(1)}, f32[1056,128]{1,0:T(8,128)S(1)}, u32[]{:S(2)}, u32[]{:S(2)}) collective-permute-start(f32[1056,128]{1,0:T(8,128)S(1)} %get-tuple-element.71), channel_id=1, source_target_pairs={{0,1},{1,0},{2,3},{3,2},{4,5},{5,4},{6,7},{7,6},{8,9},{9,8},{10,11... | collective-permute-start | bytes 1622024 | tf_op jit(solution)/shard_map/ppermute | solution.py:393
  7.8 71.9 %copy-start = (bf16[128,1024]{1,0:T(8,128)(2,1)S(1)}, bf16[128,1024]{1,0:T(8,128)(2,1)}, u32[]{:S(2)}) copy-start(bf16[128,1024]{1,0:T(8,128)(2,1)} %refs_2_.3) | copy-start | bytes 786436
  7.8 71.9 %copy-start.1 = (bf16[128,1024]{1,0:T(8,128)(2,1)S(1)}, bf16[128,1024]{1,0:T(8,128)(2,1)}, u32[]{:S(2)}) copy-start(bf16[128,1024]{1,0:T(8,128)(2,1)} %refs_3_.1) | copy-start | bytes 786436
  7.8 71.9 %copy-start.2 = (bf16[128,1024]{1,0:T(8,128)(2,1)S(1)}, bf16[128,1024]{1,0:T(8,128)(2,1)}, u32[]{:S(2)}) copy-start(bf16[128,1024]{1,0:T(8,128)(2,1)} %refs_4_.3) | copy-start | bytes 786436
  7.8 71.9 %copy-start.3 = (bf16[128,1024]{1,0:T(8,128)(2,1)S(1)}, bf16[128,1024]{1,0:T(8,128)(2,1)}, u32[]{:S(2)}) copy-start(bf16[128,1024]{1,0:T(8,128)(2,1)} %refs_5_.1) | copy-start | bytes 786436
  7.9 18.8 %all-to-all-start = ((f32[256,1,128]{2,1,0:T(1,128)}), f32[256,1,128]{2,1,0:T(1,128)S(1)}, u32[]{:S(2)}, u32[]{:S(2)}) async-start(f32[256,1,128]{2,1,0:T(1,128)} %bitcast), calls=%async_computation | async-start | bytes 262144 | tf_op jit(solution)/shard_map/cond/branch_0_fun/all_to_all | solution.py:339
  17.4 30.0 %copy-start.4 = (bf16[768,256]{1,0:T(8,128)(2,1)S(1)}, bf16[768,256]{1,0:T(8,128)(2,1)}, u32[]{:S(2)}) copy-start(bf16[768,256]{1,0:T(8,128)(2,1)} %get-tuple-element.45.refs_5_) | copy-start | bytes 1179652 | tf_op jit(solution)/shard_map/cond
  17.4 30.0 %copy-start.6 = (bf16[768,256]{1,0:T(8,128)(2,1)S(1)}, bf16[768,256]{1,0:T(8,128)(2,1)}, u32[]{:S(2)}) copy-start(bf16[768,256]{1,0:T(8,128)(2,1)} %get-tuple-element.44.refs_4_) | copy-start | bytes 1179652 | tf_op jit(solution)/shard_map/cond
  77.0 2.7 %collective-permute-start.1 = (f32[2112,128]{1,0:T(8,128)S(1)}, f32[2112,128]{1,0:T(8,128)S(1)}, u32[]{:S(2)}, u32[]{:S(2)}) collective-permute-start(f32[2112,128]{1,0:T(8,128)S(1)} %get-tuple-element.77.refs_0_), channel_id=1, source_target_pairs={{0,1},{1,0},{2,3},{3,2},{4,5},{5,4},{6,7},{7,6},{8,9},{9,8},{10,11... | collective-permute-start | bytes 3244040 | tf_op jit(solution)/shard_map/ppermute | solution.py:407

commit v5 on v4

--- a/solution.py
+++ b/solution.py
@@ -58,58 +58,53 @@
     return jnp.dot(left, right, preferred_element_type=f32)
 
 
-def pack_kernel(
-    hosts,
-    lanes,
-    early,
-    query_hbm,
-    key_hbm,
-    value_hbm,
-    filter_hbm,
-    grad_hbm,
-    own_ref,
-    other_ref,
-    early_ref,
-    query_ref,
-    key_ref,
-    value_ref,
-    grad_ref,
-    filter_ref,
-    sems,
-):
+def pack_kernel(hosts, lanes, other, *refs):
+    sources, out_ref, targets, sems = refs[:5], refs[5], refs[6:11], refs[11]
     rows = 2 * lanes + 1
     half = hosts * lanes
-    arrays = (
-        (key_hbm, key_ref),
-        (value_hbm, value_ref),
-        (grad_hbm, grad_ref),
-        (query_hbm, query_ref),
-        (filter_hbm, filter_ref),
-    )
+    core = lax.rem(lax.axis_index("context"), 2)
+    part = 1 - core if other else core
+    columns = pl.ds(pl.multiple_of(part * half, half), half)
     copies = []
-    for index, (source, target) in enumerate(arrays):
-        copies.append(pltpu.make_async_copy(source, target, sems.at[index]))
-        copies[-1].start()
-    core = lax.rem(lax.axis_index("context"), 2)
-    for index, (left, right) in enumerate(((key_ref, value_ref), (grad_ref, query_ref))):
+    for index in range(4):
+        source = sources[index].at[:, columns]
+        copies.append(pltpu.make_async_copy(source, targets[index], sems.at[index]))
+    source = sources[4].at[pl.ds(pl.multiple_of(part * hosts, hosts), hosts), :]
+    copies.append(pltpu.make_async_copy(source, targets[4], sems.at[4]))
+    for copy in copies:
+        copy.start()
+    for index in range(2):
         copies[2 * index].wait()
         copies[2 * index + 1].wait()
-        for target, side in ((other_ref, 1 - core), (own_ref, core)):
-            for start in range(0, half, 128):
-                columns = pl.ds(pl.multiple_of(side * half + start, 128), 128)
-                product = left[:, columns].astype(f32) * right[:, columns].astype(f32)
-                turned = product.T
-                for offset in range(0, 128, lanes):
-                    host = (start + offset) // lanes
-                    block = turned[offset : offset + lanes]
-                    target[pl.ds(host * rows + index * lanes, lanes), :] = block
-                    if target is own_ref and index == 0:
-                        early_ref[pl.ds(host * early, early), :] = block[:early]
+        left, right = targets[2 * index], targets[2 * index + 1]
+        for start in range(0, half, 128):
+            place = pl.ds(start, 128)
+            product = left[:, place].astype(f32) * right[:, place].astype(f32)
+            turned = product.T
+            for offset in range(0, 128, lanes):
+                first = (start + offset) // lanes * rows + index * lanes
+                out_ref[pl.ds(first, lanes), :] = turned[offset : offset + lanes]
     copies[4].wait()
-    for target, side in ((other_ref, 1 - core), (own_ref, core)):
-        target[pl.ds(2 * lanes, hosts, stride=rows), :] = filter_ref[
-            pl.ds(pl.multiple_of(side * hosts, hosts), hosts), :
-        ]
+    out_ref[pl.ds(2 * lanes, hosts, stride=rows), :] = targets[4][...]
+
+
+def take_kernel(hosts, first, own_ref, out_ref):
+    rows = own_ref.shape[0] // hosts
+    count = out_ref.shape[0] // hosts
+    for host in range(hosts):
+        out_ref[pl.ds(host * count, count), :] = own_ref[pl.ds(host * rows + first, count), :]
+
+
+def take_other_kernel(hosts, back_ref, out_ref):
+    core = lax.rem(lax.axis_index("context"), 2)
+
+    @pl.when(core == 0)
+    def _():
+        take_kernel(hosts, out_ref.shape[0] // hosts, back_ref, out_ref)
+
+    @pl.when(core == 1)
+    def _():
+        take_kernel(hosts, 0, back_ref, out_ref)
 
 
 def join_kernel(hosts, first_ref, second_ref, out_ref):
@@ -253,85 +248,65 @@
             ]
 
 
-def unpack_kernel(
-    hosts,
-    lanes,
-    own_ref,
-    given_ref,
-    query_ref,
-    key_ref,
-    value_ref,
-    grad_ref,
-    output_hbm,
-    grad_query_hbm,
-    grad_key_hbm,
-    grad_value_hbm,
-    grad_filter_hbm,
-    output_ref,
-    grad_query_ref,
-    grad_key_ref,
-    grad_value_ref,
-    grad_filter_ref,
-    sems,
-):
+def unpack_kernel(hosts, lanes, given, *refs):
+    if given:
+        in_ref, *refs = refs
+        refs = refs[:4] + refs[9:]
+    else:
+        in_ref, *refs = refs
+    query_ref, key_ref, value_ref, grad_ref, *refs = refs
+    targets, kept, filter_ref, sems = refs[:5], refs[5:9], refs[9], refs[10]
     rows = 2 * lanes + 1
     half = hosts * lanes
-    sides = (
-        (
-            (query_ref, output_ref, output_hbm),
-            (grad_ref, grad_query_ref, grad_query_hbm),
-        ),
-        (
-            (value_ref, grad_key_ref, grad_key_hbm),
-            (key_ref, grad_value_ref, grad_value_hbm),
-        ),
-    )
-
-    def finish(core):
-        mine = core * rows
-        copies = []
-        for part, source in ((core, own_ref), (1 - core, given_ref)):
-            grad_filter_ref[pl.ds(part * hosts, hosts), :] = source[
-                pl.ds(mine + 2 * lanes, hosts, stride=2 * rows), :
-            ]
-        copies.append(pltpu.make_async_copy(grad_filter_ref, grad_filter_hbm, sems.at[4, 0]))
-        copies[-1].start()
-        for index, pair in enumerate(sides):
-            for part, source in ((core, own_ref), (1 - core, given_ref)):
-                for start in range(0, half, 128):
-                    columns = pl.ds(part * half + start, 128)
-                    blocks = []
-                    for offset in range(0, 128, lanes):
-                        host = (start + offset) // lanes
-                        first = host * 2 * rows + mine + index * lanes
-                        blocks.append(source[pl.ds(first, lanes), :])
-                    signal = jnp.concatenate(blocks, axis=0).T
-                    for factor, target, _ in pair:
-                        target[:, columns] = (factor[:, columns].astype(f32) * signal).astype(
-                            bf16
-                        )
-                columns = pl.ds(part * half, half)
-                for side, (_, kept, target) in enumerate(pair):
-                    copies.append(
-                        pltpu.make_async_copy(
-                            kept.at[:, columns],
-                            target.at[:, columns],
-                            sems.at[2 * index + side, part],
-                        )
+    pairs = ((query_ref, grad_ref), (value_ref, key_ref))
+    core = lax.rem(lax.axis_index("context"), 2)
+    part = 1 - core if given else core
+    place = pl.ds(pl.multiple_of(part * half, half), half)
+
+    def finish(first, stride):
+        filter_ref[...] = in_ref[pl.ds(first + 2 * lanes, hosts, stride=stride), :]
+        copies = [
+            pltpu.make_async_copy(
+                filter_ref,
+                targets[4].at[pl.ds(pl.multiple_of(part * hosts, hosts), hosts), :],
+                sems.at[4],
+            )
+        ]
+        copies[0].start()
+        for index, pair in enumerate(pairs):
+            for start in range(0, half, 128):
+                blocks = []
+                for offset in range(0, 128, lanes):
+                    row = (start + offset) // lanes * stride + first + index * lanes
+                    blocks.append(in_ref[pl.ds(row, lanes), :])
+                signal = jnp.concatenate(blocks, axis=0).T
+                columns = pl.ds(pl.multiple_of(part * half + start, 128), 128)
+                for side, factor in enumerate(pair):
+                    kept[2 * index + side][:, pl.ds(start, 128)] = (
+                        factor[:, columns].astype(f32) * signal
+                    ).astype(bf16)
+            for side in range(2):
+                number = 2 * index + side
+                copies.append(
+                    pltpu.make_async_copy(
+                        kept[number], targets[number].at[:, place], sems.at[number]
                     )
-                    copies[-1].start()
+                )
+                copies[-1].start()
         for copy in copies:
             copy.wait()
 
-    core = lax.rem(lax.axis_index("context"), 2)
+    if given:
+        finish(0, rows)
+        return
 
     @pl.when(core == 0)
     def _():
-        finish(0)
+        finish(0, 2 * rows)
 
     @pl.when(core == 1)
     def _():
-        finish(1)
+        finish(rows, 2 * rows)
 
 
 def exchange(signal, groups):
@@ -346,33 +321,40 @@
     groups = [[2 * host + core for host in range(hosts)] for core in range(2)]
     swap = [(rank, rank ^ 1) for rank in range(peers)]
     params = pltpu.CompilerParams(vmem_limit_bytes=48 * 1024 * 1024)
-    early = 8
+    early = 4
 
     def local(query_gate, key_gate, value_in, filter_raw, grad_out):
         inner, width = query_gate.shape
         lanes = width // filter_raw.shape[1]
         rows = 2 * lanes + 1
         scale = 1.0 / math.sqrt(peers * inner)
-        held_wide = pltpu.VMEM((inner, width), bf16)
-        held_filter = pltpu.VMEM((peers, inner), f32)
         constants = [jnp.asarray(table) for table in tables(peers, inner, scale)]
 
         def block_rows(count):
             return jax.ShapeDtypeStruct((hosts * count, inner), f32)
 
-        own, other, ahead = pl.pallas_call(
-            lambda *refs: pack_kernel(hosts, lanes, early, *refs),
-            out_shape=(block_rows(rows), block_rows(rows), block_rows(early)),
-            in_specs=[pl.BlockSpec(memory_space=pltpu.HBM)] * 5,
-            scratch_shapes=[held_wide] * 4 + [held_filter, pltpu.SemaphoreType.DMA((5,))],
-            compiler_params=params,
-            name="pack",
-        )(
-            *(
-                pltpu.with_memory_space_constraint(array, pltpu.HBM)
-                for array in (query_gate, key_gate, value_in, filter_raw.T, grad_out)
-            )
-        )
+        held_half = pltpu.VMEM((inner, width // 2), bf16)
+        half_scratch = [held_half] * 4 + [
+            pltpu.VMEM((hosts, inner), f32),
+            pltpu.SemaphoreType.DMA((5,)),
+        ]
+        sources = [
+            pltpu.with_memory_space_constraint(array, pltpu.HBM)
+            for array in (key_gate, value_in, grad_out, query_gate, filter_raw.T)
+        ]
+
+        def pack(other):
+            return pl.pallas_call(
+                lambda *refs: pack_kernel(hosts, lanes, other, *refs),
+                out_shape=block_rows(rows),
+                in_specs=[pl.BlockSpec(memory_space=pltpu.HBM)] * 5,
+                scratch_shapes=half_scratch,
+                compiler_params=params,
+                name="pack",
+            )(*sources)
+
+        given = lax.ppermute(pack(True), "context", swap)
+        own = pack(False)
 
         def convolve(*held):
             count = len(held)
@@ -390,30 +372,40 @@
             )(*parts)
 
         leads = lax.rem(lax.axis_index("context"), 2) == 0
-        given = lax.ppermute(other, "context", swap)
-
-        def lead(own, ahead, given):
+        def lead(own, given):
             sent = join(lambda *refs: join_kernel(hosts, *refs), 2 * rows, own, given)
             return exchange(convolve(exchange(sent, groups)), groups)
 
-        def follow(own, ahead, given):
+        def follow(own, given):
+            ahead = join(lambda *refs: take_kernel(hosts, 0, *refs), early, own)
             sent = join(
                 lambda *refs: join_late_kernel(hosts, early, *refs), 2 * rows - early, own, given
             )
             held_ahead = exchange(ahead, groups)
             return exchange(convolve(held_ahead, exchange(sent, groups)), groups)
 
-        back = lax.cond(leads, lead, follow, own, ahead, given)
-        back_given = lax.ppermute(back, "context", swap)
+        back = lax.cond(leads, lead, follow, own, given)
+        other_back = join(lambda *refs: take_other_kernel(hosts, *refs), rows, back)
+        back_given = lax.ppermute(other_back, "context", swap)
+        factors = (query_gate, key_gate, value_in, grad_out)
         wide = jax.ShapeDtypeStruct((inner, width), bf16)
-        *outputs, grad_filter = pl.pallas_call(
-            lambda *refs: unpack_kernel(hosts, lanes, *refs),
-            out_shape=(wide,) * 4 + (jax.ShapeDtypeStruct((peers, inner), f32),),
-            out_specs=(pl.BlockSpec(memory_space=pltpu.HBM),) * 5,
-            scratch_shapes=[held_wide] * 4 + [held_filter, pltpu.SemaphoreType.DMA((5, 2))],
-            compiler_params=params,
-            name="unpack",
-        )(back, back_given, query_gate, key_gate, value_in, grad_out)
+        shapes = (wide,) * 4 + (jax.ShapeDtypeStruct((peers, inner), f32),)
+        hbm = pl.BlockSpec(memory_space=pltpu.HBM)
+        vmem = pl.BlockSpec(memory_space=pltpu.VMEM)
+
+        def unpack(given, signal, *partial):
+            return pl.pallas_call(
+                lambda *refs: unpack_kernel(hosts, lanes, given, *refs),
+                out_shape=shapes,
+                in_specs=[vmem] * 5 + [hbm] * len(partial),
+                out_specs=(hbm,) * 5,
+                scratch_shapes=half_scratch,
+                input_output_aliases={5 + index: index for index in range(len(partial))},
+                compiler_params=params,
+                name="unpack",
+            )(signal, *factors, *partial)
+
+        *outputs, grad_filter = unpack(True, back_given, *unpack(False, back))
         return (*outputs, grad_filter.T)
 
     spec = P("context", "tensor")

time: 81.2 us -> 79.4 us (0.978)
  waiting for transfers between devices: 13.5 us -> 9.16 us
  Pallas kernels: 6.4 us -> 8.24 us
  local copies, waits for them, and re-layouts: 0.07 us -> 1.05 us
    ppermute x2, waiting for transfers between devices: 4.26 us -> 0.26 us  [the longest x1 0.26 us: local(): given = lax.ppermute(pack(True), 'context', swap)]
    pallas_call x2 -> x4, Pallas kernels: 3.41 us -> 4.55 us  [the longest x2 2.59 us: pack(): pl.pallas_call(lambda *refs: pack_kernel(hosts, lanes, other, *refs), out...]
    unnamed x16 -> x20, local copies, waits for them, and re-layouts: 0.05 us -> 1.05 us
  transfers between devices with their start and end apart: 3 -> 3, of which waited for: 3 -> 2; matrix products, arithmetic and copies ran while one was open for 0% -> 0% of each run, Pallas kernels for 0% -> 3%
where the time goes in v5:
time: 79.4 us; the launch traced here: 79.1 us
  blocking collectives  47.1 us (59%)
  starting transfers between devices  12.7 us (16%)
  waiting for transfers between devices  9.16 us (12%)
  Pallas kernels  8.24 us (10%)
  local copies, waits for them, and re-layouts  1.05 us (1%)
    all_to_all x2, blocking collectives, exchange(): lax.all_to_all(pieces, 'context', 0, 0, axis_index_groups=groups, tiled=T...  47.1 us
    all_to_all x1, starting transfers between devices, exchange(): lax.all_to_all(pieces, 'context', 0, 0, axis_index_groups=groups, tiled=T...  9.3 us
    all_to_all x1, waiting for transfers between devices, exchange(): lax.all_to_all(pieces, 'context', 0, 0, axis_index_groups=groups, tiled=T...  8.9 us
    ppermute x1, starting transfers between devices, local(): given = lax.ppermute(pack(True), 'context', swap)  3.33 us
    pallas_call x1, Pallas kernels, convolve(): pl.pallas_call(lambda *refs: convolve_kernel(peers, lanes, early, refs[:c...  2.91 us
    pallas_call x2, Pallas kernels, pack(): pl.pallas_call(lambda *refs: pack_kernel(hosts, lanes, other, *refs), out...  2.59 us
    pallas_call x2, Pallas kernels, unpack(): pl.pallas_call(lambda *refs: unpack_kernel(hosts, lanes, given, *refs), o...  1.96 us
  transfers between devices with their start and end apart: 3, of which 2 were waited for; matrix products, arithmetic and copies ran while one was open for 0% of the time, Pallas kernels for 3%

profile of v5, /device:TPU:1, one launch (start us, length us, event | category | flops | bytes accessed | tf_op | source)
XLA Modules:
  0.0 79.1 jit_solution(2562443395010530764)
XLA Ops:
  0.6 1.3 %pack.3 = f32[1056,128]{1,0:T(8,128)S(1)} custom-call(bf16[128,1024]{1,0:T(8,128)(2,1)} %refs_2_.7, bf16[128,1024]{1,0:T(8,128)(2,1)} %refs_3_.7, bf16[128,1024]{1,0:T(8,128)(2,1)} %refs_4_.3, bf16[128,1024]{1,0:T(8,128)(2,1)} %refs_1_.7, f32[64,128]{1,0:T(8,128)} %bitcast.31), custom_call_target="tpu_custom_call" | custom-call | tf_op jit(solution)/shard_map/pack/pallas_call | solution.py:347
  1.9 0.0 copy-start.4
  2.0 0.0 copy-start.5
  2.0 0.0 copy-start.6
  2.0 0.0 copy-start.7
  2.0 0.0 copy-start.8
  2.0 0.0 copy-start.9
  2.0 3.3 %collective-permute-start = (f32[1056,128]{1,0:T(8,128)S(1)}, f32[1056,128]{1,0:T(8,128)S(1)}, u32[]{:S(2)}, u32[]{:S(2)}) collective-permute-start(f32[1056,128]{1,0:T(8,128)S(1)} %pack.3), channel_id=1, source_target_pairs={{0,1},{1,0},{2,3},{3,2},{4,5},{5,4},{6,7},{7,6},{8,9},{9,8},{10,11... | collective-permute-start | bytes 1622024 | tf_op jit(solution)/shard_map/ppermute | solution.py:356
  5.3 1.3 %pack.2 = f32[1056,128]{1,0:T(8,128)S(1)} custom-call(bf16[128,1024]{1,0:T(8,128)(2,1)} %refs_2_.7, bf16[128,1024]{1,0:T(8,128)(2,1)} %refs_3_.7, bf16[128,1024]{1,0:T(8,128)(2,1)} %refs_4_.3, bf16[128,1024]{1,0:T(8,128)(2,1)} %refs_1_.7, f32[64,128]{1,0:T(8,128)} %bitcast.32), custom_call_target="tpu_custom_call" | custom-call | tf_op jit(solution)/shard_map/pack/pallas_call | solution.py:347
  6.6 0.3 collective-permute-done
  6.9 0.0 copy-done.4
  6.9 0.0 copy-done.5
  6.9 0.0 copy-done.6
  6.9 0.0 copy-done.7
  6.9 0.0 copy-done.8
  6.9 0.0 copy-done.9
  6.9 69.0 %conditional.1 = (f32[2112,128]{1,0:T(8,128)S(1)}) conditional(s32[]{:T(128)} %convert_element_type.3, (f32[1056,128]{1,0:T(8,128)S(1)}, f32[1056,128]{1,0:T(8,128)S(1)}, bf16[128,192]{1,0:T(8,128)(2,1)S(1)}, bf16[64,384]{1,0:T(8,128)(2,1)S(1)}, bf16[768,256]{1,0:T(8,128)(2,1)S(1)}, /*index=5*/bf16[768,256]{1,0:T(8,128)(2,1)S(1)}, ...), branch_computations={%region_0.0_spmd, %region_1.0_spmd} | conditional | bytes 4390952 | solution.py:387
  6.9 0.6 join.4
  7.6 9.3 %all-to-all-start = ((f32[128,1,128]{2,1,0:T(1,128)}), f32[128,1,128]{2,1,0:T(1,128)S(1)}, u32[]{:S(2)}, u32[]{:S(2)}) async-start(f32[128,1,128]{2,1,0:T(1,128)} %bitcast.1), calls=%async_computation | async-start | bytes 131072 | tf_op jit(solution)/shard_map/cond/branch_0_fun/all_to_all | solution.py:314
  16.9 0.1 join.5
  17.0 8.9 %all-to-all-done = f32[128,1,128]{2,1,0:T(1,128)S(1)} async-done(((f32[128,1,128]{2,1,0:T(1,128)}), f32[128,1,128]{2,1,0:T(1,128)S(1)}, u32[]{:S(2)}, u32[]{:S(2)}) %all-to-all-start) | async-done | bytes 65568 | tf_op jit(solution)/shard_map/cond/branch_0_fun/all_to_all | solution.py:314
  25.9 21.2 %all_to_all.20 = f32[1984,1,128]{2,1,0:T(1,128)S(1)} all-to-all(f32[1984,1,128]{2,1,0:T(1,128)S(1)} %bitcast.27), channel_id=1, replica_groups={{0,2,4,6,8,10,12,14,16,18,20,22,24,26,28,30,32,34,36,38,40,42,44,46,48,..., dimensions={0} | all-to-all | bytes 2031616 | tf_op jit(solution)/shard_map/cond/branch_0_fun/all_to_all | solution.py:314
  47.1 2.9 %convolve.2 = f32[2112,128]{1,0:T(8,128)S(1)} custom-call(f32[128,128]{1,0:T(8,128)S(1)} %bitcast.28, f32[1984,128]{1,0:T(8,128)S(1)} %bitcast.26, bf16[128,192]{1,0:T(8,128)(2,1)S(1)} %get-tuple-element.39.refs_2_, bf16[64,384]{1,0:T(8,128)(2,1)S(1)} %get-tuple-element.40.refs_3_, bf16[768,256]{1,0:T(8,128)(2,1)S(1)} %get-tuple-element.41.refs_4_, ...), custom_call_target="tpu_custom_call" | custom-call | tf_op jit(solution)/shard_map/cond/branch_0_fun/convolve/pallas_call | solution.py:361
  50.0 26.0 %all_to_all.21 = f32[2112,1,128]{2,1,0:T(1,128)S(1)} all-to-all(f32[2112,1,128]{2,1,0:T(1,128)S(1)} %bitcast.22), channel_id=1, replica_groups={{0,2,4,6,8,10,12,14,16,18,20,22,24,26,28,30,32,34,36,38,40,42,44,46,48,..., dimensions={0} | all-to-all | bytes 2162688 | tf_op jit(solution)/shard_map/cond/branch_0_fun/all_to_all | solution.py:314
  75.9 0.0 copy-start
  75.9 0.0 copy-start.1
  75.9 0.0 copy-start.2
  76.0 0.0 copy-start.3
  76.0 0.1 join.7
  76.0 0.1 collective-permute-start.1
  76.1 0.8 copy-done
  76.9 0.1 copy-done.1
  77.0 0.1 copy-done.2
  77.1 0.1 copy-done.3
  77.1 1.0 %unpack.2 = (bf16[128,1024]{1,0:T(8,128)(2,1)}, bf16[128,1024]{1,0:T(8,128)(2,1)}, bf16[128,1024]{1,0:T(8,128)(2,1)}, bf16[128,1024]{1,0:T(8,128)(2,1)}, f32[64,128]{1,0:T(8,128)}) custom-call(f32[2112,128]{1,0:T(8,128)S(1)} %get-tuple-element.78.refs_0_, bf16[128,1024]{1,0:T(8,128)(2,1)S(1)} %copy-done.3, bf16[128,1024]{1,0:T(8,128)(2,1)S(1)} %copy-done, ...), custom_call_target="tpu_custom_call" | custom-call | tf_op jit(solution)/shard_map/unpack/pallas_call | solution.py:397
  78.1 0.0 collective-permute-done.1.refs_0_
  78.1 1.0 %unpack.3 = (bf16[128,1024]{1,0:T(8,128)(2,1)}, bf16[128,1024]{1,0:T(8,128)(2,1)}, bf16[128,1024]{1,0:T(8,128)(2,1)}, bf16[128,1024]{1,0:T(8,128)(2,1)}, f32[64,128]{1,0:T(8,128)}) custom-call(f32[1056,128]{1,0:T(8,128)S(1)} %collective-permute-done.1.refs_0_, ...), custom_call_target="tpu_custom_call", output_to_operand_aliasing={{0}: (5, {}), {1}: (6, {}), {2}: (7, {}), {3}: (8, {}), {4}... | custom-call | tf_op jit(solution)/shard_map/unpack/pallas_call | solution.py:397
Async XLA Ops:
  1.9 5.0 %copy-start.4 = (bf16[768,256]{1,0:T(8,128)(2,1)S(1)}, bf16[768,256]{1,0:T(8,128)(2,1)}, u32[]{:S(2)}) copy-start(bf16[768,256]{1,0:T(8,128)(2,1)} %constant.25.clone) | copy-start | bytes 1179652
  2.0 5.0 %copy-start.5 = (bf16[768,256]{1,0:T(8,128)(2,1)S(1)}, bf16[768,256]{1,0:T(8,128)(2,1)}, u32[]{:S(2)}) copy-start(bf16[768,256]{1,0:T(8,128)(2,1)} %constant.24.clone) | copy-start | bytes 1179652
  2.0 4.9 %copy-start.6 = (f32[2,64,128]{2,1,0:T(8,128)S(1)}, f32[2,64,128]{2,1,0:T(8,128)}, u32[]{:S(2)}) copy-start(f32[2,64,128]{2,1,0:T(8,128)} %constant.27.clone) | copy-start | bytes 196612
  2.0 4.9 %copy-start.7 = (f32[2,64,128]{2,1,0:T(8,128)S(1)}, f32[2,64,128]{2,1,0:T(8,128)}, u32[]{:S(2)}) copy-start(f32[2,64,128]{2,1,0:T(8,128)} %constant.26.clone) | copy-start | bytes 196612
  2.0 4.9 %copy-start.8 = (bf16[128,192]{1,0:T(8,128)(2,1)S(1)}, bf16[128,192]{1,0:T(8,128)(2,1)}, u32[]{:S(2)}) copy-start(bf16[128,192]{1,0:T(8,128)(2,1)} %constant.22.clone) | copy-start | bytes 147460
  2.0 4.9 %copy-start.9 = (bf16[64,384]{1,0:T(8,128)(2,1)S(1)}, bf16[64,384]{1,0:T(8,128)(2,1)}, u32[]{:S(2)}) copy-start(bf16[64,384]{1,0:T(8,128)(2,1)} %constant.23.clone) | copy-start | bytes 147460
  2.0 4.9 %collective-permute-start = (f32[1056,128]{1,0:T(8,128)S(1)}, f32[1056,128]{1,0:T(8,128)S(1)}, u32[]{:S(2)}, u32[]{:S(2)}) collective-permute-start(f32[1056,128]{1,0:T(8,128)S(1)} %pack.3), channel_id=1, source_target_pairs={{0,1},{1,0},{2,3},{3,2},{4,5},{5,4},{6,7},{7,6},{8,9},{9,8},{10,11... | collective-permute-start | bytes 1622024 | tf_op jit(solution)/shard_map/ppermute | solution.py:356
  7.6 18.3 %all-to-all-start = ((f32[128,1,128]{2,1,0:T(1,128)}), f32[128,1,128]{2,1,0:T(1,128)S(1)}, u32[]{:S(2)}, u32[]{:S(2)}) async-start(f32[128,1,128]{2,1,0:T(1,128)} %bitcast.1), calls=%async_computation | async-start | bytes 131072 | tf_op jit(solution)/shard_map/cond/branch_0_fun/all_to_all | solution.py:314
  75.9 1.0 %copy-start = (bf16[128,1024]{1,0:T(8,128)(2,1)S(1)}, bf16[128,1024]{1,0:T(8,128)(2,1)}, u32[]{:S(2)}) copy-start(bf16[128,1024]{1,0:T(8,128)(2,1)} %refs_2_.7) | copy-start | bytes 786436
  75.9 1.0 %copy-start.1 = (bf16[128,1024]{1,0:T(8,128)(2,1)S(1)}, bf16[128,1024]{1,0:T(8,128)(2,1)}, u32[]{:S(2)}) copy-start(bf16[128,1024]{1,0:T(8,128)(2,1)} %refs_3_.7) | copy-start | bytes 786436
  75.9 1.1 %copy-start.2 = (bf16[128,1024]{1,0:T(8,128)(2,1)S(1)}, bf16[128,1024]{1,0:T(8,128)(2,1)}, u32[]{:S(2)}) copy-start(bf16[128,1024]{1,0:T(8,128)(2,1)} %refs_4_.3) | copy-start | bytes 786436
  76.0 1.2 %copy-start.3 = (bf16[128,1024]{1,0:T(8,128)(2,1)S(1)}, bf16[128,1024]{1,0:T(8,128)(2,1)}, u32[]{:S(2)}) copy-start(bf16[128,1024]{1,0:T(8,128)(2,1)} %refs_1_.7) | copy-start | bytes 786436
  76.0 2.1 %collective-permute-start.1 = (f32[1056,128]{1,0:T(8,128)S(1)}, f32[1056,128]{1,0:T(8,128)S(1)}, u32[]{:S(2)}, u32[]{:S(2)}) collective-permute-start(f32[1056,128]{1,0:T(8,128)S(1)} %join.7), channel_id=1, source_target_pairs={{0,1},{1,0},{2,3},{3,2},{4,5},{5,4},{6,7},{7,6},{8,9},{9,8},{10,11... | collective-permute-start | bytes 1622024 | tf_op jit(solution)/shard_map/ppermute | solution.py:389

commit v6 on v5

--- a/solution.py
+++ b/solution.py
@@ -41,7 +41,7 @@
     bh, bl = split_table(wide_back)
     return (
         np.concatenate([fore_high, fore_high, fore_low], axis=1),
-        np.concatenate([back_high, back_high, back_low], axis=1),
+        np.block([[back_high, back_high], [back_low, np.zeros_like(back_low)]]),
         np.concatenate([fh, fh, fl], axis=0),
         np.concatenate([bh, bh, bl], axis=0),
         turn_fore,
@@ -240,8 +240,9 @@
             high, low = high_ref[place(row), :], low_ref[place(row), :]
             high = jnp.concatenate([high[:, :inner], high[:, inner:]], axis=0)
             low = jnp.concatenate([low[:, :inner], low[:, inner:]], axis=0)
-            columns.append(jnp.concatenate([high, low, high], axis=0))
+            columns.append(jnp.concatenate([high, low], axis=0))
         signal = dot(back, jnp.concatenate(columns, axis=1))
+        signal = signal[:peers] + signal[peers:]
         for index in range(len(columns)):
             out_ref[pl.ds(start + index, peers, stride=rows), :] = signal[
                 :, index * inner : (index + 1) * inner
@@ -321,7 +322,7 @@
     groups = [[2 * host + core for host in range(hosts)] for core in range(2)]
     swap = [(rank, rank ^ 1) for rank in range(peers)]
     params = pltpu.CompilerParams(vmem_limit_bytes=48 * 1024 * 1024)
-    early = 4
+    early = 3
 
     def local(query_gate, key_gate, value_in, filter_raw, grad_out):
         inner, width = query_gate.shape

time: 79.4 us -> 79 us (level)
  no operation moved by 1% of the time
where the time goes in v6:
time: 79 us; the launch traced here: 78.7 us
  blocking collectives  47 us (59%)
  starting transfers between devices  12.7 us (16%)
  waiting for transfers between devices  9.09 us (12%)
  Pallas kernels  8.11 us (10%)
  local copies, waits for them, and re-layouts  1.05 us (1%)
    all_to_all x2, blocking collectives, exchange(): lax.all_to_all(pieces, 'context', 0, 0, axis_index_groups=groups, tiled=T...  47 us
    all_to_all x1, starting transfers between devices, exchange(): lax.all_to_all(pieces, 'context', 0, 0, axis_index_groups=groups, tiled=T...  9.3 us
    all_to_all x1, waiting for transfers between devices, exchange(): lax.all_to_all(pieces, 'context', 0, 0, axis_index_groups=groups, tiled=T...  8.83 us
    ppermute x1, starting transfers between devices, local(): given = lax.ppermute(pack(True), 'context', swap)  3.33 us
    pallas_call x1, Pallas kernels, convolve(): pl.pallas_call(lambda *refs: convolve_kernel(peers, lanes, early, refs[:c...  2.78 us
    pallas_call x2, Pallas kernels, pack(): pl.pallas_call(lambda *refs: pack_kernel(hosts, lanes, other, *refs), out...  2.59 us
    pallas_call x2, Pallas kernels, unpack(): pl.pallas_call(lambda *refs: unpack_kernel(hosts, lanes, given, *refs), o...  1.96 us
  transfers between devices with their start and end apart: 3, of which 2 were waited for; matrix products, arithmetic and copies ran while one was open for 0% of the time, Pallas kernels for 3%

profile of v6, /device:TPU:1, one launch (start us, length us, event | category | flops | bytes accessed | tf_op | source)
XLA Modules:
  0.0 78.7 jit_solution(14795388275068752415)
XLA Ops:
  0.6 1.3 %pack.3 = f32[1056,128]{1,0:T(8,128)S(1)} custom-call(bf16[128,1024]{1,0:T(8,128)(2,1)} %refs_2_.7, bf16[128,1024]{1,0:T(8,128)(2,1)} %refs_3_.7, bf16[128,1024]{1,0:T(8,128)(2,1)} %refs_4_.3, bf16[128,1024]{1,0:T(8,128)(2,1)} %refs_1_.7, f32[64,128]{1,0:T(8,128)} %bitcast.31), custom_call_target="tpu_custom_call" | custom-call | tf_op jit(solution)/shard_map/pack/pallas_call | solution.py:348
  1.9 0.0 copy-start.4
  2.0 0.0 copy-start.5
  2.0 0.0 copy-start.6
  2.0 0.0 copy-start.7
  2.0 0.0 copy-start.8
  2.0 0.0 copy-start.9
  2.0 3.3 %collective-permute-start = (f32[1056,128]{1,0:T(8,128)S(1)}, f32[1056,128]{1,0:T(8,128)S(1)}, u32[]{:S(2)}, u32[]{:S(2)}) collective-permute-start(f32[1056,128]{1,0:T(8,128)S(1)} %pack.3), channel_id=1, source_target_pairs={{0,1},{1,0},{2,3},{3,2},{4,5},{5,4},{6,7},{7,6},{8,9},{9,8},{10,11... | collective-permute-start | bytes 1622024 | tf_op jit(solution)/shard_map/ppermute | solution.py:357
  5.3 1.3 %pack.2 = f32[1056,128]{1,0:T(8,128)S(1)} custom-call(bf16[128,1024]{1,0:T(8,128)(2,1)} %refs_2_.7, bf16[128,1024]{1,0:T(8,128)(2,1)} %refs_3_.7, bf16[128,1024]{1,0:T(8,128)(2,1)} %refs_4_.3, bf16[128,1024]{1,0:T(8,128)(2,1)} %refs_1_.7, f32[64,128]{1,0:T(8,128)} %bitcast.32), custom_call_target="tpu_custom_call" | custom-call | tf_op jit(solution)/shard_map/pack/pallas_call | solution.py:348
  6.6 0.3 collective-permute-done
  6.9 0.0 copy-done.4
  6.9 0.0 copy-done.5
  6.9 0.0 copy-done.6
  6.9 0.0 copy-done.7
  6.9 0.0 copy-done.8
  6.9 0.0 copy-done.9
  6.9 68.6 %conditional.1 = (f32[2112,128]{1,0:T(8,128)S(1)}) conditional(s32[]{:T(128)} %convert_element_type.3, (f32[1056,128]{1,0:T(8,128)S(1)}, f32[1056,128]{1,0:T(8,128)S(1)}, bf16[128,192]{1,0:T(8,128)(2,1)S(1)}, bf16[128,256]{1,0:T(8,128)(2,1)S(1)}, bf16[768,256]{1,0:T(8,128)(2,1)S(1)}, /*index=5*/bf16[768,256]{1,0:T(8,128)(2,1)S(1)}, ...), branch_computations={%region_0.0_spmd, %region_1.0_spmd} | conditional | bytes 4374568 | solution.py:388
  6.9 0.6 join.4
  7.6 9.3 %all-to-all-start = ((f32[96,1,128]{2,1,0:T(1,128)}), f32[96,1,128]{2,1,0:T(1,128)S(1)}, u32[]{:S(2)}, u32[]{:S(2)}) async-start(f32[96,1,128]{2,1,0:T(1,128)} %bitcast.1), calls=%async_computation | async-start | bytes 98304 | tf_op jit(solution)/shard_map/cond/branch_0_fun/all_to_all | solution.py:315
  16.9 0.1 join.5
  17.0 8.8 %all-to-all-done = f32[96,1,128]{2,1,0:T(1,128)S(1)} async-done(((f32[96,1,128]{2,1,0:T(1,128)}), f32[96,1,128]{2,1,0:T(1,128)S(1)}, u32[]{:S(2)}, u32[]{:S(2)}) %all-to-all-start) | async-done | bytes 49184 | tf_op jit(solution)/shard_map/cond/branch_0_fun/all_to_all | solution.py:315
  25.8 21.2 %all_to_all.20 = f32[2016,1,128]{2,1,0:T(1,128)S(1)} all-to-all(f32[2016,1,128]{2,1,0:T(1,128)S(1)} %bitcast.27), channel_id=1, replica_groups={{0,2,4,6,8,10,12,14,16,18,20,22,24,26,28,30,32,34,36,38,40,42,44,46,48,..., dimensions={0} | all-to-all | bytes 2064384 | tf_op jit(solution)/shard_map/cond/branch_0_fun/all_to_all | solution.py:315
  47.0 2.8 %convolve.2 = f32[2112,128]{1,0:T(8,128)S(1)} custom-call(f32[96,128]{1,0:T(8,128)S(1)} %bitcast.28, f32[2016,128]{1,0:T(8,128)S(1)} %bitcast.26, bf16[128,192]{1,0:T(8,128)(2,1)S(1)} %get-tuple-element.39.refs_2_, bf16[128,256]{1,0:T(8,128)(2,1)S(1)} %get-tuple-element.40.refs_3_, bf16[768,256]{1,0:T(8,128)(2,1)S(1)} %get-tuple-element.41.refs_4_, ...), custom_call_target="tpu_custom_call" | custom-call | tf_op jit(solution)/shard_map/cond/branch_0_fun/convolve/pallas_call | solution.py:362
  49.8 25.8 %all_to_all.21 = f32[2112,1,128]{2,1,0:T(1,128)S(1)} all-to-all(f32[2112,1,128]{2,1,0:T(1,128)S(1)} %bitcast.22), channel_id=1, replica_groups={{0,2,4,6,8,10,12,14,16,18,20,22,24,26,28,30,32,34,36,38,40,42,44,46,48,..., dimensions={0} | all-to-all | bytes 2162688 | tf_op jit(solution)/shard_map/cond/branch_0_fun/all_to_all | solution.py:315
  75.6 0.0 copy-start
  75.6 0.0 copy-start.1
  75.6 0.0 copy-start.2
  75.6 0.0 copy-start.3
  75.6 0.1 join.7
  75.6 0.1 collective-permute-start.1
  75.7 0.8 copy-done
  76.5 0.1 copy-done.1
  76.6 0.1 copy-done.2
  76.7 0.1 copy-done.3
  76.8 1.0 %unpack.2 = (bf16[128,1024]{1,0:T(8,128)(2,1)}, bf16[128,1024]{1,0:T(8,128)(2,1)}, bf16[128,1024]{1,0:T(8,128)(2,1)}, bf16[128,1024]{1,0:T(8,128)(2,1)}, f32[64,128]{1,0:T(8,128)}) custom-call(f32[2112,128]{1,0:T(8,128)S(1)} %get-tuple-element.78.refs_0_, bf16[128,1024]{1,0:T(8,128)(2,1)S(1)} %copy-done.3, bf16[128,1024]{1,0:T(8,128)(2,1)S(1)} %copy-done, ...), custom_call_target="tpu_custom_call" | custom-call | tf_op jit(solution)/shard_map/unpack/pallas_call | solution.py:398
  77.7 0.0 collective-permute-done.1.refs_0_
  77.8 1.0 %unpack.3 = (bf16[128,1024]{1,0:T(8,128)(2,1)}, bf16[128,1024]{1,0:T(8,128)(2,1)}, bf16[128,1024]{1,0:T(8,128)(2,1)}, bf16[128,1024]{1,0:T(8,128)(2,1)}, f32[64,128]{1,0:T(8,128)}) custom-call(f32[1056,128]{1,0:T(8,128)S(1)} %collective-permute-done.1.refs_0_, ...), custom_call_target="tpu_custom_call", output_to_operand_aliasing={{0}: (5, {}), {1}: (6, {}), {2}: (7, {}), {3}: (8, {}), {4}... | custom-call | tf_op jit(solution)/shard_map/unpack/pallas_call | solution.py:398
Async XLA Ops:
  1.9 5.0 %copy-start.4 = (bf16[768,256]{1,0:T(8,128)(2,1)S(1)}, bf16[768,256]{1,0:T(8,128)(2,1)}, u32[]{:S(2)}) copy-start(bf16[768,256]{1,0:T(8,128)(2,1)} %constant.25.clone) | copy-start | bytes 1179652
  2.0 5.0 %copy-start.5 = (bf16[768,256]{1,0:T(8,128)(2,1)S(1)}, bf16[768,256]{1,0:T(8,128)(2,1)}, u32[]{:S(2)}) copy-start(bf16[768,256]{1,0:T(8,128)(2,1)} %constant.24.clone) | copy-start | bytes 1179652
  2.0 4.9 %copy-start.6 = (f32[2,64,128]{2,1,0:T(8,128)S(1)}, f32[2,64,128]{2,1,0:T(8,128)}, u32[]{:S(2)}) copy-start(f32[2,64,128]{2,1,0:T(8,128)} %constant.27.clone) | copy-start | bytes 196612
  2.0 4.9 %copy-start.7 = (f32[2,64,128]{2,1,0:T(8,128)S(1)}, f32[2,64,128]{2,1,0:T(8,128)}, u32[]{:S(2)}) copy-start(f32[2,64,128]{2,1,0:T(8,128)} %constant.26.clone) | copy-start | bytes 196612
  2.0 4.9 %copy-start.8 = (bf16[128,256]{1,0:T(8,128)(2,1)S(1)}, bf16[128,256]{1,0:T(8,128)(2,1)}, u32[]{:S(2)}) copy-start(bf16[128,256]{1,0:T(8,128)(2,1)} %constant.23.clone) | copy-start | bytes 196612
  2.0 4.9 %copy-start.9 = (bf16[128,192]{1,0:T(8,128)(2,1)S(1)}, bf16[128,192]{1,0:T(8,128)(2,1)}, u32[]{:S(2)}) copy-start(bf16[128,192]{1,0:T(8,128)(2,1)} %constant.22.clone) | copy-start | bytes 147460
  2.0 4.9 %collective-permute-start = (f32[1056,128]{1,0:T(8,128)S(1)}, f32[1056,128]{1,0:T(8,128)S(1)}, u32[]{:S(2)}, u32[]{:S(2)}) collective-permute-start(f32[1056,128]{1,0:T(8,128)S(1)} %pack.3), channel_id=1, source_target_pairs={{0,1},{1,0},{2,3},{3,2},{4,5},{5,4},{6,7},{7,6},{8,9},{9,8},{10,11... | collective-permute-start | bytes 1622024 | tf_op jit(solution)/shard_map/ppermute | solution.py:357
  7.6 18.2 %all-to-all-start = ((f32[96,1,128]{2,1,0:T(1,128)}), f32[96,1,128]{2,1,0:T(1,128)S(1)}, u32[]{:S(2)}, u32[]{:S(2)}) async-start(f32[96,1,128]{2,1,0:T(1,128)} %bitcast.1), calls=%async_computation | async-start | bytes 98304 | tf_op jit(solution)/shard_map/cond/branch_0_fun/all_to_all | solution.py:315
  75.6 1.0 %copy-start = (bf16[128,1024]{1,0:T(8,128)(2,1)S(1)}, bf16[128,1024]{1,0:T(8,128)(2,1)}, u32[]{:S(2)}) copy-start(bf16[128,1024]{1,0:T(8,128)(2,1)} %refs_2_.7) | copy-start | bytes 786436
  75.6 1.0 %copy-start.1 = (bf16[128,1024]{1,0:T(8,128)(2,1)S(1)}, bf16[128,1024]{1,0:T(8,128)(2,1)}, u32[]{:S(2)}) copy-start(bf16[128,1024]{1,0:T(8,128)(2,1)} %refs_3_.7) | copy-start | bytes 786436
  75.6 1.1 %copy-start.2 = (bf16[128,1024]{1,0:T(8,128)(2,1)S(1)}, bf16[128,1024]{1,0:T(8,128)(2,1)}, u32[]{:S(2)}) copy-start(bf16[128,1024]{1,0:T(8,128)(2,1)} %refs_4_.3) | copy-start | bytes 786436
  75.6 1.2 %copy-start.3 = (bf16[128,1024]{1,0:T(8,128)(2,1)S(1)}, bf16[128,1024]{1,0:T(8,128)(2,1)}, u32[]{:S(2)}) copy-start(bf16[128,1024]{1,0:T(8,128)(2,1)} %refs_1_.7) | copy-start | bytes 786436
  75.6 2.1 %collective-permute-start.1 = (f32[1056,128]{1,0:T(8,128)S(1)}, f32[1056,128]{1,0:T(8,128)S(1)}, u32[]{:S(2)}, u32[]{:S(2)}) collective-permute-start(f32[1056,128]{1,0:T(8,128)S(1)} %join.7), channel_id=1, source_target_pairs={{0,1},{1,0},{2,3},{3,2},{4,5},{5,4},{6,7},{7,6},{8,9},{9,8},{10,11... | collective-permute-start | bytes 1622024 | tf_op jit(solution)/shard_map/ppermute | solution.py:390

commit v7 on v6

--- a/solution.py
+++ b/solution.py
@@ -42,8 +42,8 @@
     return (
         np.concatenate([fore_high, fore_high, fore_low], axis=1),
         np.block([[back_high, back_high], [back_low, np.zeros_like(back_low)]]),
-        np.concatenate([fh, fh, fl], axis=0),
-        np.concatenate([bh, bh, bl], axis=0),
+        np.concatenate([fh, fl], axis=0),
+        np.concatenate([bh, bl], axis=0),
         turn_fore,
         turn_back,
     )
@@ -157,7 +157,8 @@
     def transformed(first, count, table_ref):
         high = high_ref[place(first, count), :]
         low = low_ref[place(first, count), :]
-        return dot(jnp.concatenate([high, low, high], axis=1), table_ref[...])
+        high_table = table_ref[: 2 * inner, :]
+        return dot(high, high_table) + dot(low, high_table) + dot(high, table_ref[2 * inner :, :])
 
     def rotated(real, imag, turn_ref):
         cosine, sine = turn_ref[0], turn_ref[1]
@@ -226,8 +227,8 @@
             corr_im = corr_im + (gated_re * grad_im - gated_im * grad_re)
     put(2 * lanes, jnp.concatenate([corr_re, corr_im], axis=1))
 
-    for first in range(0, rows, chunk):
-        count = min(chunk, rows - first)
+    for first in range(0, rows, 3):
+        count = min(3, rows - first)
         spec = transformed(first, count, wide_back_ref)
         for index in range(count):
             part = spec[index * peers : (index + 1) * peers]
@@ -255,7 +256,7 @@
         refs = refs[:4] + refs[9:]
     else:
         in_ref, *refs = refs
-    query_ref, key_ref, value_ref, grad_ref, *refs = refs
+    key_ref, value_ref, grad_ref, query_ref, *refs = refs
     targets, kept, filter_ref, sems = refs[:5], refs[5:9], refs[9], refs[10]
     rows = 2 * lanes + 1
     half = hosts * lanes
@@ -281,9 +282,9 @@
                     row = (start + offset) // lanes * stride + first + index * lanes
                     blocks.append(in_ref[pl.ds(row, lanes), :])
                 signal = jnp.concatenate(blocks, axis=0).T
-                columns = pl.ds(pl.multiple_of(part * half + start, 128), 128)
+                columns = pl.ds(start, 128)
                 for side, factor in enumerate(pair):
-                    kept[2 * index + side][:, pl.ds(start, 128)] = (
+                    kept[2 * index + side][:, columns] = (
                         factor[:, columns].astype(f32) * signal
                     ).astype(bf16)
             for side in range(2):
@@ -339,6 +340,7 @@
             pltpu.VMEM((hosts, inner), f32),
             pltpu.SemaphoreType.DMA((5,)),
         ]
+        half_wide = jax.ShapeDtypeStruct((inner, width // 2), bf16)
         sources = [
             pltpu.with_memory_space_constraint(array, pltpu.HBM)
             for array in (key_gate, value_in, grad_out, query_gate, filter_raw.T)
@@ -347,15 +349,16 @@
         def pack(other):
             return pl.pallas_call(
                 lambda *refs: pack_kernel(hosts, lanes, other, *refs),
-                out_shape=block_rows(rows),
+                out_shape=(block_rows(rows),) + (half_wide,) * 4,
                 in_specs=[pl.BlockSpec(memory_space=pltpu.HBM)] * 5,
-                scratch_shapes=half_scratch,
+                scratch_shapes=half_scratch[4:],
                 compiler_params=params,
                 name="pack",
             )(*sources)
 
-        given = lax.ppermute(pack(True), "context", swap)
-        own = pack(False)
+        other, *other_factors = pack(True)
+        given = lax.ppermute(other, "context", swap)
+        own, *own_factors = pack(False)
 
         def convolve(*held):
             count = len(held)
@@ -388,13 +391,12 @@
         back = lax.cond(leads, lead, follow, own, given)
         other_back = join(lambda *refs: take_other_kernel(hosts, *refs), rows, back)
         back_given = lax.ppermute(other_back, "context", swap)
-        factors = (query_gate, key_gate, value_in, grad_out)
         wide = jax.ShapeDtypeStruct((inner, width), bf16)
         shapes = (wide,) * 4 + (jax.ShapeDtypeStruct((peers, inner), f32),)
         hbm = pl.BlockSpec(memory_space=pltpu.HBM)
         vmem = pl.BlockSpec(memory_space=pltpu.VMEM)
 
-        def unpack(given, signal, *partial):
+        def unpack(given, signal, factors, *partial):
             return pl.pallas_call(
                 lambda *refs: unpack_kernel(hosts, lanes, given, *refs),
                 out_shape=shapes,
@@ -406,7 +408,9 @@
                 name="unpack",
             )(signal, *factors, *partial)
 
-        *outputs, grad_filter = unpack(True, back_given, *unpack(False, back))
+        *outputs, grad_filter = unpack(
+            True, back_given, other_factors, *unpack(False, back, own_factors)
+        )
         return (*outputs, grad_filter.T)
 
     spec = P("context", "tensor")

time: 79 us -> 79 us (level)
  local copies, waits for them, and re-layouts: 1.05 us -> 0.04 us
  waiting for transfers between devices: 9.09 us -> 9.97 us
    unnamed x20 -> x4, local copies, waits for them, and re-layouts: 1.05 us -> 0.01 us
    ppermute x1, waiting for transfers between devices: 0.01 us -> 0.93 us  [local(): back_given = lax.ppermute(other_back, 'context', swap)]
  transfers between devices with their start and end apart: 3 -> 3, of which waited for: 2 -> 3; matrix products, arithmetic and copies ran while one was open for 0% -> 0% of each run, Pallas kernels for 3% -> 3%
where the time goes in v7:
time: 79 us; the launch traced here: 78.7 us
  blocking collectives  47.2 us (60%)
  starting transfers between devices  12.7 us (16%)
  waiting for transfers between devices  9.97 us (13%)
  Pallas kernels  7.97 us (10%)
    all_to_all x2, blocking collectives, exchange(): lax.all_to_all(pieces, 'context', 0, 0, axis_index_groups=groups, tiled=T...  47.2 us
    all_to_all x1, starting transfers between devices, exchange(): lax.all_to_all(pieces, 'context', 0, 0, axis_index_groups=groups, tiled=T...  9.3 us
    all_to_all x1, waiting for transfers between devices, exchange(): lax.all_to_all(pieces, 'context', 0, 0, axis_index_groups=groups, tiled=T...  8.78 us
    ppermute x1, starting transfers between devices, local(): given = lax.ppermute(other, 'context', swap)  3.33 us
    pallas_call x1, Pallas kernels, convolve(): pl.pallas_call(lambda *refs: convolve_kernel(peers, lanes, early, refs[:c...  2.63 us
    pallas_call x2, Pallas kernels, pack(): pl.pallas_call(lambda *refs: pack_kernel(hosts, lanes, other, *refs), out...  2.63 us
    pallas_call x2, Pallas kernels, unpack(): pl.pallas_call(lambda *refs: unpack_kernel(hosts, lanes, given, *refs), o...  1.94 us
  transfers between devices with their start and end apart: 3, of which 3 were waited for; matrix products, arithmetic and copies ran while one was open for 0% of the time, Pallas kernels for 3%

profile of v7, /device:TPU:1, one launch (start us, length us, event | category | flops | bytes accessed | tf_op | source)
XLA Modules:
  0.0 78.7 jit_solution(1416759780690037308)
XLA Ops:
  0.6 0.0 copy-start
  0.6 0.0 copy-start.3
  0.7 1.3 %pack.3 = (f32[1056,128]{1,0:T(8,128)S(1)}, bf16[128,512]{1,0:T(8,128)(2,1)S(1)}, bf16[128,512]{1,0:T(8,128)(2,1)S(1)}, bf16[128,512]{1,0:T(8,128)(2,1)S(1)}, bf16[128,512]{1,0:T(8,128)(2,1)S(1)}) custom-call(bf16[128,1024]{1,0:T(8,128)(2,1)} %refs_0_.3, bf16[128,1024]{1,0:T(8,128)(2,1)} %refs_1_.3, bf16[128,1024]{1,0:T(8,128)(2,1)} %refs_2_.3, ...), custom_call_target="tpu_custom_call" | custom-call | tf_op jit(solution)/shard_map/pack/pallas_call | solution.py:350
  2.0 3.3 %collective-permute-start = (f32[1056,128]{1,0:T(8,128)S(1)}, f32[1056,128]{1,0:T(8,128)S(1)}, u32[]{:S(2)}, u32[]{:S(2)}) collective-permute-start(f32[1056,128]{1,0:T(8,128)S(1)} %get-tuple-element.79), channel_id=1, source_target_pairs={{0,1},{1,0},{2,3},{3,2},{4,5},{5,4},{6,7},{7,6},{8,9},{9,8},{10,11... | collective-permute-start | bytes 1622024 | tf_op jit(solution)/shard_map/ppermute | solution.py:360
  5.3 1.3 %pack.2 = (f32[1056,128]{1,0:T(8,128)S(1)}, bf16[128,512]{1,0:T(8,128)(2,1)S(1)}, bf16[128,512]{1,0:T(8,128)(2,1)S(1)}, bf16[128,512]{1,0:T(8,128)(2,1)S(1)}, bf16[128,512]{1,0:T(8,128)(2,1)S(1)}) custom-call(bf16[128,1024]{1,0:T(8,128)(2,1)} %refs_0_.3, bf16[128,1024]{1,0:T(8,128)(2,1)} %refs_1_.3, bf16[128,1024]{1,0:T(8,128)(2,1)} %refs_2_.3, ...), custom_call_target="tpu_custom_call" | custom-call | tf_op jit(solution)/shard_map/pack/pallas_call | solution.py:350
  6.6 0.3 collective-permute-done
  6.9 0.0 copy-done
  6.9 0.0 copy-done.3
  6.9 68.8 %conditional.1 = (f32[2112,128]{1,0:T(8,128)S(1)}) conditional(s32[]{:T(128)} %convert_element_type.3, (f32[1056,128]{1,0:T(8,128)S(1)}, f32[1056,128]{1,0:T(8,128)S(1)}, bf16[128,192]{1,0:T(8,128)(2,1)}, bf16[128,256]{1,0:T(8,128)(2,1)}, bf16[512,256]{1,0:T(8,128)(2,1)}, /*index=5*/bf16[512,256]{1,0:T(8,128)(2,1)S(1)}, f32[2,64,128]{2,1,0:T(8,128)}, ...), branch_computations={%region_0.0_spmd, %region_1.0_spmd} | conditional | bytes 6144152 | solution.py:391
  6.9 0.6 join.4
  7.5 9.3 %all-to-all-start = ((f32[96,1,128]{2,1,0:T(1,128)}), f32[96,1,128]{2,1,0:T(1,128)S(1)}, u32[]{:S(2)}, u32[]{:S(2)}) async-start(f32[96,1,128]{2,1,0:T(1,128)} %bitcast.1), calls=%async_computation | async-start | bytes 98304 | tf_op jit(solution)/shard_map/cond/branch_0_fun/all_to_all | solution.py:316
  16.8 0.1 join.5
  16.9 0.0 copy-start.4
  16.9 0.0 copy-start.6
  17.0 0.0 copy-start.8
  17.0 8.8 %all-to-all-done = f32[96,1,128]{2,1,0:T(1,128)S(1)} async-done(((f32[96,1,128]{2,1,0:T(1,128)}), f32[96,1,128]{2,1,0:T(1,128)S(1)}, u32[]{:S(2)}, u32[]{:S(2)}) %all-to-all-start) | async-done | bytes 49184 | tf_op jit(solution)/shard_map/cond/branch_0_fun/all_to_all | solution.py:316
  25.8 0.0 copy-start.1
  25.8 20.7 %all_to_all.20 = f32[2016,1,128]{2,1,0:T(1,128)S(1)} all-to-all(f32[2016,1,128]{2,1,0:T(1,128)S(1)} %bitcast.27), channel_id=1, replica_groups={{0,2,4,6,8,10,12,14,16,18,20,22,24,26,28,30,32,34,36,38,40,42,44,46,48,..., dimensions={0} | all-to-all | bytes 2064384 | tf_op jit(solution)/shard_map/cond/branch_0_fun/all_to_all | solution.py:316
  46.5 0.0 copy-done.4
  46.5 0.0 copy-done.6
  46.5 0.0 copy-done.8
  46.5 0.0 copy-done.1
  46.5 2.6 %convolve.2 = f32[2112,128]{1,0:T(8,128)S(1)} custom-call(f32[96,128]{1,0:T(8,128)S(1)} %bitcast.28, f32[2016,128]{1,0:T(8,128)S(1)} %bitcast.26, bf16[128,192]{1,0:T(8,128)(2,1)S(1)} %copy-done.8, bf16[128,256]{1,0:T(8,128)(2,1)S(1)} %copy-done.6, bf16[512,256]{1,0:T(8,128)(2,1)S(1)} %copy-done.1, bf16[512,256]{1,0:T(8,128)(2,1)S(1)} %get-tuple-element.42.refs_5_, ...), custom_call_target="tpu_custom_call" | custom-call | tf_op jit(solution)/shard_map/cond/branch_0_fun/convolve/pallas_call | solution.py:365
  49.1 26.5 %all_to_all.21 = f32[2112,1,128]{2,1,0:T(1,128)S(1)} all-to-all(f32[2112,1,128]{2,1,0:T(1,128)S(1)} %bitcast.23), channel_id=1, replica_groups={{0,2,4,6,8,10,12,14,16,18,20,22,24,26,28,30,32,34,36,38,40,42,44,46,48,..., dimensions={0} | all-to-all | bytes 2162688 | tf_op jit(solution)/shard_map/cond/branch_0_fun/all_to_all | solution.py:316
  75.7 0.1 collective-permute-start.1
  75.8 1.0 %unpack.2 = (bf16[128,1024]{1,0:T(8,128)(2,1)}, bf16[128,1024]{1,0:T(8,128)(2,1)}, bf16[128,1024]{1,0:T(8,128)(2,1)}, bf16[128,1024]{1,0:T(8,128)(2,1)}, f32[64,128]{1,0:T(8,128)}) custom-call(f32[2112,128]{1,0:T(8,128)S(1)} %get-tuple-element.98.refs_0_, bf16[128,512]{1,0:T(8,128)(2,1)S(1)} %get-tuple-element.84.refs_1_, ...), custom_call_target="tpu_custom_call" | custom-call | tf_op jit(solution)/shard_map/unpack/pallas_call | solution.py:400
  76.8 0.9 %collective-permute-done.1.refs_0_ = f32[1056,128]{1,0:T(8,128)S(1)} collective-permute-done((f32[1056,128]{1,0:T(8,128)S(1)}, f32[1056,128]{1,0:T(8,128)S(1)}, u32[]{:S(2)}, u32[]{:S(2)}) %collective-permute-start.1) | collective-permute-done | bytes 540704 | tf_op jit(solution)/shard_map/ppermute | solution.py:393
  77.7 1.0 %unpack.3 = (bf16[128,1024]{1,0:T(8,128)(2,1)}, bf16[128,1024]{1,0:T(8,128)(2,1)}, bf16[128,1024]{1,0:T(8,128)(2,1)}, bf16[128,1024]{1,0:T(8,128)(2,1)}, f32[64,128]{1,0:T(8,128)}) custom-call(f32[1056,128]{1,0:T(8,128)S(1)} %collective-permute-done.1.refs_0_, ...), custom_call_target="tpu_custom_call", output_to_operand_aliasing={{0}: (5, {}), {1}: (6, {}), {2}: (7, {}), {3}: (8, {}), {4}... | custom-call | tf_op jit(solution)/shard_map/unpack/pallas_call | solution.py:400
  (1 shorter events, 0.0 us)
Async XLA Ops:
  0.6 6.3 %copy-start = (bf16[512,256]{1,0:T(8,128)(2,1)S(1)}, bf16[512,256]{1,0:T(8,128)(2,1)}, u32[]{:S(2)}) copy-start(bf16[512,256]{1,0:T(8,128)(2,1)} %constant.25.clone) | copy-start | bytes 786436
  0.6 6.3 %copy-start.3 = (f32[2,64,128]{2,1,0:T(8,128)S(1)}, f32[2,64,128]{2,1,0:T(8,128)}, u32[]{:S(2)}) copy-start(f32[2,64,128]{2,1,0:T(8,128)} %constant.27.clone) | copy-start | bytes 196612
  2.0 4.9 %collective-permute-start = (f32[1056,128]{1,0:T(8,128)S(1)}, f32[1056,128]{1,0:T(8,128)S(1)}, u32[]{:S(2)}, u32[]{:S(2)}) collective-permute-start(f32[1056,128]{1,0:T(8,128)S(1)} %get-tuple-element.79), channel_id=1, source_target_pairs={{0,1},{1,0},{2,3},{3,2},{4,5},{5,4},{6,7},{7,6},{8,9},{9,8},{10,11... | collective-permute-start | bytes 1622024 | tf_op jit(solution)/shard_map/ppermute | solution.py:360
  7.5 18.2 %all-to-all-start = ((f32[96,1,128]{2,1,0:T(1,128)}), f32[96,1,128]{2,1,0:T(1,128)S(1)}, u32[]{:S(2)}, u32[]{:S(2)}) async-start(f32[96,1,128]{2,1,0:T(1,128)} %bitcast.1), calls=%async_computation | async-start | bytes 98304 | tf_op jit(solution)/shard_map/cond/branch_0_fun/all_to_all | solution.py:316
  16.9 29.5 %copy-start.4 = (f32[2,64,128]{2,1,0:T(8,128)S(1)}, f32[2,64,128]{2,1,0:T(8,128)}, u32[]{:S(2)}) copy-start(f32[2,64,128]{2,1,0:T(8,128)} %get-tuple-element.43.refs_6_) | copy-start | bytes 196612 | tf_op jit(solution)/shard_map/cond
  16.9 29.5 %copy-start.6 = (bf16[128,256]{1,0:T(8,128)(2,1)S(1)}, bf16[128,256]{1,0:T(8,128)(2,1)}, u32[]{:S(2)}) copy-start(bf16[128,256]{1,0:T(8,128)(2,1)} %get-tuple-element.40.refs_3_) | copy-start | bytes 196612 | tf_op jit(solution)/shard_map/cond
  17.0 29.5 %copy-start.8 = (bf16[128,192]{1,0:T(8,128)(2,1)S(1)}, bf16[128,192]{1,0:T(8,128)(2,1)}, u32[]{:S(2)}) copy-start(bf16[128,192]{1,0:T(8,128)(2,1)} %get-tuple-element.39.refs_2_) | copy-start | bytes 147460 | tf_op jit(solution)/shard_map/cond
  25.8 20.7 %copy-start.1 = (bf16[512,256]{1,0:T(8,128)(2,1)S(1)}, bf16[512,256]{1,0:T(8,128)(2,1)}, u32[]{:S(2)}) copy-start(bf16[512,256]{1,0:T(8,128)(2,1)} %get-tuple-element.41.refs_4_) | copy-start | bytes 786436 | tf_op jit(solution)/shard_map/cond
  75.7 2.0 %collective-permute-start.1 = (f32[1056,128]{1,0:T(8,128)S(1)}, f32[1056,128]{1,0:T(8,128)S(1)}, u32[]{:S(2)}, u32[]{:S(2)}) collective-permute-start(f32[1056,128]{1,0:T(8,128)S(1)} %join.7), channel_id=1, source_target_pairs={{0,1},{1,0},{2,3},{3,2},{4,5},{5,4},{6,7},{7,6},{8,9},{9,8},{10,11... | collective-permute-start | bytes 1622024 | tf_op jit(solution)/shard_map/ppermute | solution.py:393

commit v8 on v7

--- a/solution.py
+++ b/solution.py
@@ -385,7 +385,7 @@
             sent = join(
                 lambda *refs: join_late_kernel(hosts, early, *refs), 2 * rows - early, own, given
             )
-            held_ahead = exchange(ahead, groups)
+            held_ahead, sent = lax.optimization_barrier((exchange(ahead, groups), sent))
             return exchange(convolve(held_ahead, exchange(sent, groups)), groups)
 
         back = lax.cond(leads, lead, follow, own, given)

time: 79 us -> 79 us (level)
  no operation moved by 1% of the time
where the time goes in v8:
time: 79 us; the launch traced here: 78.7 us
  blocking collectives  47.2 us (60%)
  starting transfers between devices  12.7 us (16%)
  waiting for transfers between devices  9.97 us (13%)
  Pallas kernels  7.97 us (10%)
    all_to_all x2, blocking collectives, exchange(): lax.all_to_all(pieces, 'context', 0, 0, axis_index_groups=groups, tiled=T...  47.2 us
    all_to_all x1, starting transfers between devices, exchange(): lax.all_to_all(pieces, 'context', 0, 0, axis_index_groups=groups, tiled=T...  9.3 us
    all_to_all x1, waiting for transfers between devices, exchange(): lax.all_to_all(pieces, 'context', 0, 0, axis_index_groups=groups, tiled=T...  8.78 us
    ppermute x1, starting transfers between devices, local(): given = lax.ppermute(other, 'context', swap)  3.33 us
    pallas_call x1, Pallas kernels, convolve(): pl.pallas_call(lambda *refs: convolve_kernel(peers, lanes, early, refs[:c...  2.63 us
    pallas_call x2, Pallas kernels, pack(): pl.pallas_call(lambda *refs: pack_kernel(hosts, lanes, other, *refs), out...  2.63 us
    pallas_call x2, Pallas kernels, unpack(): pl.pallas_call(lambda *refs: unpack_kernel(hosts, lanes, given, *refs), o...  1.94 us
  transfers between devices with their start and end apart: 3, of which 3 were waited for; matrix products, arithmetic and copies ran while one was open for 0% of the time, Pallas kernels for 3%

profile of v8, /device:TPU:1, one launch (start us, length us, event | category | flops | bytes accessed | tf_op | source)
XLA Modules:
  0.0 78.7 jit_solution(1416759780690037308)
XLA Ops:
  0.6 0.0 copy-start
  0.6 0.0 copy-start.3
  0.7 1.3 %pack.3 = (f32[1056,128]{1,0:T(8,128)S(1)}, bf16[128,512]{1,0:T(8,128)(2,1)S(1)}, bf16[128,512]{1,0:T(8,128)(2,1)S(1)}, bf16[128,512]{1,0:T(8,128)(2,1)S(1)}, bf16[128,512]{1,0:T(8,128)(2,1)S(1)}) custom-call(bf16[128,1024]{1,0:T(8,128)(2,1)} %refs_0_.3, bf16[128,1024]{1,0:T(8,128)(2,1)} %refs_1_.3, bf16[128,1024]{1,0:T(8,128)(2,1)} %refs_2_.3, ...), custom_call_target="tpu_custom_call" | custom-call | tf_op jit(solution)/shard_map/pack/pallas_call | solution.py:350
  2.0 3.3 %collective-permute-start = (f32[1056,128]{1,0:T(8,128)S(1)}, f32[1056,128]{1,0:T(8,128)S(1)}, u32[]{:S(2)}, u32[]{:S(2)}) collective-permute-start(f32[1056,128]{1,0:T(8,128)S(1)} %get-tuple-element.81), channel_id=1, source_target_pairs={{0,1},{1,0},{2,3},{3,2},{4,5},{5,4},{6,7},{7,6},{8,9},{9,8},{10,11... | collective-permute-start | bytes 1622024 | tf_op jit(solution)/shard_map/ppermute | solution.py:360
  5.3 1.3 %pack.2 = (f32[1056,128]{1,0:T(8,128)S(1)}, bf16[128,512]{1,0:T(8,128)(2,1)S(1)}, bf16[128,512]{1,0:T(8,128)(2,1)S(1)}, bf16[128,512]{1,0:T(8,128)(2,1)S(1)}, bf16[128,512]{1,0:T(8,128)(2,1)S(1)}) custom-call(bf16[128,1024]{1,0:T(8,128)(2,1)} %refs_0_.3, bf16[128,1024]{1,0:T(8,128)(2,1)} %refs_1_.3, bf16[128,1024]{1,0:T(8,128)(2,1)} %refs_2_.3, ...), custom_call_target="tpu_custom_call" | custom-call | tf_op jit(solution)/shard_map/pack/pallas_call | solution.py:350
  6.6 0.3 collective-permute-done
  6.9 0.0 copy-done
  6.9 0.0 copy-done.3
  6.9 68.8 %conditional.1 = (f32[2112,128]{1,0:T(8,128)S(1)}) conditional(s32[]{:T(128)} %convert_element_type.3, (f32[1056,128]{1,0:T(8,128)S(1)}, f32[1056,128]{1,0:T(8,128)S(1)}, bf16[128,192]{1,0:T(8,128)(2,1)}, bf16[128,256]{1,0:T(8,128)(2,1)}, bf16[512,256]{1,0:T(8,128)(2,1)}, /*index=5*/bf16[512,256]{1,0:T(8,128)(2,1)S(1)}, f32[2,64,128]{2,1,0:T(8,128)}, ...), branch_computations={%region_0.0_spmd, %region_1.0_spmd} | conditional | bytes 6144152 | solution.py:391
  6.9 0.6 join.4
  7.5 9.3 %all-to-all-start = ((f32[96,1,128]{2,1,0:T(1,128)}), f32[96,1,128]{2,1,0:T(1,128)S(1)}, u32[]{:S(2)}, u32[]{:S(2)}) async-start(f32[96,1,128]{2,1,0:T(1,128)} %bitcast.1), calls=%async_computation | async-start | bytes 98304 | tf_op jit(solution)/shard_map/cond/branch_0_fun/all_to_all | solution.py:316
  16.8 0.1 join.5
  16.9 0.0 copy-start.4
  16.9 0.0 copy-start.6
  17.0 0.0 copy-start.8
  17.0 8.8 %all-to-all-done = f32[96,1,128]{2,1,0:T(1,128)S(1)} async-done(((f32[96,1,128]{2,1,0:T(1,128)}), f32[96,1,128]{2,1,0:T(1,128)S(1)}, u32[]{:S(2)}, u32[]{:S(2)}) %all-to-all-start) | async-done | bytes 49184 | tf_op jit(solution)/shard_map/cond/branch_0_fun/all_to_all | solution.py:316
  25.8 0.0 copy-start.1
  25.8 20.7 %all_to_all.20 = f32[2016,1,128]{2,1,0:T(1,128)S(1)} all-to-all(f32[2016,1,128]{2,1,0:T(1,128)S(1)} %bitcast.27), channel_id=1, replica_groups={{0,2,4,6,8,10,12,14,16,18,20,22,24,26,28,30,32,34,36,38,40,42,44,46,48,..., dimensions={0} | all-to-all | bytes 2064384 | tf_op jit(solution)/shard_map/cond/branch_0_fun/all_to_all | solution.py:316
  46.5 0.0 copy-done.4
  46.5 0.0 copy-done.6
  46.5 0.0 copy-done.8
  46.5 0.0 copy-done.1
  46.5 2.6 %convolve.2 = f32[2112,128]{1,0:T(8,128)S(1)} custom-call(f32[96,128]{1,0:T(8,128)S(1)} %bitcast.28, f32[2016,128]{1,0:T(8,128)S(1)} %bitcast.26, bf16[128,192]{1,0:T(8,128)(2,1)S(1)} %copy-done.8, bf16[128,256]{1,0:T(8,128)(2,1)S(1)} %copy-done.6, bf16[512,256]{1,0:T(8,128)(2,1)S(1)} %copy-done.1, bf16[512,256]{1,0:T(8,128)(2,1)S(1)} %get-tuple-element.44.refs_5_, ...), custom_call_target="tpu_custom_call" | custom-call | tf_op jit(solution)/shard_map/cond/branch_0_fun/convolve/pallas_call | solution.py:365
  49.1 26.5 %all_to_all.21 = f32[2112,1,128]{2,1,0:T(1,128)S(1)} all-to-all(f32[2112,1,128]{2,1,0:T(1,128)S(1)} %bitcast.23), channel_id=1, replica_groups={{0,2,4,6,8,10,12,14,16,18,20,22,24,26,28,30,32,34,36,38,40,42,44,46,48,..., dimensions={0} | all-to-all | bytes 2162688 | tf_op jit(solution)/shard_map/cond/branch_0_fun/all_to_all | solution.py:316
  75.7 0.1 collective-permute-start.1
  75.8 1.0 %unpack.2 = (bf16[128,1024]{1,0:T(8,128)(2,1)}, bf16[128,1024]{1,0:T(8,128)(2,1)}, bf16[128,1024]{1,0:T(8,128)(2,1)}, bf16[128,1024]{1,0:T(8,128)(2,1)}, f32[64,128]{1,0:T(8,128)}) custom-call(f32[2112,128]{1,0:T(8,128)S(1)} %get-tuple-element.100.refs_0_, bf16[128,512]{1,0:T(8,128)(2,1)S(1)} %get-tuple-element.86.refs_1_, ...), custom_call_target="tpu_custom_call" | custom-call | tf_op jit(solution)/shard_map/unpack/pallas_call | solution.py:400
  76.8 0.9 %collective-permute-done.1.refs_0_ = f32[1056,128]{1,0:T(8,128)S(1)} collective-permute-done((f32[1056,128]{1,0:T(8,128)S(1)}, f32[1056,128]{1,0:T(8,128)S(1)}, u32[]{:S(2)}, u32[]{:S(2)}) %collective-permute-start.1) | collective-permute-done | bytes 540704 | tf_op jit(solution)/shard_map/ppermute | solution.py:393
  77.7 1.0 %unpack.3 = (bf16[128,1024]{1,0:T(8,128)(2,1)}, bf16[128,1024]{1,0:T(8,128)(2,1)}, bf16[128,1024]{1,0:T(8,128)(2,1)}, bf16[128,1024]{1,0:T(8,128)(2,1)}, f32[64,128]{1,0:T(8,128)}) custom-call(f32[1056,128]{1,0:T(8,128)S(1)} %collective-permute-done.1.refs_0_, ...), custom_call_target="tpu_custom_call", output_to_operand_aliasing={{0}: (5, {}), {1}: (6, {}), {2}: (7, {}), {3}: (8, {}), {4}... | custom-call | tf_op jit(solution)/shard_map/unpack/pallas_call | solution.py:400
  (1 shorter events, 0.0 us)
Async XLA Ops:
  0.6 6.3 %copy-start = (bf16[512,256]{1,0:T(8,128)(2,1)S(1)}, bf16[512,256]{1,0:T(8,128)(2,1)}, u32[]{:S(2)}) copy-start(bf16[512,256]{1,0:T(8,128)(2,1)} %constant.25.clone) | copy-start | bytes 786436
  0.6 6.3 %copy-start.3 = (f32[2,64,128]{2,1,0:T(8,128)S(1)}, f32[2,64,128]{2,1,0:T(8,128)}, u32[]{:S(2)}) copy-start(f32[2,64,128]{2,1,0:T(8,128)} %constant.27.clone) | copy-start | bytes 196612
  2.0 4.9 %collective-permute-start = (f32[1056,128]{1,0:T(8,128)S(1)}, f32[1056,128]{1,0:T(8,128)S(1)}, u32[]{:S(2)}, u32[]{:S(2)}) collective-permute-start(f32[1056,128]{1,0:T(8,128)S(1)} %get-tuple-element.81), channel_id=1, source_target_pairs={{0,1},{1,0},{2,3},{3,2},{4,5},{5,4},{6,7},{7,6},{8,9},{9,8},{10,11... | collective-permute-start | bytes 1622024 | tf_op jit(solution)/shard_map/ppermute | solution.py:360
  7.5 18.2 %all-to-all-start = ((f32[96,1,128]{2,1,0:T(1,128)}), f32[96,1,128]{2,1,0:T(1,128)S(1)}, u32[]{:S(2)}, u32[]{:S(2)}) async-start(f32[96,1,128]{2,1,0:T(1,128)} %bitcast.1), calls=%async_computation | async-start | bytes 98304 | tf_op jit(solution)/shard_map/cond/branch_0_fun/all_to_all | solution.py:316
  16.9 29.5 %copy-start.4 = (f32[2,64,128]{2,1,0:T(8,128)S(1)}, f32[2,64,128]{2,1,0:T(8,128)}, u32[]{:S(2)}) copy-start(f32[2,64,128]{2,1,0:T(8,128)} %get-tuple-element.45.refs_6_) | copy-start | bytes 196612 | tf_op jit(solution)/shard_map/cond
  16.9 29.5 %copy-start.6 = (bf16[128,256]{1,0:T(8,128)(2,1)S(1)}, bf16[128,256]{1,0:T(8,128)(2,1)}, u32[]{:S(2)}) copy-start(bf16[128,256]{1,0:T(8,128)(2,1)} %get-tuple-element.42.refs_3_) | copy-start | bytes 196612 | tf_op jit(solution)/shard_map/cond
  17.0 29.5 %copy-start.8 = (bf16[128,192]{1,0:T(8,128)(2,1)S(1)}, bf16[128,192]{1,0:T(8,128)(2,1)}, u32[]{:S(2)}) copy-start(bf16[128,192]{1,0:T(8,128)(2,1)} %get-tuple-element.41.refs_2_) | copy-start | bytes 147460 | tf_op jit(solution)/shard_map/cond
  25.8 20.7 %copy-start.1 = (bf16[512,256]{1,0:T(8,128)(2,1)S(1)}, bf16[512,256]{1,0:T(8,128)(2,1)}, u32[]{:S(2)}) copy-start(bf16[512,256]{1,0:T(8,128)(2,1)} %get-tuple-element.43.refs_4_) | copy-start | bytes 786436 | tf_op jit(solution)/shard_map/cond
  75.7 2.0 %collective-permute-start.1 = (f32[1056,128]{1,0:T(8,128)S(1)}, f32[1056,128]{1,0:T(8,128)S(1)}, u32[]{:S(2)}, u32[]{:S(2)}) collective-permute-start(f32[1056,128]{1,0:T(8,128)S(1)} %join.7), channel_id=1, source_target_pairs={{0,1},{1,0},{2,3},{3,2},{4,5},{5,4},{6,7},{7,6},{8,9},{9,8},{10,11... | collective-permute-start | bytes 1622024 | tf_op jit(solution)/shard_map/ppermute | solution.py:393

commit v9 on v8

--- a/solution.py
+++ b/solution.py
@@ -59,7 +59,9 @@
 
 
 def pack_kernel(hosts, lanes, other, *refs):
-    sources, out_ref, targets, sems = refs[:5], refs[5], refs[6:11], refs[11]
+    sources, sems = refs[:5], refs[-1]
+    outs, targets = refs[5:-6], refs[-6:-1]
+    first_rows = (0, lanes) if other else (0, 0)
     rows = 2 * lanes + 1
     half = hosts * lanes
     core = lax.rem(lax.axis_index("context"), 2)
@@ -82,10 +84,14 @@
             product = left[:, place].astype(f32) * right[:, place].astype(f32)
             turned = product.T
             for offset in range(0, 128, lanes):
-                first = (start + offset) // lanes * rows + index * lanes
+                out_ref = outs[index] if other else outs[0]
+                stride = out_ref.shape[0] // hosts
+                first = (start + offset) // lanes * stride + index * lanes - first_rows[index]
                 out_ref[pl.ds(first, lanes), :] = turned[offset : offset + lanes]
     copies[4].wait()
-    out_ref[pl.ds(2 * lanes, hosts, stride=rows), :] = targets[4][...]
+    out_ref = outs[1] if other else outs[0]
+    stride = out_ref.shape[0] // hosts
+    out_ref[pl.ds(stride - 1, hosts, stride=stride), :] = targets[4][...]
 
 
 def take_kernel(hosts, first, own_ref, out_ref):
@@ -107,22 +113,16 @@
         take_kernel(hosts, 0, back_ref, out_ref)
 
 
-def join_kernel(hosts, first_ref, second_ref, out_ref):
-    rows = first_ref.shape[0] // hosts
-    more = second_ref.shape[0] // hosts
+def join_kernel(hosts, skipped, *refs):
+    *parts, out_ref = refs
+    total = out_ref.shape[0] // hosts
     for host in range(hosts):
-        start = host * (rows + more)
-        out_ref[pl.ds(start, rows), :] = first_ref[pl.ds(host * rows, rows), :]
-        out_ref[pl.ds(start + rows, more), :] = second_ref[pl.ds(host * more, more), :]
-
-
-def join_late_kernel(hosts, early, own_ref, given_ref, out_ref):
-    rows = own_ref.shape[0] // hosts
-    late = rows - early
-    for host in range(hosts):
-        start = host * (rows + late)
-        out_ref[pl.ds(start, late), :] = own_ref[pl.ds(host * rows + early, late), :]
-        out_ref[pl.ds(start + late, rows), :] = given_ref[pl.ds(host * rows, rows), :]
+        start = host * total
+        for index, part in enumerate(parts):
+            rows = part.shape[0] // hosts
+            skip = 0 if index else skipped
+            out_ref[pl.ds(start, rows - skip), :] = part[pl.ds(host * rows + skip, rows - skip), :]
+            start += rows - skip
 
 
 def convolve_kernel(
@@ -349,15 +349,19 @@
         def pack(other):
             return pl.pallas_call(
                 lambda *refs: pack_kernel(hosts, lanes, other, *refs),
-                out_shape=(block_rows(rows),) + (half_wide,) * 4,
+                out_shape=(
+                    (block_rows(lanes), block_rows(lanes + 1)) if other else (block_rows(rows),)
+                )
+                + (half_wide,) * 4,
                 in_specs=[pl.BlockSpec(memory_space=pltpu.HBM)] * 5,
                 scratch_shapes=half_scratch[4:],
                 compiler_params=params,
                 name="pack",
             )(*sources)
 
-        other, *other_factors = pack(True)
-        given = lax.ppermute(other, "context", swap)
+        other_gated, other_grad, *other_factors = pack(True)
+        given_gated = lax.ppermute(other_gated, "context", swap)
+        given_grad = lax.ppermute(other_grad, "context", swap)
         own, *own_factors = pack(False)
 
         def convolve(*held):
@@ -376,19 +380,19 @@
             )(*parts)
 
         leads = lax.rem(lax.axis_index("context"), 2) == 0
-        def lead(own, given):
-            sent = join(lambda *refs: join_kernel(hosts, *refs), 2 * rows, own, given)
+        def lead(*parts):
+            sent = join(lambda *refs: join_kernel(hosts, 0, *refs), 2 * rows, *parts)
             return exchange(convolve(exchange(sent, groups)), groups)
 
-        def follow(own, given):
+        def follow(own, *given):
             ahead = join(lambda *refs: take_kernel(hosts, 0, *refs), early, own)
             sent = join(
-                lambda *refs: join_late_kernel(hosts, early, *refs), 2 * rows - early, own, given
+                lambda *refs: join_kernel(hosts, early, *refs), 2 * rows - early, own, *given
             )
             held_ahead, sent = lax.optimization_barrier((exchange(ahead, groups), sent))
             return exchange(convolve(held_ahead, exchange(sent, groups)), groups)
 
-        back = lax.cond(leads, lead, follow, own, given)
+        back = lax.cond(leads, lead, follow, own, given_gated, given_grad)
         other_back = join(lambda *refs: take_other_kernel(hosts, *refs), rows, back)
         back_given = lax.ppermute(other_back, "context", swap)
         wide = jax.ShapeDtypeStruct((inner, width), bf16)

time: 79 us -> 78.9 us (level)
  waiting for transfers between devices: 9.97 us -> 8.93 us
  Pallas kernels: 7.97 us -> 8.98 us
    pallas_call x3, Pallas kernels: 0.75 us -> 1.76 us  [join(): pl.pallas_call(kernel, out_shape=block_rows(size), compiler_params=params...]
    all_to_all x1, waiting for transfers between devices: 8.78 us -> 7.84 us  [exchange(): lax.all_to_all(pieces, 'context', 0, 0, axis_index_groups=groups, tiled=T...]
    ppermute x1 -> x2, starting transfers between devices: 3.33 us -> 3.43 us  [the longest x1 3.33 us: local(): given_grad = lax.ppermute(other_grad, 'context', swap)]
  transfers between devices with their start and end apart: 3 -> 4, of which waited for: 3 -> 3; matrix products, arithmetic and copies ran while one was open for 0% -> 0% of each run, Pallas kernels for 3% -> 4%
where the time goes in v9:
time: 78.9 us; the launch traced here: 78.7 us
  blocking collectives  47.1 us (60%)
  starting transfers between devices  12.8 us (16%)
  Pallas kernels  8.98 us (11%)
  waiting for transfers between devices  8.93 us (11%)
    all_to_all x2, blocking collectives, exchange(): lax.all_to_all(pieces, 'context', 0, 0, axis_index_groups=groups, tiled=T...  47.1 us
    all_to_all x1, starting transfers between devices, exchange(): lax.all_to_all(pieces, 'context', 0, 0, axis_index_groups=groups, tiled=T...  9.3 us
    all_to_all x1, waiting for transfers between devices, exchange(): lax.all_to_all(pieces, 'context', 0, 0, axis_index_groups=groups, tiled=T...  7.84 us
    ppermute x1, starting transfers between devices, local(): given_grad = lax.ppermute(other_grad, 'context', swap)  3.33 us
    pallas_call x2, Pallas kernels, pack(): pl.pallas_call(lambda *refs: pack_kernel(hosts, lanes, other, *refs), out...  2.65 us
    pallas_call x1, Pallas kernels, convolve(): pl.pallas_call(lambda *refs: convolve_kernel(peers, lanes, early, refs[:c...  2.63 us
    pallas_call x2, Pallas kernels, unpack(): pl.pallas_call(lambda *refs: unpack_kernel(hosts, lanes, given, *refs), o...  1.94 us
    pallas_call x3, Pallas kernels, join(): pl.pallas_call(kernel, out_shape=block_rows(size), compiler_params=params...  1.76 us
  transfers between devices with their start and end apart: 4, of which 3 were waited for; matrix products, arithmetic and copies ran while one was open for 0% of the time, Pallas kernels for 4%

profile of v9, /device:TPU:1, one launch (start us, length us, event | category | flops | bytes accessed | tf_op | source)
XLA Modules:
  0.0 78.7 jit_solution(14728063520510470341)
XLA Ops:
  0.6 0.0 copy-start
  0.6 0.0 copy-start.1
  0.7 0.0 copy-start.3
  0.7 1.4 %pack.3 = (f32[512,128]{1,0:T(8,128)S(1)}, f32[544,128]{1,0:T(8,128)S(1)}, bf16[128,512]{1,0:T(8,128)(2,1)S(1)}, bf16[128,512]{1,0:T(8,128)(2,1)S(1)}, bf16[128,...) custom-call(bf16[128,1024]{1,0:T(8,128)(2,1)} %refs_0_.3, bf16[128,1024]{1,0:T(8,128)(2,1)} %refs_1_.3, ...), custom_call_target="tpu_custom_call" | custom-call | tf_op jit(solution)/shard_map/pack/pallas_call | solution.py:350
  2.0 3.3 %collective-permute-start.1 = (f32[544,128]{1,0:T(8,128)S(1)}, f32[544,128]{1,0:T(8,128)S(1)}, u32[]{:S(2)}, u32[]{:S(2)}) collective-permute-start(f32[544,128]{1,0:T(8,128)S(1)} %get-tuple-element.89), channel_id=1, source_target_pairs={{0,1},{1,0},{2,3},{3,2},{4,5},{5,4},{6,7},{7,6},{8,9},{9,8},{10,11... | collective-permute-start | bytes 835592 | tf_op jit(solution)/shard_map/ppermute | solution.py:364
  5.4 0.1 collective-permute-start
  5.5 1.3 %pack.2 = (f32[1056,128]{1,0:T(8,128)S(1)}, bf16[128,512]{1,0:T(8,128)(2,1)S(1)}, bf16[128,512]{1,0:T(8,128)(2,1)S(1)}, bf16[128,512]{1,0:T(8,128)(2,1)S(1)}, bf16[128,512]{1,0:T(8,128)(2,1)S(1)}) custom-call(bf16[128,1024]{1,0:T(8,128)(2,1)} %refs_0_.3, bf16[128,1024]{1,0:T(8,128)(2,1)} %refs_1_.3, bf16[128,1024]{1,0:T(8,128)(2,1)} %refs_2_.3, ...), custom_call_target="tpu_custom_call" | custom-call | tf_op jit(solution)/shard_map/pack/pallas_call | solution.py:350
  6.8 0.2 collective-permute-done
  6.9 0.0 collective-permute-done.1
  6.9 0.0 copy-done
  6.9 0.0 copy-done.1
  6.9 0.0 copy-done.3
  6.9 68.7 %conditional.1 = (f32[2112,128]{1,0:T(8,128)S(1)}) conditional(s32[]{:T(128)} %convert_element_type.3, (f32[1056,128]{1,0:T(8,128)S(1)}, f32[512,128]{1,0:T(8,128)S(1)}, f32[544,128]{1,0:T(8,128)S(1)}, bf16[128,192]{1,0:T(8,128)(2,1)}, bf16[128,256]{1,0:T(8,128)(2,1)}, /*index=5*/bf16[512,256]{1,0:T(8,128)(2,1)S(1)}, bf16[512,256]{1,0:T(8,128)(2,1)S(1)}, ...), branch_computations={%region_0.0_spmd, %region_1.0_spmd} | conditional | bytes 6144152 | solution.py:395
  6.9 0.0 copy-start.2
  7.0 0.7 join.4
  7.6 9.3 %all-to-all-start = ((f32[96,1,128]{2,1,0:T(1,128)}), f32[96,1,128]{2,1,0:T(1,128)S(1)}, u32[]{:S(2)}, u32[]{:S(2)}) async-start(f32[96,1,128]{2,1,0:T(1,128)} %bitcast.1), calls=%async_computation | async-start | bytes 98304 | tf_op jit(solution)/shard_map/cond/branch_0_fun/all_to_all | solution.py:316
  17.0 0.0 copy-done.2
  17.0 1.0 %join.5 = f32[2016,128]{1,0:T(8,128)S(1)} custom-call(f32[1056,128]{1,0:T(8,128)S(1)} %get-tuple-element.41.refs_0_, f32[512,128]{1,0:T(8,128)} %copy-done.2, f32[544,128]{1,0:T(8,128)S(1)} %get-tuple-element.43.refs_2_), custom_call_target="tpu_custom_call" | custom-call | tf_op jit(solution)/shard_map/cond/branch_0_fun/join/pallas_call | solution.py:378
  18.0 0.0 copy-start.4
  18.0 0.0 copy-start.6
  18.0 0.0 copy-start.8
  18.0 7.8 %all-to-all-done = f32[96,1,128]{2,1,0:T(1,128)S(1)} async-done(((f32[96,1,128]{2,1,0:T(1,128)}), f32[96,1,128]{2,1,0:T(1,128)S(1)}, u32[]{:S(2)}, u32[]{:S(2)}) %all-to-all-start) | async-done | bytes 49184 | tf_op jit(solution)/shard_map/cond/branch_0_fun/all_to_all | solution.py:316
  25.9 20.8 %all_to_all.20 = f32[2016,1,128]{2,1,0:T(1,128)S(1)} all-to-all(f32[2016,1,128]{2,1,0:T(1,128)S(1)} %bitcast.27), channel_id=1, replica_groups={{0,2,4,6,8,10,12,14,16,18,20,22,24,26,28,30,32,34,36,38,40,42,44,46,48,..., dimensions={0} | all-to-all | bytes 2064384 | tf_op jit(solution)/shard_map/cond/branch_0_fun/all_to_all | solution.py:316
  46.7 0.0 copy-done.4
  46.7 0.0 copy-done.6
  46.7 0.0 copy-done.8
  46.7 2.6 %convolve.2 = f32[2112,128]{1,0:T(8,128)S(1)} custom-call(f32[96,128]{1,0:T(8,128)S(1)} %bitcast.28, f32[2016,128]{1,0:T(8,128)S(1)} %bitcast.26, bf16[128,192]{1,0:T(8,128)(2,1)S(1)} %copy-done.8, bf16[128,256]{1,0:T(8,128)(2,1)S(1)} %copy-done.6, bf16[512,256]{1,0:T(8,128)(2,1)S(1)} %get-tuple-element.48.refs_4_, ...), custom_call_target="tpu_custom_call" | custom-call | tf_op jit(solution)/shard_map/cond/branch_0_fun/convolve/pallas_call | solution.py:369
  49.4 26.2 %all_to_all.21 = f32[2112,1,128]{2,1,0:T(1,128)S(1)} all-to-all(f32[2112,1,128]{2,1,0:T(1,128)S(1)} %bitcast.23), channel_id=1, replica_groups={{0,2,4,6,8,10,12,14,16,18,20,22,24,26,28,30,32,34,36,38,40,42,44,46,48,..., dimensions={0} | all-to-all | bytes 2162688 | tf_op jit(solution)/shard_map/cond/branch_0_fun/all_to_all | solution.py:316
  75.7 0.1 collective-permute-start.2
  75.8 1.0 %unpack.2 = (bf16[128,1024]{1,0:T(8,128)(2,1)}, bf16[128,1024]{1,0:T(8,128)(2,1)}, bf16[128,1024]{1,0:T(8,128)(2,1)}, bf16[128,1024]{1,0:T(8,128)(2,1)}, f32[64,128]{1,0:T(8,128)}) custom-call(f32[2112,128]{1,0:T(8,128)S(1)} %get-tuple-element.108.refs_0_, bf16[128,512]{1,0:T(8,128)(2,1)S(1)} %get-tuple-element.94.refs_1_, ...), custom_call_target="tpu_custom_call" | custom-call | tf_op jit(solution)/shard_map/unpack/pallas_call | solution.py:404
  76.8 0.9 %collective-permute-done.2.refs_0_ = f32[1056,128]{1,0:T(8,128)S(1)} collective-permute-done((f32[1056,128]{1,0:T(8,128)S(1)}, f32[1056,128]{1,0:T(8,128)S(1)}, u32[]{:S(2)}, u32[]{:S(2)}) %collective-permute-start.2) | collective-permute-done | bytes 540704 | tf_op jit(solution)/shard_map/ppermute | solution.py:397
  77.7 1.0 %unpack.3 = (bf16[128,1024]{1,0:T(8,128)(2,1)}, bf16[128,1024]{1,0:T(8,128)(2,1)}, bf16[128,1024]{1,0:T(8,128)(2,1)}, bf16[128,1024]{1,0:T(8,128)(2,1)}, f32[64,128]{1,0:T(8,128)}) custom-call(f32[1056,128]{1,0:T(8,128)S(1)} %collective-permute-done.2.refs_0_, ...), custom_call_target="tpu_custom_call", output_to_operand_aliasing={{0}: (5, {}), {1}: (6, {}), {2}: (7, {}), {3}: (8, {}), {4}... | custom-call | tf_op jit(solution)/shard_map/unpack/pallas_call | solution.py:404
  (1 shorter events, 0.0 us)
Async XLA Ops:
  0.6 6.3 %copy-start = (bf16[512,256]{1,0:T(8,128)(2,1)S(1)}, bf16[512,256]{1,0:T(8,128)(2,1)}, u32[]{:S(2)}) copy-start(bf16[512,256]{1,0:T(8,128)(2,1)} %constant.25.clone) | copy-start | bytes 786436
  0.6 6.3 %copy-start.1 = (bf16[512,256]{1,0:T(8,128)(2,1)S(1)}, bf16[512,256]{1,0:T(8,128)(2,1)}, u32[]{:S(2)}) copy-start(bf16[512,256]{1,0:T(8,128)(2,1)} %constant.24.clone) | copy-start | bytes 786436
  0.7 6.3 %copy-start.3 = (f32[2,64,128]{2,1,0:T(8,128)S(1)}, f32[2,64,128]{2,1,0:T(8,128)}, u32[]{:S(2)}) copy-start(f32[2,64,128]{2,1,0:T(8,128)} %constant.27.clone) | copy-start | bytes 196612
  2.0 4.9 %collective-permute-start.1 = (f32[544,128]{1,0:T(8,128)S(1)}, f32[544,128]{1,0:T(8,128)S(1)}, u32[]{:S(2)}, u32[]{:S(2)}) collective-permute-start(f32[544,128]{1,0:T(8,128)S(1)} %get-tuple-element.89), channel_id=1, source_target_pairs={{0,1},{1,0},{2,3},{3,2},{4,5},{5,4},{6,7},{7,6},{8,9},{9,8},{10,11... | collective-permute-start | bytes 835592 | tf_op jit(solution)/shard_map/ppermute | solution.py:364
  5.4 1.6 %collective-permute-start = (f32[512,128]{1,0:T(8,128)S(1)}, f32[512,128]{1,0:T(8,128)S(1)}, u32[]{:S(2)}, u32[]{:S(2)}) collective-permute-start(f32[512,128]{1,0:T(8,128)S(1)} %get-tuple-element.88), channel_id=1, source_target_pairs={{0,1},{1,0},{2,3},{3,2},{4,5},{5,4},{6,7},{7,6},{8,9},{9,8},{10,11... | collective-permute-start | bytes 786440 | tf_op jit(solution)/shard_map/ppermute | solution.py:363
  6.9 10.0 %copy-start.2 = (f32[512,128]{1,0:T(8,128)}, f32[512,128]{1,0:T(8,128)S(1)}, u32[]{:S(2)}) copy-start(f32[512,128]{1,0:T(8,128)S(1)} %get-tuple-element.42.refs_1_) | copy-start | bytes 786436 | tf_op jit(solution)/shard_map/cond
  7.6 18.2 %all-to-all-start = ((f32[96,1,128]{2,1,0:T(1,128)}), f32[96,1,128]{2,1,0:T(1,128)S(1)}, u32[]{:S(2)}, u32[]{:S(2)}) async-start(f32[96,1,128]{2,1,0:T(1,128)} %bitcast.1), calls=%async_computation | async-start | bytes 98304 | tf_op jit(solution)/shard_map/cond/branch_0_fun/all_to_all | solution.py:316
  18.0 28.7 %copy-start.4 = (f32[2,64,128]{2,1,0:T(8,128)S(1)}, f32[2,64,128]{2,1,0:T(8,128)}, u32[]{:S(2)}) copy-start(f32[2,64,128]{2,1,0:T(8,128)} %get-tuple-element.50.refs_6_) | copy-start | bytes 196612 | tf_op jit(solution)/shard_map/cond
  18.0 28.7 %copy-start.6 = (bf16[128,256]{1,0:T(8,128)(2,1)S(1)}, bf16[128,256]{1,0:T(8,128)(2,1)}, u32[]{:S(2)}) copy-start(bf16[128,256]{1,0:T(8,128)(2,1)} %get-tuple-element.47.refs_3_) | copy-start | bytes 196612 | tf_op jit(solution)/shard_map/cond
  18.0 28.7 %copy-start.8 = (bf16[128,192]{1,0:T(8,128)(2,1)S(1)}, bf16[128,192]{1,0:T(8,128)(2,1)}, u32[]{:S(2)}) copy-start(bf16[128,192]{1,0:T(8,128)(2,1)} %get-tuple-element.46.refs_2_) | copy-start | bytes 147460 | tf_op jit(solution)/shard_map/cond
  75.7 2.0 %collective-permute-start.2 = (f32[1056,128]{1,0:T(8,128)S(1)}, f32[1056,128]{1,0:T(8,128)S(1)}, u32[]{:S(2)}, u32[]{:S(2)}) collective-permute-start(f32[1056,128]{1,0:T(8,128)S(1)} %join.7), channel_id=1, source_target_pairs={{0,1},{1,0},{2,3},{3,2},{4,5},{5,4},{6,7},{7,6},{8,9},{9,8},{10,11... | collective-permute-start | bytes 1622024 | tf_op jit(solution)/shard_map/ppermute | solution.py:397

commit v10 on v9

--- a/solution.py
+++ b/solution.py
@@ -58,40 +58,71 @@
     return jnp.dot(left, right, preferred_element_type=f32)
 
 
-def pack_kernel(hosts, lanes, other, *refs):
-    sources, sems = refs[:5], refs[-1]
-    outs, targets = refs[5:-6], refs[-6:-1]
-    first_rows = (0, lanes) if other else (0, 0)
+def pack_rows(hosts, lanes, factors, outs, ready):
     rows = 2 * lanes + 1
+    for index in range(2):
+        ready(index)
+        left, right = factors[2 * index], factors[2 * index + 1]
+        out_ref = outs[index % len(outs)]
+        stride = out_ref.shape[0] // hosts
+        skip = index * lanes if stride == rows else 0
+        for start in range(0, hosts * lanes, 128):
+            place = pl.ds(start, 128)
+            turned = (left[:, place].astype(f32) * right[:, place].astype(f32)).T
+            for offset in range(0, 128, lanes):
+                first = (start + offset) // lanes * stride + skip
+                out_ref[pl.ds(first, lanes), :] = turned[offset : offset + lanes]
+
+
+def pack_filter(hosts, part, filter_hbm, filter_ref, sem):
+    rows = pl.ds(pl.multiple_of(part * hosts, hosts), hosts)
+    return pltpu.make_async_copy(filter_hbm.at[rows, :], filter_ref, sem)
+
+
+def pack_other_kernel(hosts, lanes, *refs):
+    sources, outs, other, own, filter_ref, sems = (
+        refs[:5],
+        refs[5:7],
+        refs[7:11],
+        refs[11:15],
+        refs[15],
+        refs[16],
+    )
     half = hosts * lanes
     core = lax.rem(lax.axis_index("context"), 2)
-    part = 1 - core if other else core
-    columns = pl.ds(pl.multiple_of(part * half, half), half)
     copies = []
-    for index in range(4):
-        source = sources[index].at[:, columns]
-        copies.append(pltpu.make_async_copy(source, targets[index], sems.at[index]))
-    source = sources[4].at[pl.ds(pl.multiple_of(part * hosts, hosts), hosts), :]
-    copies.append(pltpu.make_async_copy(source, targets[4], sems.at[4]))
+    for number, (targets, part) in enumerate(((other, 1 - core), (own, core))):
+        columns = pl.ds(pl.multiple_of(part * half, half), half)
+        for index in range(4):
+            source = sources[index].at[:, columns]
+            copies.append(
+                pltpu.make_async_copy(source, targets[index], sems.at[4 * number + index])
+            )
+    copies.append(pack_filter(hosts, 1 - core, sources[4], filter_ref, sems.at[8]))
     for copy in copies:
         copy.start()
-    for index in range(2):
+
+    def ready(index):
         copies[2 * index].wait()
         copies[2 * index + 1].wait()
-        left, right = targets[2 * index], targets[2 * index + 1]
-        for start in range(0, half, 128):
-            place = pl.ds(start, 128)
-            product = left[:, place].astype(f32) * right[:, place].astype(f32)
-            turned = product.T
-            for offset in range(0, 128, lanes):
-                out_ref = outs[index] if other else outs[0]
-                stride = out_ref.shape[0] // hosts
-                first = (start + offset) // lanes * stride + index * lanes - first_rows[index]
-                out_ref[pl.ds(first, lanes), :] = turned[offset : offset + lanes]
-    copies[4].wait()
-    out_ref = outs[1] if other else outs[0]
+
+    pack_rows(hosts, lanes, other, outs, ready)
+    copies[8].wait()
+    stride = outs[1].shape[0] // hosts
+    outs[1][pl.ds(stride - 1, hosts, stride=stride), :] = filter_ref[...]
+    for copy in copies[4:8]:
+        copy.wait()
+
+
+def pack_own_kernel(hosts, lanes, *refs):
+    factors, filter_hbm, out_ref, filter_ref, sems = refs[:4], refs[4], refs[5], refs[6], refs[7]
+    core = lax.rem(lax.axis_index("context"), 2)
+    copy = pack_filter(hosts, core, filter_hbm, filter_ref, sems.at[0])
+    copy.start()
+    pack_rows(hosts, lanes, factors, (out_ref,), lambda index: None)
+    copy.wait()
     stride = out_ref.shape[0] // hosts
-    out_ref[pl.ds(stride - 1, hosts, stride=stride), :] = targets[4][...]
+    out_ref[pl.ds(stride - 1, hosts, stride=stride), :] = filter_ref[...]
 
 
 def take_kernel(hosts, first, own_ref, out_ref):
@@ -346,23 +377,28 @@
             for array in (key_gate, value_in, grad_out, query_gate, filter_raw.T)
         ]
 
-        def pack(other):
-            return pl.pallas_call(
-                lambda *refs: pack_kernel(hosts, lanes, other, *refs),
-                out_shape=(
-                    (block_rows(lanes), block_rows(lanes + 1)) if other else (block_rows(rows),)
-                )
-                + (half_wide,) * 4,
-                in_specs=[pl.BlockSpec(memory_space=pltpu.HBM)] * 5,
-                scratch_shapes=half_scratch[4:],
-                compiler_params=params,
-                name="pack",
-            )(*sources)
-
-        other_gated, other_grad, *other_factors = pack(True)
+        hbm = pl.BlockSpec(memory_space=pltpu.HBM)
+        vmem = pl.BlockSpec(memory_space=pltpu.VMEM)
+        filter_half = pltpu.VMEM((hosts, inner), f32)
+        other_gated, other_grad, *factors = pl.pallas_call(
+            lambda *refs: pack_other_kernel(hosts, lanes, *refs),
+            out_shape=(block_rows(lanes), block_rows(lanes + 1)) + (half_wide,) * 8,
+            in_specs=[hbm] * 5,
+            scratch_shapes=[filter_half, pltpu.SemaphoreType.DMA((9,))],
+            compiler_params=params,
+            name="pack_other",
+        )(*sources)
+        other_factors, own_factors = factors[:4], factors[4:]
         given_gated = lax.ppermute(other_gated, "context", swap)
         given_grad = lax.ppermute(other_grad, "context", swap)
-        own, *own_factors = pack(False)
+        own = pl.pallas_call(
+            lambda *refs: pack_own_kernel(hosts, lanes, *refs),
+            out_shape=block_rows(rows),
+            in_specs=[vmem] * 4 + [hbm],
+            scratch_shapes=[filter_half, pltpu.SemaphoreType.DMA((1,))],
+            compiler_params=params,
+            name="pack_own",
+        )(*own_factors, sources[4])
 
         def convolve(*held):
             count = len(held)

time: 78.9 us -> 79.1 us (level)
  no operation moved by 1% of the time
where the time goes in v10:
time: 79.1 us; the launch traced here: 78.7 us
  blocking collectives  47.1 us (60%)
  starting transfers between devices  12.8 us (16%)
  waiting for transfers between devices  9.46 us (12%)
  Pallas kernels  8.52 us (11%)
    all_to_all x2, blocking collectives, exchange(): lax.all_to_all(pieces, 'context', 0, 0, axis_index_groups=groups, tiled=T...  47.1 us
    all_to_all x1, starting transfers between devices, exchange(): lax.all_to_all(pieces, 'context', 0, 0, axis_index_groups=groups, tiled=T...  9.3 us
    all_to_all x1, waiting for transfers between devices, exchange(): lax.all_to_all(pieces, 'context', 0, 0, axis_index_groups=groups, tiled=T...  7.84 us
    ppermute x1, starting transfers between devices, local(): given_grad = lax.ppermute(other_grad, 'context', swap)  3.33 us
    pallas_call x1, Pallas kernels, convolve(): pl.pallas_call(lambda *refs: convolve_kernel(peers, lanes, early, refs[:c...  2.63 us
    pallas_call x2, Pallas kernels, unpack(): pl.pallas_call(lambda *refs: unpack_kernel(hosts, lanes, given, *refs), o...  1.94 us
    pallas_call x3, Pallas kernels, join(): pl.pallas_call(kernel, out_shape=block_rows(size), compiler_params=params...  1.76 us
  transfers between devices with their start and end apart: 4, of which 3 were waited for; matrix products, arithmetic and copies ran while one was open for 0% of the time, Pallas kernels for 4%

profile of v10, /device:TPU:1, one launch (start us, length us, event | category | flops | bytes accessed | tf_op | source)
XLA Modules:
  0.0 78.7 jit_solution(2965587074066333368)
XLA Ops:
  0.6 0.0 copy-start
  0.6 0.0 copy-start.1
  0.7 0.0 copy-start.3
  0.7 1.4 %pack_other.1 = (f32[512,128]{1,0:T(8,128)S(1)}, f32[544,128]{1,0:T(8,128)S(1)}, bf16[128,512]{1,0:T(8,128)(2,1)S(1)}, bf16[128,512]{1,0:T(8,128)(2,1)S(1)}, bf1...) custom-call(bf16[128,1024]{1,0:T(8,128)(2,1)} %refs_0_.1, ...), custom_call_target="tpu_custom_call" | custom-call | tf_op jit(solution)/shard_map/pack_other/pallas_call | solution.py:383
  2.1 3.3 %collective-permute-start.1 = (f32[544,128]{1,0:T(8,128)S(1)}, f32[544,128]{1,0:T(8,128)S(1)}, u32[]{:S(2)}, u32[]{:S(2)}) collective-permute-start(f32[544,128]{1,0:T(8,128)S(1)} %get-tuple-element.91), channel_id=1, source_target_pairs={{0,1},{1,0},{2,3},{3,2},{4,5},{5,4},{6,7},{7,6},{8,9},{9,8},{10,11... | collective-permute-start | bytes 835592 | tf_op jit(solution)/shard_map/ppermute | solution.py:393
  5.4 0.1 collective-permute-start
  5.5 0.8 pack_own.1
  6.3 0.7 collective-permute-done
  7.0 0.0 collective-permute-done.1
  7.0 0.0 copy-done
  7.0 0.0 copy-done.1
  7.0 0.0 copy-done.3
  7.0 68.7 %conditional.1 = (f32[2112,128]{1,0:T(8,128)S(1)}) conditional(s32[]{:T(128)} %convert_element_type.3, (f32[1056,128]{1,0:T(8,128)S(1)}, f32[512,128]{1,0:T(8,128)S(1)}, f32[544,128]{1,0:T(8,128)S(1)}, bf16[128,192]{1,0:T(8,128)(2,1)}, bf16[128,256]{1,0:T(8,128)(2,1)}, /*index=5*/bf16[512,256]{1,0:T(8,128)(2,1)S(1)}, bf16[512,256]{1,0:T(8,128)(2,1)S(1)}, ...), branch_computations={%region_0.0_spmd, %region_1.0_spmd} | conditional | bytes 6144152 | solution.py:431
  7.0 0.0 copy-start.2
  7.0 0.7 join.4
  7.7 9.3 %all-to-all-start = ((f32[96,1,128]{2,1,0:T(1,128)}), f32[96,1,128]{2,1,0:T(1,128)S(1)}, u32[]{:S(2)}, u32[]{:S(2)}) async-start(f32[96,1,128]{2,1,0:T(1,128)} %bitcast.1), calls=%async_computation | async-start | bytes 98304 | tf_op jit(solution)/shard_map/cond/branch_0_fun/all_to_all | solution.py:347
  17.0 0.0 copy-done.2
  17.0 1.0 %join.5 = f32[2016,128]{1,0:T(8,128)S(1)} custom-call(f32[1056,128]{1,0:T(8,128)S(1)} %get-tuple-element.41.refs_0_, f32[512,128]{1,0:T(8,128)} %copy-done.2, f32[544,128]{1,0:T(8,128)S(1)} %get-tuple-element.43.refs_2_), custom_call_target="tpu_custom_call" | custom-call | tf_op jit(solution)/shard_map/cond/branch_0_fun/join/pallas_call | solution.py:414
  18.1 0.0 copy-start.4
  18.1 0.0 copy-start.6
  18.1 0.0 copy-start.8
  18.1 7.8 %all-to-all-done = f32[96,1,128]{2,1,0:T(1,128)S(1)} async-done(((f32[96,1,128]{2,1,0:T(1,128)}), f32[96,1,128]{2,1,0:T(1,128)S(1)}, u32[]{:S(2)}, u32[]{:S(2)}) %all-to-all-start) | async-done | bytes 49184 | tf_op jit(solution)/shard_map/cond/branch_0_fun/all_to_all | solution.py:347
  25.9 20.9 %all_to_all.20 = f32[2016,1,128]{2,1,0:T(1,128)S(1)} all-to-all(f32[2016,1,128]{2,1,0:T(1,128)S(1)} %bitcast.27), channel_id=1, replica_groups={{0,2,4,6,8,10,12,14,16,18,20,22,24,26,28,30,32,34,36,38,40,42,44,46,48,..., dimensions={0} | all-to-all | bytes 2064384 | tf_op jit(solution)/shard_map/cond/branch_0_fun/all_to_all | solution.py:347
  46.8 0.0 copy-done.4
  46.8 0.0 copy-done.6
  46.8 0.0 copy-done.8
  46.8 2.6 %convolve.2 = f32[2112,128]{1,0:T(8,128)S(1)} custom-call(f32[96,128]{1,0:T(8,128)S(1)} %bitcast.28, f32[2016,128]{1,0:T(8,128)S(1)} %bitcast.26, bf16[128,192]{1,0:T(8,128)(2,1)S(1)} %copy-done.8, bf16[128,256]{1,0:T(8,128)(2,1)S(1)} %copy-done.6, bf16[512,256]{1,0:T(8,128)(2,1)S(1)} %get-tuple-element.48.refs_4_, ...), custom_call_target="tpu_custom_call" | custom-call | tf_op jit(solution)/shard_map/cond/branch_0_fun/convolve/pallas_call | solution.py:405
  49.5 26.3 %all_to_all.21 = f32[2112,1,128]{2,1,0:T(1,128)S(1)} all-to-all(f32[2112,1,128]{2,1,0:T(1,128)S(1)} %bitcast.23), channel_id=1, replica_groups={{0,2,4,6,8,10,12,14,16,18,20,22,24,26,28,30,32,34,36,38,40,42,44,46,48,..., dimensions={0} | all-to-all | bytes 2162688 | tf_op jit(solution)/shard_map/cond/branch_0_fun/all_to_all | solution.py:347
  75.8 0.1 collective-permute-start.2
  75.9 1.0 %unpack.2 = (bf16[128,1024]{1,0:T(8,128)(2,1)}, bf16[128,1024]{1,0:T(8,128)(2,1)}, bf16[128,1024]{1,0:T(8,128)(2,1)}, bf16[128,1024]{1,0:T(8,128)(2,1)}, f32[64,128]{1,0:T(8,128)}) custom-call(f32[2112,128]{1,0:T(8,128)S(1)} %get-tuple-element.106.refs_0_, bf16[128,512]{1,0:T(8,128)(2,1)S(1)} %get-tuple-element.86.refs_0_.refs_1_, ...), custom_call_target="tpu_custom_call" | custom-call | tf_op jit(solution)/shard_map/unpack/pallas_call | solution.py:440
  76.8 0.9 %collective-permute-done.2.refs_0_ = f32[1056,128]{1,0:T(8,128)S(1)} collective-permute-done((f32[1056,128]{1,0:T(8,128)S(1)}, f32[1056,128]{1,0:T(8,128)S(1)}, u32[]{:S(2)}, u32[]{:S(2)}) %collective-permute-start.2) | collective-permute-done | bytes 540704 | tf_op jit(solution)/shard_map/ppermute | solution.py:433
  77.8 1.0 %unpack.3 = (bf16[128,1024]{1,0:T(8,128)(2,1)}, bf16[128,1024]{1,0:T(8,128)(2,1)}, bf16[128,1024]{1,0:T(8,128)(2,1)}, bf16[128,1024]{1,0:T(8,128)(2,1)}, f32[64,128]{1,0:T(8,128)}) custom-call(f32[1056,128]{1,0:T(8,128)S(1)} %collective-permute-done.2.refs_0_, ...), custom_call_target="tpu_custom_call", output_to_operand_aliasing={{0}: (5, {}), {1}: (6, {}), {2}: (7, {}), {3}: (8, {}), {4}... | custom-call | tf_op jit(solution)/shard_map/unpack/pallas_call | solution.py:440
  (1 shorter events, 0.0 us)
Async XLA Ops:
  0.6 6.4 %copy-start = (bf16[512,256]{1,0:T(8,128)(2,1)S(1)}, bf16[512,256]{1,0:T(8,128)(2,1)}, u32[]{:S(2)}) copy-start(bf16[512,256]{1,0:T(8,128)(2,1)} %constant.25.clone) | copy-start | bytes 786436
  0.6 6.3 %copy-start.1 = (bf16[512,256]{1,0:T(8,128)(2,1)S(1)}, bf16[512,256]{1,0:T(8,128)(2,1)}, u32[]{:S(2)}) copy-start(bf16[512,256]{1,0:T(8,128)(2,1)} %constant.24.clone) | copy-start | bytes 786436
  0.7 6.3 %copy-start.3 = (f32[2,64,128]{2,1,0:T(8,128)S(1)}, f32[2,64,128]{2,1,0:T(8,128)}, u32[]{:S(2)}) copy-start(f32[2,64,128]{2,1,0:T(8,128)} %constant.27.clone) | copy-start | bytes 196612
  2.1 4.9 %collective-permute-start.1 = (f32[544,128]{1,0:T(8,128)S(1)}, f32[544,128]{1,0:T(8,128)S(1)}, u32[]{:S(2)}, u32[]{:S(2)}) collective-permute-start(f32[544,128]{1,0:T(8,128)S(1)} %get-tuple-element.91), channel_id=1, source_target_pairs={{0,1},{1,0},{2,3},{3,2},{4,5},{5,4},{6,7},{7,6},{8,9},{9,8},{10,11... | collective-permute-start | bytes 835592 | tf_op jit(solution)/shard_map/ppermute | solution.py:393
  5.4 1.6 %collective-permute-start = (f32[512,128]{1,0:T(8,128)S(1)}, f32[512,128]{1,0:T(8,128)S(1)}, u32[]{:S(2)}, u32[]{:S(2)}) collective-permute-start(f32[512,128]{1,0:T(8,128)S(1)} %get-tuple-element.90), channel_id=1, source_target_pairs={{0,1},{1,0},{2,3},{3,2},{4,5},{5,4},{6,7},{7,6},{8,9},{9,8},{10,11... | collective-permute-start | bytes 786440 | tf_op jit(solution)/shard_map/ppermute | solution.py:392
  7.0 10.0 %copy-start.2 = (f32[512,128]{1,0:T(8,128)}, f32[512,128]{1,0:T(8,128)S(1)}, u32[]{:S(2)}) copy-start(f32[512,128]{1,0:T(8,128)S(1)} %get-tuple-element.42.refs_1_) | copy-start | bytes 786436 | tf_op jit(solution)/shard_map/cond
  7.7 18.2 %all-to-all-start = ((f32[96,1,128]{2,1,0:T(1,128)}), f32[96,1,128]{2,1,0:T(1,128)S(1)}, u32[]{:S(2)}, u32[]{:S(2)}) async-start(f32[96,1,128]{2,1,0:T(1,128)} %bitcast.1), calls=%async_computation | async-start | bytes 98304 | tf_op jit(solution)/shard_map/cond/branch_0_fun/all_to_all | solution.py:347
  18.1 28.7 %copy-start.4 = (f32[2,64,128]{2,1,0:T(8,128)S(1)}, f32[2,64,128]{2,1,0:T(8,128)}, u32[]{:S(2)}) copy-start(f32[2,64,128]{2,1,0:T(8,128)} %get-tuple-element.50.refs_6_) | copy-start | bytes 196612 | tf_op jit(solution)/shard_map/cond
  18.1 28.7 %copy-start.6 = (bf16[128,256]{1,0:T(8,128)(2,1)S(1)}, bf16[128,256]{1,0:T(8,128)(2,1)}, u32[]{:S(2)}) copy-start(bf16[128,256]{1,0:T(8,128)(2,1)} %get-tuple-element.47.refs_3_) | copy-start | bytes 196612 | tf_op jit(solution)/shard_map/cond
  18.1 28.7 %copy-start.8 = (bf16[128,192]{1,0:T(8,128)(2,1)S(1)}, bf16[128,192]{1,0:T(8,128)(2,1)}, u32[]{:S(2)}) copy-start(bf16[128,192]{1,0:T(8,128)(2,1)} %get-tuple-element.46.refs_2_) | copy-start | bytes 147460 | tf_op jit(solution)/shard_map/cond
  75.8 2.0 %collective-permute-start.2 = (f32[1056,128]{1,0:T(8,128)S(1)}, f32[1056,128]{1,0:T(8,128)S(1)}, u32[]{:S(2)}, u32[]{:S(2)}) collective-permute-start(f32[1056,128]{1,0:T(8,128)S(1)} %join.7), channel_id=1, source_target_pairs={{0,1},{1,0},{2,3},{3,2},{4,5},{5,4},{6,7},{7,6},{8,9},{9,8},{10,11... | collective-permute-start | bytes 1622024 | tf_op jit(solution)/shard_map/ppermute | solution.py:433

commit v11 on v10

--- a/solution.py
+++ b/solution.py
@@ -354,7 +354,7 @@
     groups = [[2 * host + core for host in range(hosts)] for core in range(2)]
     swap = [(rank, rank ^ 1) for rank in range(peers)]
     params = pltpu.CompilerParams(vmem_limit_bytes=48 * 1024 * 1024)
-    early = 3
+    early = 4
 
     def local(query_gate, key_gate, value_in, filter_raw, grad_out):
         inner, width = query_gate.shape

time: 79.1 us -> 79.2 us (level)
  no operation moved by 1% of the time
where the time goes in v11:
time: 79.2 us; the launch traced here: 78.9 us
  blocking collectives  47.2 us (60%)
  starting transfers between devices  12.8 us (16%)
  waiting for transfers between devices  9.54 us (12%)
  Pallas kernels  8.54 us (11%)
    all_to_all x2, blocking collectives, exchange(): lax.all_to_all(pieces, 'context', 0, 0, axis_index_groups=groups, tiled=T...  47.2 us
    all_to_all x1, starting transfers between devices, exchange(): lax.all_to_all(pieces, 'context', 0, 0, axis_index_groups=groups, tiled=T...  9.3 us
    all_to_all x1, waiting for transfers between devices, exchange(): lax.all_to_all(pieces, 'context', 0, 0, axis_index_groups=groups, tiled=T...  7.91 us
    ppermute x1, starting transfers between devices, local(): given_grad = lax.ppermute(other_grad, 'context', swap)  3.33 us
    pallas_call x1, Pallas kernels, convolve(): pl.pallas_call(lambda *refs: convolve_kernel(peers, lanes, early, refs[:c...  2.64 us
    pallas_call x2, Pallas kernels, unpack(): pl.pallas_call(lambda *refs: unpack_kernel(hosts, lanes, given, *refs), o...  1.94 us
    pallas_call x3, Pallas kernels, join(): pl.pallas_call(kernel, out_shape=block_rows(size), compiler_params=params...  1.78 us
  transfers between devices with their start and end apart: 4, of which 3 were waited for; matrix products, arithmetic and copies ran while one was open for 0% of the time, Pallas kernels for 4%

profile of v11, /device:TPU:1, one launch (start us, length us, event | category | flops | bytes accessed | tf_op | source)
XLA Modules:
  0.0 78.9 jit_solution(16929168160103004259)
XLA Ops:
  0.6 0.0 copy-start
  0.6 0.0 copy-start.1
  0.7 0.0 copy-start.3
  0.7 1.4 %pack_other.1 = (f32[512,128]{1,0:T(8,128)S(1)}, f32[544,128]{1,0:T(8,128)S(1)}, bf16[128,512]{1,0:T(8,128)(2,1)S(1)}, bf16[128,512]{1,0:T(8,128)(2,1)S(1)}, bf1...) custom-call(bf16[128,1024]{1,0:T(8,128)(2,1)} %refs_0_.1, ...), custom_call_target="tpu_custom_call" | custom-call | tf_op jit(solution)/shard_map/pack_other/pallas_call | solution.py:383
  2.1 3.3 %collective-permute-start.1 = (f32[544,128]{1,0:T(8,128)S(1)}, f32[544,128]{1,0:T(8,128)S(1)}, u32[]{:S(2)}, u32[]{:S(2)}) collective-permute-start(f32[544,128]{1,0:T(8,128)S(1)} %get-tuple-element.91), channel_id=1, source_target_pairs={{0,1},{1,0},{2,3},{3,2},{4,5},{5,4},{6,7},{7,6},{8,9},{9,8},{10,11... | collective-permute-start | bytes 835592 | tf_op jit(solution)/shard_map/ppermute | solution.py:393
  5.4 0.1 collective-permute-start
  5.5 0.8 pack_own.1
  6.3 0.7 collective-permute-done
  7.0 0.0 collective-permute-done.1
  7.0 0.0 copy-done
  7.0 0.0 copy-done.1
  7.0 0.0 copy-done.3
  7.0 68.8 %conditional.1 = (f32[2112,128]{1,0:T(8,128)S(1)}) conditional(s32[]{:T(128)} %convert_element_type.3, (f32[1056,128]{1,0:T(8,128)S(1)}, f32[512,128]{1,0:T(8,128)S(1)}, f32[544,128]{1,0:T(8,128)S(1)}, bf16[128,192]{1,0:T(8,128)(2,1)}, bf16[128,256]{1,0:T(8,128)(2,1)}, /*index=5*/bf16[512,256]{1,0:T(8,128)(2,1)S(1)}, bf16[512,256]{1,0:T(8,128)(2,1)S(1)}, ...), branch_computations={%region_0.0_spmd, %region_1.0_spmd} | conditional | bytes 6160536 | solution.py:431
  7.0 0.0 copy-start.2
  7.0 0.7 join.4
  7.7 9.3 %all-to-all-start = ((f32[128,1,128]{2,1,0:T(1,128)}), f32[128,1,128]{2,1,0:T(1,128)S(1)}, u32[]{:S(2)}, u32[]{:S(2)}) async-start(f32[128,1,128]{2,1,0:T(1,128)} %bitcast.1), calls=%async_computation | async-start | bytes 131072 | tf_op jit(solution)/shard_map/cond/branch_0_fun/all_to_all | solution.py:347
  17.0 0.0 copy-done.2
  17.1 1.0 %join.5 = f32[1984,128]{1,0:T(8,128)S(1)} custom-call(f32[1056,128]{1,0:T(8,128)S(1)} %get-tuple-element.41.refs_0_, f32[512,128]{1,0:T(8,128)} %copy-done.2, f32[544,128]{1,0:T(8,128)S(1)} %get-tuple-element.43.refs_2_), custom_call_target="tpu_custom_call" | custom-call | tf_op jit(solution)/shard_map/cond/branch_0_fun/join/pallas_call | solution.py:414
  18.1 0.0 copy-start.4
  18.1 0.0 copy-start.6
  18.1 0.0 copy-start.8
  18.1 7.9 %all-to-all-done = f32[128,1,128]{2,1,0:T(1,128)S(1)} async-done(((f32[128,1,128]{2,1,0:T(1,128)}), f32[128,1,128]{2,1,0:T(1,128)S(1)}, u32[]{:S(2)}, u32[]{:S(2)}) %all-to-all-start) | async-done | bytes 65568 | tf_op jit(solution)/shard_map/cond/branch_0_fun/all_to_all | solution.py:347
  26.0 21.2 %all_to_all.20 = f32[1984,1,128]{2,1,0:T(1,128)S(1)} all-to-all(f32[1984,1,128]{2,1,0:T(1,128)S(1)} %bitcast.27), channel_id=1, replica_groups={{0,2,4,6,8,10,12,14,16,18,20,22,24,26,28,30,32,34,36,38,40,42,44,46,48,..., dimensions={0} | all-to-all | bytes 2031616 | tf_op jit(solution)/shard_map/cond/branch_0_fun/all_to_all | solution.py:347
  47.2 0.0 copy-done.4
  47.2 0.0 copy-done.6
  47.2 0.0 copy-done.8
  47.2 2.6 %convolve.2 = f32[2112,128]{1,0:T(8,128)S(1)} custom-call(f32[128,128]{1,0:T(8,128)S(1)} %bitcast.28, f32[1984,128]{1,0:T(8,128)S(1)} %bitcast.26, bf16[128,192]{1,0:T(8,128)(2,1)S(1)} %copy-done.8, bf16[128,256]{1,0:T(8,128)(2,1)S(1)} %copy-done.6, bf16[512,256]{1,0:T(8,128)(2,1)S(1)} %get-tuple-element.48.refs_4_, ...), custom_call_target="tpu_custom_call" | custom-call | tf_op jit(solution)/shard_map/cond/branch_0_fun/convolve/pallas_call | solution.py:405
  49.9 26.0 %all_to_all.21 = f32[2112,1,128]{2,1,0:T(1,128)S(1)} all-to-all(f32[2112,1,128]{2,1,0:T(1,128)S(1)} %bitcast.23), channel_id=1, replica_groups={{0,2,4,6,8,10,12,14,16,18,20,22,24,26,28,30,32,34,36,38,40,42,44,46,48,..., dimensions={0} | all-to-all | bytes 2162688 | tf_op jit(solution)/shard_map/cond/branch_0_fun/all_to_all | solution.py:347
  75.9 0.1 collective-permute-start.2
  76.0 1.0 %unpack.2 = (bf16[128,1024]{1,0:T(8,128)(2,1)}, bf16[128,1024]{1,0:T(8,128)(2,1)}, bf16[128,1024]{1,0:T(8,128)(2,1)}, bf16[128,1024]{1,0:T(8,128)(2,1)}, f32[64,128]{1,0:T(8,128)}) custom-call(f32[2112,128]{1,0:T(8,128)S(1)} %get-tuple-element.106.refs_0_, bf16[128,512]{1,0:T(8,128)(2,1)S(1)} %get-tuple-element.86.refs_0_.refs_1_, ...), custom_call_target="tpu_custom_call" | custom-call | tf_op jit(solution)/shard_map/unpack/pallas_call | solution.py:440
  77.0 0.9 %collective-permute-done.2.refs_0_ = f32[1056,128]{1,0:T(8,128)S(1)} collective-permute-done((f32[1056,128]{1,0:T(8,128)S(1)}, f32[1056,128]{1,0:T(8,128)S(1)}, u32[]{:S(2)}, u32[]{:S(2)}) %collective-permute-start.2) | collective-permute-done | bytes 540704 | tf_op jit(solution)/shard_map/ppermute | solution.py:433
  77.9 1.0 %unpack.3 = (bf16[128,1024]{1,0:T(8,128)(2,1)}, bf16[128,1024]{1,0:T(8,128)(2,1)}, bf16[128,1024]{1,0:T(8,128)(2,1)}, bf16[128,1024]{1,0:T(8,128)(2,1)}, f32[64,128]{1,0:T(8,128)}) custom-call(f32[1056,128]{1,0:T(8,128)S(1)} %collective-permute-done.2.refs_0_, ...), custom_call_target="tpu_custom_call", output_to_operand_aliasing={{0}: (5, {}), {1}: (6, {}), {2}: (7, {}), {3}: (8, {}), {4}... | custom-call | tf_op jit(solution)/shard_map/unpack/pallas_call | solution.py:440
  (1 shorter events, 0.0 us)
Async XLA Ops:
  0.6 6.4 %copy-start = (bf16[512,256]{1,0:T(8,128)(2,1)S(1)}, bf16[512,256]{1,0:T(8,128)(2,1)}, u32[]{:S(2)}) copy-start(bf16[512,256]{1,0:T(8,128)(2,1)} %constant.25.clone) | copy-start | bytes 786436
  0.6 6.3 %copy-start.1 = (bf16[512,256]{1,0:T(8,128)(2,1)S(1)}, bf16[512,256]{1,0:T(8,128)(2,1)}, u32[]{:S(2)}) copy-start(bf16[512,256]{1,0:T(8,128)(2,1)} %constant.24.clone) | copy-start | bytes 786436
  0.7 6.3 %copy-start.3 = (f32[2,64,128]{2,1,0:T(8,128)S(1)}, f32[2,64,128]{2,1,0:T(8,128)}, u32[]{:S(2)}) copy-start(f32[2,64,128]{2,1,0:T(8,128)} %constant.27.clone) | copy-start | bytes 196612
  2.1 4.9 %collective-permute-start.1 = (f32[544,128]{1,0:T(8,128)S(1)}, f32[544,128]{1,0:T(8,128)S(1)}, u32[]{:S(2)}, u32[]{:S(2)}) collective-permute-start(f32[544,128]{1,0:T(8,128)S(1)} %get-tuple-element.91), channel_id=1, source_target_pairs={{0,1},{1,0},{2,3},{3,2},{4,5},{5,4},{6,7},{7,6},{8,9},{9,8},{10,11... | collective-permute-start | bytes 835592 | tf_op jit(solution)/shard_map/ppermute | solution.py:393
  5.4 1.6 %collective-permute-start = (f32[512,128]{1,0:T(8,128)S(1)}, f32[512,128]{1,0:T(8,128)S(1)}, u32[]{:S(2)}, u32[]{:S(2)}) collective-permute-start(f32[512,128]{1,0:T(8,128)S(1)} %get-tuple-element.90), channel_id=1, source_target_pairs={{0,1},{1,0},{2,3},{3,2},{4,5},{5,4},{6,7},{7,6},{8,9},{9,8},{10,11... | collective-permute-start | bytes 786440 | tf_op jit(solution)/shard_map/ppermute | solution.py:392
  7.0 10.0 %copy-start.2 = (f32[512,128]{1,0:T(8,128)}, f32[512,128]{1,0:T(8,128)S(1)}, u32[]{:S(2)}) copy-start(f32[512,128]{1,0:T(8,128)S(1)} %get-tuple-element.42.refs_1_) | copy-start | bytes 786436 | tf_op jit(solution)/shard_map/cond
  7.7 18.3 %all-to-all-start = ((f32[128,1,128]{2,1,0:T(1,128)}), f32[128,1,128]{2,1,0:T(1,128)S(1)}, u32[]{:S(2)}, u32[]{:S(2)}) async-start(f32[128,1,128]{2,1,0:T(1,128)} %bitcast.1), calls=%async_computation | async-start | bytes 131072 | tf_op jit(solution)/shard_map/cond/branch_0_fun/all_to_all | solution.py:347
  18.1 29.1 %copy-start.4 = (f32[2,64,128]{2,1,0:T(8,128)S(1)}, f32[2,64,128]{2,1,0:T(8,128)}, u32[]{:S(2)}) copy-start(f32[2,64,128]{2,1,0:T(8,128)} %get-tuple-element.50.refs_6_) | copy-start | bytes 196612 | tf_op jit(solution)/shard_map/cond
  18.1 29.1 %copy-start.6 = (bf16[128,256]{1,0:T(8,128)(2,1)S(1)}, bf16[128,256]{1,0:T(8,128)(2,1)}, u32[]{:S(2)}) copy-start(bf16[128,256]{1,0:T(8,128)(2,1)} %get-tuple-element.47.refs_3_) | copy-start | bytes 196612 | tf_op jit(solution)/shard_map/cond
  18.1 29.1 %copy-start.8 = (bf16[128,192]{1,0:T(8,128)(2,1)S(1)}, bf16[128,192]{1,0:T(8,128)(2,1)}, u32[]{:S(2)}) copy-start(bf16[128,192]{1,0:T(8,128)(2,1)} %get-tuple-element.46.refs_2_) | copy-start | bytes 147460 | tf_op jit(solution)/shard_map/cond
  75.9 2.0 %collective-permute-start.2 = (f32[1056,128]{1,0:T(8,128)S(1)}, f32[1056,128]{1,0:T(8,128)S(1)}, u32[]{:S(2)}, u32[]{:S(2)}) collective-permute-start(f32[1056,128]{1,0:T(8,128)S(1)} %join.7), channel_id=1, source_target_pairs={{0,1},{1,0},{2,3},{3,2},{4,5},{5,4},{6,7},{7,6},{8,9},{9,8},{10,11... | collective-permute-start | bytes 1622024 | tf_op jit(solution)/shard_map/ppermute | solution.py:433
